TPU v7x, 32 devices: a whole 2x2x4 slice. The times are simulated.
32 devices in a mesh: res: 8 (over z, x), hid: 4 (over y, core).
Axes of the slice: x: 2, y: 2, z: 4, core: 2. Of those that a mesh axis runs over, the one named last changes fastest.
Arguments:
- node_in: bfloat16 [2048, 512], P(('res', 'hid')), may hold values from -6 to 6
- edge_in: bfloat16 [2048, 60, 192], P(('res', 'hid')), may hold values from -6 to 6
- neighbours: int32 [2048, 60], P(('res', 'hid')), may hold values from 0 to 2047, as said below
- live_counts: int32 [2048], P(('res', 'hid')), may hold values from 30 to 60
- message_first: bfloat16 [1216, 512], replicated, may hold values from -0.15625 to 0.15625
- message_first_bias: float32 [512], replicated, may hold values from -3 to 3
- message_second: bfloat16 [512, 512], replicated, may hold values from -0.25 to 0.25
- message_second_bias: float32 [512], replicated, may hold values from -3 to 3
- message_third: bfloat16 [512, 512], replicated, may hold values from -1 to 1
- message_third_bias: float32 [512], replicated, may hold values from -3 to 3
- norm_one: float32 [512], replicated, may hold values from 0.5 to 1.5
- feed_first: bfloat16 [512, 2048], P(None, 'hid'), may hold values from -0.25 to 0.25
- feed_first_bias: float32 [2048], P('hid'), may hold values from -3 to 3
- feed_second: bfloat16 [2048, 512], P('hid'), may hold values from -0.125 to 0.125
- feed_second_bias: float32 [512], replicated, may hold values from -3 to 3
- norm_two: float32 [512], replicated, may hold values from 0.5 to 1.5
- edge_first: bfloat16 [1216, 192], replicated, may hold values from -0.15625 to 0.15625
- edge_first_bias: float32 [192], replicated, may hold values from -3 to 3
- edge_second: bfloat16 [192, 192], replicated, may hold values from -0.4375 to 0.4375
- edge_second_bias: float32 [192], replicated, may hold values from -3 to 3
- edge_third: bfloat16 [192, 192], replicated, may hold values from -0.4375 to 0.4375
- edge_third_bias: float32 [192], replicated, may hold values from -3 to 3
- norm_three: float32 [192], replicated, may hold values from 0.5 to 1.5
- node_cotangent: bfloat16 [2048, 512], P(('res', 'hid')), may hold values from -6 to 6
- edge_cotangent: bfloat16 [2048, 60, 192], P(('res', 'hid')), may hold values from -6 to 6
Outputs:
- node_out: bfloat16 [2048, 512], P(('res', 'hid'))
- edge_out: bfloat16 [2048, 60, 192], P(('res', 'hid'))
- node_gradient: float32 [2048, 512], P(('res', 'hid'))
- edge_gradient: float32 [2048, 60, 192], P(('res', 'hid'))
- message_first_gradient: float32 [1216, 512], replicated
- message_first_bias_gradient: float32 [512], replicated
- message_second_gradient: float32 [512, 512], replicated
- message_second_bias_gradient: float32 [512], replicated
- message_third_gradient: float32 [512, 512], replicated
- message_third_bias_gradient: float32 [512], replicated
- norm_one_gradient: float32 [512], replicated
- feed_first_gradient: float32 [512, 2048], P(None, 'hid')
- feed_first_bias_gradient: float32 [2048], P('hid')
- feed_second_gradient: float32 [2048, 512], P('hid')
- feed_second_bias_gradient: float32 [512], replicated
- norm_two_gradient: float32 [512], replicated
- edge_first_gradient: float32 [1216, 192], replicated
- edge_first_bias_gradient: float32 [192], replicated
- edge_second_gradient: float32 [192, 192], replicated
- edge_second_bias_gradient: float32 [192], replicated
- edge_third_gradient: float32 [192, 192], replicated
- edge_third_bias_gradient: float32 [192], replicated
- norm_three_gradient: float32 [192], replicated
Inputs may be any that keep to these rules, and one draw needn't show every extreme that they name: `neighbours`: in each block of 64 consecutive residues, the table's 64 x 60 entries name residues of each aligned group of 256 residues exactly 480 times, repeats counted.
All inputs are finite; a program needn't handle non-finite values.
Results may differ from a plain program's by a relative error of at most 0.018.
Values may be sent and summed in bfloat16 or wider, within the bound.
No kernel may reach another device: no remote copies, remote signals or barrier semaphores. Data moves between devices by JAX's collectives and lax.ppermute only.
A program may use at most 256 MiB of HBM per device.

v0:
```python
import functools

import jax
import jax.numpy as jnp
from jax import lax
from jax.experimental import pallas as pl
from jax.experimental.pallas import tpu as pltpu
from jax.sharding import PartitionSpec as P

EPS = 1e-05
AXES = ("res", "hid")
F32 = jnp.float32
BF16 = jnp.bfloat16
TANH_SCALE = 0.7978845608028654
TANH_CUBE = 0.044715
LANES = 128
CHUNK = 2048
MIB = 1024 * 1024
VMEM = 58 * MIB


def dot(left, right):
    return lax.dot_general(left, right, (((1,), (0,)), ((), ())), preferred_element_type=F32)


def dot_rows(left, right):
    return lax.dot_general(left, right, (((0,), (0,)), ((), ())), preferred_element_type=F32)


def dot_back(left, right):
    return lax.dot_general(left, right, (((1,), (1,)), ((), ())), preferred_element_type=F32)


def halves(value):
    high = value.astype(BF16)
    return high, (value - high.astype(F32)).astype(BF16)


def fine(product, value, weights):
    high, low = halves(value)
    return product(high, weights) + product(low, weights)


def gelu_parts(x):
    square = x * x
    t = jnp.tanh(x * (TANH_SCALE + (TANH_SCALE * TANH_CUBE) * square))
    gate = 0.5 + 0.5 * t
    act = x * gate
    slope = gate + act * (1.0 - gate) * (2 * TANH_SCALE + (6 * TANH_SCALE * TANH_CUBE) * square)
    return act, slope


def index_columns(idx_row):
    parts = [
        jnp.broadcast_to(idx_row[:, first : first + LANES], (LANES, LANES)).T
        for first in range(0, idx_row.shape[1], LANES)
    ]
    return jnp.concatenate(parts, axis=0)


def one_hot_columns(idx, start, count):
    one, zero = jnp.ones((), BF16), jnp.zeros((), BF16)
    idx = idx.astype(jnp.int16)
    lane = lax.broadcasted_iota(jnp.int32, idx.shape, 1).astype(jnp.int16)
    parts = [
        jnp.where(idx == lane + jnp.int16(start + first), one, zero)
        for first in range(0, count, LANES)
    ]
    return jnp.concatenate(parts, axis=1)


def pick_rows(idx, table_refs):
    total, start = None, 0
    for ref in table_refs:
        rows = ref.shape[0]
        step = min(rows, CHUNK)
        for first in range(0, rows, step):
            part = dot(one_hot_columns(idx, start + first, step), ref[first : first + step, :])
            total = part if total is None else total + part
        start += rows
    return total


def one_hot_rows(idx_row, start, count):
    shape = (count, idx_row.shape[1])
    row = (lax.broadcasted_iota(jnp.int32, shape, 0) + start).astype(jnp.int16)
    names = jnp.broadcast_to(idx_row, shape).astype(jnp.int16)
    return jnp.where(names == row, jnp.ones((), BF16), jnp.zeros((), BF16))


def group_rows(order, first, count, rows_ref, moved, width):
    for e in range(count):
        at = pl.multiple_of(order[0, first + e] * 8, 8)
        moved[e * 8 : e * 8 + 8, :] = rows_ref[pl.ds(at, 8), :]

    def column(at):
        return moved[pl.ds(at, count, stride=8), :]

    tiles = pl.cdiv(width, LANES)
    parts = [column(at)[:, : min(LANES, width - at * LANES)] for at in range(tiles)]
    return jnp.concatenate(parts, axis=1).astype(BF16), column(tiles)


def group_sums(rows, local, residues):
    lane = lax.broadcasted_iota(jnp.int32, local.shape, 1).astype(F32)
    picks = [
        jnp.where(local == lane + float(first), 1.0, 0.0).astype(BF16)
        for first in range(0, residues, LANES)
    ]
    return dot_rows(jnp.concatenate(picks, axis=1), rows)


def order_kernel(groups, count, names, out):
    rows = names.shape[0]
    row = lax.broadcasted_iota(jnp.int32, (LANES, LANES), 0)
    column = lax.broadcasted_iota(jnp.int32, (LANES, LANES), 1)
    upto = jnp.where(row <= column, 1.0, 0.0).astype(BF16)
    ones = jnp.ones((LANES, LANES), BF16)
    above = lax.broadcasted_iota(jnp.int32, (rows, rows), 0)
    before = jnp.where(lax.broadcasted_iota(jnp.int32, (rows, rows), 1) < above, 1.0, 0.0).astype(BF16)
    place = jnp.full(names.shape, float(2 * LANES * LANES), F32)
    for group in range(groups):
        here = names[...] == group
        low = jnp.where(here, 1.0, 0.0).astype(BF16)
        rank = dot(low, upto) + dot(before, dot(low, ones).astype(BF16))
        place = jnp.where(here, rank + float(group * count - 1), place)
    high = total = None
    for at in range(rows):
        where = jnp.broadcast_to(place[at : at + 1, :], (LANES, LANES)).T.astype(jnp.int32)
        left = jnp.where(where // LANES == column, 1.0, 0.0)
        right = jnp.where(where % LANES == column, 1.0, 0.0)
        part = dot_rows(left.astype(BF16), (right * float(at)).astype(BF16))
        high = part if high is None else high + part
        part = dot_rows(left.astype(BF16), (right * row.astype(F32)).astype(BF16))
        total = part if total is None else total + part
    number = high * float(LANES) + total
    out[...] = number[: out.shape[0], : out.shape[1]].astype(jnp.int32)


def group_order(names, groups):
    edges = names.shape[0]
    rows = pl.cdiv(pl.cdiv(edges, LANES), 8) * 8
    padded = jnp.pad(names, (0, rows * LANES - edges), constant_values=groups)
    out = small_call(
        functools.partial(order_kernel, groups, edges // groups),
        (padded.reshape(rows, LANES),), [((edges // LANES, LANES), jnp.int32)], "group_order",
    )[0]
    return out.reshape(1, edges)


def spread(column, width):
    return jnp.concatenate([column] * (width // LANES), axis=1)


def norm(value):
    centre = value - jnp.mean(value, -1, keepdims=True)
    scale = lax.rsqrt(jnp.mean(centre * centre, -1, keepdims=True) + EPS)
    return centre * scale, scale


def norm_back(inner, normed, scale):
    mean_first = jnp.mean(inner, -1, keepdims=True)
    mean_second = jnp.mean(inner * normed, -1, keepdims=True)
    return scale * (inner - mean_first - normed * mean_second)


def column_sum(value):
    return jnp.sum(value, axis=0, keepdims=True)


def whole(*_):
    return (0, 0)


def const_spec(shape):
    return pl.BlockSpec(shape, lambda *_: (0,) * len(shape), pipeline_mode=pl.Buffered(1))


def small_call(kernel, args, shapes, name, scratch=(), flops=0, moved=0, exps=0, scalars=0):
    return pl.pallas_call(
        kernel,
        grid=(1,),
        in_specs=[pl.BlockSpec(memory_space=pltpu.SMEM)] * scalars
        + [const_spec(a.shape) for a in args[scalars:]],
        out_specs=[pl.BlockSpec(s, lambda *_, n=len(s): (0,) * n) for s, _ in shapes],
        out_shape=[jax.ShapeDtypeStruct(*s) for s in shapes],
        scratch_shapes=list(scratch),
        compiler_params=pltpu.CompilerParams(vmem_limit_bytes=VMEM),
        name=name,
        cost_estimate=pl.CostEstimate(flops=flops, bytes_accessed=moved, transcendentals=exps),
    )(*args)


def tile_count(shape):
    return pl.cdiv(shape[0], 16) * pl.cdiv(shape[1], LANES)


def all_tiles(shapes):
    return sum(tile_count(s) for s in shapes)


def pack(slab, values, at=0):
    for value in values:
        rows, columns = value.shape
        count = rows // 16
        for first in range(0, columns, LANES):
            take = min(LANES, columns - first)
            tile = value[:, first : first + take].astype(BF16).reshape(count, 16, take)
            slab[at : at + count, :, :take] = tile
            at += count


def unpack(slab, at, rows, columns):
    count = rows // 16
    parts = [
        slab[at + i * count : at + (i + 1) * count].reshape(rows, LANES).astype(F32)
        for i in range(pl.cdiv(columns, LANES))
    ]
    return jnp.concatenate(parts, axis=1)


def order_out(slab, base, codes, keep, send):
    size = slab.shape[0] // len(codes)
    half = len(codes) // 2
    for place, code in enumerate(codes):
        out = keep if place < half else send
        at = (place % half) * size
        out[at : at + size] = slab[pl.ds((base ^ code) * size, size)]


def half_shapes(tiles):
    return [((tiles // 2, 16, LANES), BF16)] * 2


def slab_scratch(tiles):
    return pltpu.VMEM((tiles, 16, LANES), BF16)


def slab_tiles(shapes, chunks):
    return pl.cdiv(all_tiles(shapes), chunks)


def order_in(slab, base, codes, first, second):
    size = slab.shape[0] // len(codes)
    half = len(codes) // 2
    for place, code in enumerate(codes):
        source = first if place < half else second
        at = (place % half) * size
        slab[pl.ds((base ^ code) * size, size)] = source[at : at + size]


def padded_rows(parts, width):
    return jnp.concatenate(parts + [jnp.zeros((16 - len(parts), width), F32)], axis=0)


def slot_block(slots):
    for size in (10, 12, 8, 6, 5, 4, 3, 2):
        if slots % size == 0:
            return size
    return 1


def far_table(node_lo, node_hi, weights, put):
    tile = min(512, node_lo.shape[0])
    for source, start in ((node_lo, 0), (node_hi, node_lo.shape[0])):
        def body(i, carry, source=source, start=start):
            at = pl.multiple_of(i * tile, tile)
            put(start + at, dot(source[pl.ds(at, tile), :], weights))
            return carry
        lax.fori_loop(0, source.shape[0] // tile, body, 0)


def message_forward_kernel(
    sb, by_rows, node_lo, node_hi, node_own, edge, idx_row, names, live_col, m1, b1, m2, b2,
    a1_out, s1_out, s2_out, sum_out, table, far, near, lhs, z,
):
    step = pl.program_id(0)
    width = node_own.shape[1]
    edge_width = edge.shape[2]
    rows = edge.shape[1]
    block = sb * rows
    lanes = width // LANES

    @pl.when(step == 0)
    def _():
        weights = m1[width + edge_width :, :]
        if by_rows:
            def put(first, value):
                for at in range(8):
                    column = at % lanes * LANES
                    table[pl.ds(first * 8 + at, value.shape[0], stride=8), :] = value[
                        :, column : column + LANES
                    ]
        else:
            def put(first, value):
                table[pl.ds(first, value.shape[0]), :] = value.astype(BF16)
        far_table(node_lo, node_hi, weights, put)
        near[:edge_width, :] = m1[width : width + edge_width, :]
        near[edge_width:, :] = jnp.zeros_like(near[edge_width:, :])
        near[edge_width : edge_width + rows, :] = (
            dot(node_own[...], m1[:width, :]) + b1[...]
        ).astype(BF16)
        shape = (rows, near.shape[0] - edge_width)
        eye = lax.broadcasted_iota(jnp.int32, shape, 0) == lax.broadcasted_iota(jnp.int32, shape, 1)
        for at in range(0, block, rows):
            lhs[at : at + rows, edge_width:] = jnp.where(eye, 1.0, 0.0).astype(BF16)
        sum_out[...] = jnp.zeros_like(sum_out)

    lhs[:, :edge_width] = edge[...].reshape(block, edge_width)
    z[...] = dot(lhs[...], near[...])
    if not by_rows:
        z[...] += pick_rows(index_columns(idx_row[...]), (table,))
    upper = lax.broadcasted_iota(jnp.int32, (8, LANES), 0) < lanes

    def fetch(at):
        for e in range(at, at + 16, 2):
            pair = [
                table[pl.ds(pl.multiple_of(names[0, step * block + e + i] * 8, 8), 8), :]
                for i in range(2)
            ]
            far[e * lanes : e * lanes + 8, :] = jnp.where(upper, *pair)

    def fetched(at):
        return jnp.concatenate(
            [far[pl.ds(at * lanes + j, 16, stride=lanes), :] for j in range(lanes)], axis=1
        )

    if by_rows:
        fetch(0)
    for at in range(0, block, 16):
        value = z[at : at + 16, :]
        if by_rows:
            if at + 16 < block:
                fetch(at + 16)
            value = value + fetched(at)
        act, slope = gelu_parts(value)
        a1_out[at : at + 16, :] = act.astype(BF16)
        s1_out[at : at + 16, :] = slope.astype(BF16)
    z[...] = dot(a1_out[...], m2[...])
    bias = b2[...]
    for row in range(0, rows, 16):
        count = live_col[row : row + 16, :]
        inverse = 1.0 / count.astype(F32)
        total = sum_out[row : row + 16, :]
        for s in range(sb):
            at = s * rows + row
            act, slope = gelu_parts(z[at : at + 16, :] + bias)
            s2_out[at : at + 16, :] = slope.astype(BF16)
            share = jnp.where(count > step * sb + s, inverse, 0.0)
            total = total + act.astype(BF16).astype(F32) * spread(share, width)
        sum_out[row : row + 16, :] = total


def message_forward(node_lo, node_hi, node_own, edge, idx_row, live_col, m1, b1, m2, b2):
    slots, rows, edge_width = edge.shape
    width = node_own.shape[1]
    residues = 2 * node_lo.shape[0]
    by_rows = residues <= 4096 and width == 4 * LANES
    sb = slot_block(slots) if by_rows else 4
    block = sb * rows
    edges = slots * rows
    near = pl.cdiv(edge_width + rows, LANES) * LANES
    row_spec = pl.BlockSpec((block, width), lambda i: (i, 0))
    return pl.pallas_call(
        functools.partial(message_forward_kernel, sb, by_rows),
        grid=(slots // sb,),
        in_specs=[
            const_spec(node_lo.shape),
            const_spec(node_hi.shape),
            const_spec(node_own.shape),
            pl.BlockSpec((sb, rows, edge_width), lambda i: (i, 0, 0)),
            pl.BlockSpec((1, block), lambda i: (0, i)),
            pl.BlockSpec(memory_space=pltpu.SMEM),
            const_spec(live_col.shape),
            const_spec(m1.shape),
            const_spec(b1.shape),
            const_spec(m2.shape),
            const_spec(b2.shape),
        ],
        out_specs=[row_spec, row_spec, row_spec, pl.BlockSpec((rows, width), whole)],
        out_shape=[jax.ShapeDtypeStruct((edges, width), BF16)] * 3
        + [jax.ShapeDtypeStruct((rows, width), F32)],
        scratch_shapes=[
            pltpu.VMEM((residues * 8, LANES), F32) if by_rows else pltpu.VMEM((residues, width), BF16),
            pltpu.VMEM((block * 4 if by_rows else 8, LANES), F32),
            pltpu.VMEM((near, width), BF16),
            pltpu.VMEM((block, near), BF16),
            pltpu.VMEM((block, width), F32),
        ],
        compiler_params=pltpu.CompilerParams(vmem_limit_bytes=VMEM),
        name="message_forward",
        cost_estimate=pl.CostEstimate(
            flops=2 * edges * width * (residues + edge_width + width),
            bytes_accessed=edges * width * 6 + edges * edge_width * 2 + edges * LANES * 4,
            transcendentals=2 * edges * width,
        ),
    )(node_lo, node_hi, node_own, edge, idx_row, idx_row, live_col, m1, b1, m2, b2)


def residue_forward_kernel(parts, node, total, m3, b3, g1, fb2, g2, e_first, e_far, eb, *refs):
    f1, f2 = refs[:parts], refs[parts : 2 * parts]
    h1b_out, n1_out, sc1_out, n2_out, sc2_out, slope_out, h2b_out, far_out, own_out = refs[2 * parts :]
    width, hidden = node.shape[1], f1[0].shape[1]
    u1 = node[...].astype(F32) + fine(dot, total[...], m3[...]) + b3[...]
    n1, sc1 = norm(u1)
    h1 = n1 * g1[...]
    h1b = h1.astype(BF16)
    h1b_out[...] = h1b
    n1_out[...] = n1
    sc1_out[...] = jnp.broadcast_to(sc1, sc1_out.shape)
    y2 = None
    for p in range(parts):
        bias = f1[p][width : width + 16, :].astype(F32)
        bias = bias[0:1] + bias[1:2] + bias[2:3]
        act, slope = gelu_parts(dot(h1b, f1[p][:width, :]) + bias)
        slope_out[:, p * hidden : (p + 1) * hidden] = slope
        part = dot(act.astype(BF16), f2[p][...])
        y2 = part if y2 is None else y2 + part
    n2, sc2 = norm(h1 + (y2 + fb2[...]))
    h2b = (n2 * g2[...]).astype(BF16)
    n2_out[...] = n2
    sc2_out[...] = jnp.broadcast_to(sc2, sc2_out.shape)
    h2b_out[...] = h2b
    far_out[...] = dot_back(h2b, e_far[...]).astype(BF16)
    own_out[...] = dot_back(h2b, e_first[:, :width]) + eb[...]


def residue_forward(node, total, m3, b3, g1, fb2, g2, e_first, e_far, eb, f1, f2):
    rows, width = node.shape
    edge_width = e_first.shape[0]
    hidden = len(f1) * f1[0].shape[1]
    shapes = [
        ((rows, width), BF16),
        ((rows, width), F32),
        ((rows, LANES), F32),
        ((rows, width), F32),
        ((rows, LANES), F32),
        ((rows, hidden), F32),
        ((rows, width), BF16),
        ((rows, edge_width), BF16),
        ((rows, edge_width), F32),
    ]
    return small_call(
        functools.partial(residue_forward_kernel, len(f1)),
        (node, total, m3, b3, g1, fb2, g2, e_first, e_far, eb, *f1, *f2),
        shapes, "residue_forward", flops=4 * rows * width * hidden, moved=5 * MIB,
        exps=rows * hidden,
    )


def edge_kernel(
    sb, blocks, hi_chunks, by_rows, far_lo, far_hi, own, edge, cot, idx, idx_row, names, live_col,
    e_first, e2, eb2, e3, eb3, g3,
    edge_out, act_one_out, act_two_out, low_three_out, low_two_out, low_one_out, hi_out, lo_out, own_out, gain_out,
    low_first, gs, table, far, z, slope_ref,
):
    step = pl.program_id(0)
    rows, width = own.shape
    node_width = (e_first.shape[1] - width) // 2
    e_mid = e_first.at[:, node_width : node_width + width]
    tiles = pl.cdiv(width, LANES)
    per = 8 // tiles
    size = 32

    @pl.when(step == 0)
    def _():
        own_out[...] = jnp.zeros_like(own_out)
        gs[...] = jnp.zeros_like(gs)
        half = far_lo.shape[0]
        if by_rows:
            for source, start in ((far_lo, 0), (far_hi, half)):
                for first in range(0, half, 512):
                    value = source[first : first + 512, :].astype(F32)
                    for at in range(8):
                        column = at % tiles * LANES
                        take = min(LANES, width - column)
                        table[pl.ds((start + first) * 8 + at, value.shape[0], stride=8), :take] = value[
                            :, column : column + take
                        ]

    @pl.when(step < blocks)
    def _():
        block = sb * rows
        flat = edge[...].reshape(block, width)
        z[...] = dot_back(flat, e_mid[...])
        if not by_rows:
            z[...] += pick_rows(index_columns(idx[...]), (far_lo, far_hi))
        sub = lax.broadcasted_iota(jnp.int32, (8, LANES), 0)

        def fetch(at):
            for e in range(at, at + size, per):
                got = [
                    table[pl.ds(pl.multiple_of(names[0, step * block + e + i] * 8, 8), 8), :]
                    for i in range(per)
                ]
                value = got[-1]
                for i in range(per - 2, -1, -1):
                    value = jnp.where(sub < (i + 1) * tiles, got[i], value)
                far[e * tiles : e * tiles + 8, :] = value

        def fetched(at):
            parts = [
                far[pl.ds(at * tiles + j, size, stride=tiles), :][:, : min(LANES, width - j * LANES)]
                for j in range(tiles)
            ]
            return jnp.concatenate(parts, axis=1)

        if by_rows:
            fetch(0)
        for at in range(0, block, size):
            value = z[at : at + size, :] + own[at % rows : at % rows + size, :]
            if by_rows:
                if at + size < block:
                    fetch(at + size)
                value = value + fetched(at)
            act, slope = gelu_parts(value)
            act_one_out[at : at + size, :] = act.astype(BF16)
            slope_ref[at : at + size, :] = slope
        act_one = act_one_out[...]
        act_two, slope_two = gelu_parts(dot(act_one, e2[...]) + eb2[...])
        act_two = act_two.astype(BF16)
        act_two_out[...] = act_two
        w_three = dot(act_two, e3[...]) + eb3[...]
        normed, scale = norm(flat.astype(F32) + w_three)
        count = spread(live_col[...], pl.cdiv(width, LANES) * LANES)[:, :width]
        live = jnp.concatenate(
            [jnp.where(count > step * sb + s, 1.0, 0.0) for s in range(sb)], axis=0
        )
        edge_out[...] = (normed * g3[...] * live).astype(BF16).reshape(sb, rows, width)
        grad = cot[...].reshape(block, width).astype(F32) * live
        gs[...] += jnp.sum((grad * normed).reshape(sb, rows, width), axis=0)
        low_three = norm_back(grad * g3[...], normed, scale).astype(BF16)
        low_three_out[...] = low_three
        low_two = (dot_back(low_three, e3[...]) * slope_two).astype(BF16)
        low_two_out[...] = low_two
        low_one = (dot_back(low_two, e2[...]) * slope_ref[...]).astype(BF16)
        low_one_out[...] = low_one
        own_out[...] += jnp.sum(low_one.astype(F32).reshape(sb, rows, width), axis=0)
        low_first[pl.ds(pl.multiple_of(step * block, block), block), :] = low_one

    chunk = hi_out.shape[0]

    @pl.when((step >= blocks) & (step < blocks + hi_chunks))
    def _():
        start = (step - blocks + hi_chunks) * chunk
        hi_out[...] = dot(one_hot_rows(idx_row[...], start, chunk), low_first[...]).astype(BF16)

    @pl.when(step >= blocks + hi_chunks)
    def _():
        start = (step - blocks - hi_chunks) * chunk
        lo_out[...] = dot(one_hot_rows(idx_row[...], start, chunk), low_first[...])

    @pl.when(step == blocks + 2 * hi_chunks - 1)
    def _():
        gain_out[...] = column_sum(gs[...])


def edge_branch(far_lo, far_hi, own, edge, cot, idx_row, live_col, e_first, e2, eb2, e3, eb3, g3):
    slots, rows, width = edge.shape
    sb = slot_block(slots)
    edges = slots * rows
    block = sb * rows
    blocks = slots // sb
    half = far_lo.shape[0]
    chunk = min(512, half)
    hi_chunks = half // chunk
    by_rows = half <= 2048 and 8 % pl.cdiv(width, LANES) == 0
    blk = lambda i: jnp.minimum(i, blocks - 1)
    hi_at = lambda i: (jnp.clip(i - blocks, 0, hi_chunks - 1), 0)
    lo_at = lambda i: (jnp.clip(i - blocks - hi_chunks, 0, hi_chunks - 1), 0)
    slot_spec = pl.BlockSpec((sb, rows, width), lambda i: (blk(i), 0, 0))
    row_spec = pl.BlockSpec((block, width), lambda i: (blk(i), 0))
    return pl.pallas_call(
        functools.partial(edge_kernel, sb, blocks, hi_chunks, by_rows),
        grid=(blocks + 2 * hi_chunks,),
        in_specs=[
            const_spec(far_lo.shape),
            const_spec(far_hi.shape),
            const_spec(own.shape),
            slot_spec,
            slot_spec,
            pl.BlockSpec((1, block), lambda i: (0, blk(i))),
            const_spec(idx_row.shape),
            pl.BlockSpec(memory_space=pltpu.SMEM),
            const_spec(live_col.shape),
            const_spec(e_first.shape),
            const_spec(e2.shape),
            const_spec(eb2.shape),
            const_spec(e3.shape),
            const_spec(eb3.shape),
            const_spec(g3.shape),
        ],
        out_specs=[slot_spec]
        + [row_spec] * 5
        + [
            pl.BlockSpec((chunk, width), hi_at),
            pl.BlockSpec((chunk, width), lo_at),
            pl.BlockSpec((rows, width), whole),
            pl.BlockSpec((1, width), whole),
        ],
        out_shape=[jax.ShapeDtypeStruct((slots, rows, width), BF16)]
        + [jax.ShapeDtypeStruct((edges, width), BF16)] * 5
        + [
            jax.ShapeDtypeStruct((half, width), BF16),
            jax.ShapeDtypeStruct((half, width), F32),
            jax.ShapeDtypeStruct((rows, width), F32),
            jax.ShapeDtypeStruct((1, width), F32),
        ],
        scratch_shapes=[
            pltpu.VMEM((edges, width), BF16),
            pltpu.VMEM((rows, width), F32),
            pltpu.VMEM((half * 16 if by_rows else 8, LANES), F32),
            pltpu.VMEM((block * 8, LANES), F32),
            pltpu.VMEM((block, width), F32),
            pltpu.VMEM((block, width), F32),
        ],
        compiler_params=pltpu.CompilerParams(vmem_limit_bytes=VMEM),
        name="edge_branch",
        cost_estimate=pl.CostEstimate(
            flops=2 * edges * width * (4 * half + 5 * width),
            bytes_accessed=edges * width * 16,
            transcendentals=2 * edges * width,
        ),
    )(far_lo, far_hi, own, edge, cot, idx_row, idx_row, idx_row, live_col, e_first, e2, eb2, e3, eb3, g3)


def edge_weights_kernel(blocks, pairs, *refs):
    step = pl.program_id(0)
    lefts, rights = refs[:pairs], refs[pairs : 2 * pairs]
    grads, biases, sums = refs[2 * pairs : 3 * pairs], refs[3 * pairs : 4 * pairs], refs[-1]
    rows = sums.shape[1]

    @pl.when(step == 0)
    def _():
        for ref in (*grads, sums):
            ref[...] = jnp.zeros_like(ref)

    for at in range(pairs):
        left, right = [r[...].reshape(-1, r.shape[-1]) for r in (lefts[at], rights[at])]
        grads[at][...] += dot_rows(left, right)
        low = left if lefts[at].ndim < rights[at].ndim else right
        sums[at] += jnp.sum(low.astype(F32).reshape(-1, rows, low.shape[1]), axis=0)

    @pl.when(step == blocks - 1)
    def _():
        for at in range(pairs):
            biases[at][...] = column_sum(sums[at])


def edge_weights(lefts, rights, rows):
    pairs = len(lefts)
    edges, width = lefts[0].shape
    slots = edges // rows
    sb = slot_block(slots)

    def spec(array):
        if array.ndim == 3:
            return pl.BlockSpec((sb, rows, width), lambda i: (i, 0, 0))
        return pl.BlockSpec((sb * rows, width), lambda i: (i, 0))

    shapes = [(width, width)] * pairs + [(1, width)] * pairs
    return pl.pallas_call(
        functools.partial(edge_weights_kernel, slots // sb, pairs),
        grid=(slots // sb,),
        in_specs=[spec(array) for array in (*lefts, *rights)],
        out_specs=[pl.BlockSpec(s, whole) for s in shapes],
        out_shape=[jax.ShapeDtypeStruct(s, F32) for s in shapes],
        scratch_shapes=[pltpu.VMEM((pairs, rows, width), F32)],
        compiler_params=pltpu.CompilerParams(vmem_limit_bytes=VMEM),
        name="edge_weights",
        cost_estimate=pl.CostEstimate(
            flops=2 * pairs * edges * width * width,
            bytes_accessed=pairs * edges * width * 4,
            transcendentals=0,
        ),
    )(*lefts, *rights)


def early_shapes(width, edge_width):
    return [
        (width, width),
        (edge_width, width),
        (edge_width, width),
        (edge_width, edge_width),
        (edge_width, edge_width),
        (16, width),
        (16, edge_width),
    ]


def residue_backward_kernel(
    parts, pieces, node_cot, own_sum, e_first, e_far, h1b, h2b, n1, sc1, n2, sc2, slope, g1, g2, m3,
    total, e2g, e3g, eb2, eb3, edge_gain, *refs,
):
    far = refs[:pieces]
    f1 = refs[pieces : pieces + parts]
    f2 = refs[pieces + parts : pieces + 2 * parts]
    gu1_out, v_out, both_out, slab = refs[pieces + 2 * parts :]
    width, hidden = h2b.shape[1], f1[0].shape[1]
    far_sum = far[0][: far[1].shape[0], :]
    for ref in far[1:]:
        far_sum = far_sum + ref[...].astype(F32)
    own = own_sum[...]
    g_h2 = (
        node_cot[...].astype(F32)
        + fine(dot, own, e_first[:, :width])
        + fine(dot, far_sum, e_far[...])
    )
    gain_two = column_sum(g_h2 * n2[...])
    g_u2 = norm_back(g_h2 * g2[...], n2[...], sc2[:, :1])
    gy2 = g_u2.astype(BF16)
    both_out[:, :width] = h1b[...]
    both_out[:, width:] = gy2
    g_h1 = g_u2
    for p in range(parts):
        gy1 = dot_back(gy2, f2[p][...]) * slope[:, p * hidden : (p + 1) * hidden]
        g_h1 = g_h1 + dot_back(gy1.astype(BF16), f1[p][:width, :])
    gain_one = column_sum(g_h1 * n1[...])
    g_u1 = norm_back(g_h1 * g1[...], n1[...], sc1[:, :1])
    gu1_out[...] = g_u1
    v_out[...] = fine(dot_back, g_u1, m3[...])
    bias = [gain_one, gain_two, column_sum(gy2.astype(F32)), column_sum(g_u1)]
    slab[...] = jnp.zeros_like(slab)
    pack(
        slab,
        [
            dot_rows(total[...].astype(BF16), g_u1.astype(BF16)),
            dot_rows(own.astype(BF16), h2b[...]),
            dot_rows(far_sum.astype(BF16), h2b[...]),
            e2g[...],
            e3g[...],
            padded_rows(bias, width),
            padded_rows([eb2[...], eb3[...], edge_gain[...]], own.shape[1]),
        ],
    )


def residue_backward(args, far, f1, f2):
    node_cot, e_first, slope = args[0], args[2], args[10]
    rows, width = node_cot.shape
    shapes = [
        ((rows, width), F32),
        ((rows, width), F32),
        ((rows, 2 * width), BF16),
        ((all_tiles(early_shapes(width, e_first.shape[0])), 16, LANES), BF16),
    ]
    return small_call(
        functools.partial(residue_backward_kernel, len(f1), len(far)),
        (*args, *far, *f1, *f2),
        shapes, "residue_backward",
        flops=4 * rows * width * slope.shape[1], moved=8 * MIB,
    )


def feed_kernel(first, second, f1, fb1, f2, f1g, f2g, fb1g):
    width = f1.shape[0]

    @pl.when(pl.program_id(0) == 0)
    def _():
        for ref in (f1g, f2g, fb1g):
            ref[...] = jnp.zeros_like(ref)

    for both in (first, second):
        h1b, gy2 = both[:, :width], both[:, width:]
        act, slope = gelu_parts(dot(h1b, f1[...]) + fb1[...])
        gy1 = (dot_back(gy2, f2[...]) * slope).astype(BF16)
        f1g[...] += dot_rows(h1b, gy1)
        f2g[...] += dot_rows(act.astype(BF16), gy2)
        fb1g[...] += column_sum(gy1.astype(F32))


def feed_gradients(both, f1, fb1, f2):
    width, hidden = f1.shape
    half = both[0].shape[0]
    chunk = min(512, half)
    shapes = [(width, hidden), (hidden, width), (1, hidden)]
    return pl.pallas_call(
        feed_kernel,
        grid=(half // chunk,),
        in_specs=[pl.BlockSpec((chunk, 2 * width), lambda i: (i, 0))] * 2
        + [const_spec(a.shape) for a in (f1, fb1, f2)],
        out_specs=[pl.BlockSpec(s, whole) for s in shapes],
        out_shape=[jax.ShapeDtypeStruct(s, F32) for s in shapes],
        compiler_params=pltpu.CompilerParams(vmem_limit_bytes=VMEM),
        name="feed_gradients",
        cost_estimate=pl.CostEstimate(
            flops=16 * half * width * hidden,
            bytes_accessed=8 * half * width,
            transcendentals=2 * half * hidden,
        ),
    )(*both, f1, fb1, f2)


def late_shapes(width, edge_width):
    return [
        (width, width),
        (width, width),
        (edge_width, width),
        (16, width),
        (width, width),
        (edge_width, edge_width),
        (16, edge_width),
    ]


def weight_shapes(width, edge_width):
    return early_shapes(width, edge_width) + late_shapes(width, edge_width)


def message_backward_kernel(
    sb, blocks, groups, codes, base, order, v, a1, s1, s2, edge, low_three, low_edge, local_row, live_col,
    m1, m2, e_first, node_lo, node_hi, node, early, e1g, eb1,
    edge_grad, far_keep, far_send, own, keep, send,
    low_two, low_one, grad, rows_ref, moved, m2g, m1eg, m1fg, b2s, slab,
):
    step = pl.program_id(0)
    rows, width = v.shape
    edge_width = edge.shape[2]
    block = sb * rows
    tiles = width // LANES
    size = 16

    @pl.when(step == 0)
    def _():
        for ref in (own, m2g, m1eg, m1fg, b2s):
            ref[...] = jnp.zeros_like(ref)

    @pl.when(step < blocks)
    def _():
        for row in range(0, rows, size):
            count = live_col[row : row + size, :]
            inverse = 1.0 / count.astype(F32)
            value = v[row : row + size, :]
            total = b2s[row : row + size, :]
            for s in range(sb):
                at = s * rows + row
                share = jnp.where(count > step * sb + s, inverse, 0.0)
                low = (value * spread(share, width) * s2[at : at + size, :].astype(F32)).astype(BF16)
                low_two[at : at + size, :] = low
                total = total + low.astype(F32)
            b2s[row : row + size, :] = total
        grad[...] = dot_back(low_two[...], m2[...])
        m2g[...] += dot_rows(a1[...], low_two[...])
        first = pl.multiple_of(step * (block * 8), 8)
        rows_ref[pl.ds(first + tiles, block, stride=8), :] = index_columns(local_row[...]).astype(F32)
        for row in range(0, rows, size):
            total = own[row : row + size, :]
            for s in range(sb):
                at = s * rows + row
                low = (grad[at : at + size, :] * s1[at : at + size, :].astype(F32)).astype(BF16)
                low_one[at : at + size, :] = low
                low = low.astype(F32)
                total = total + low
                for j in range(tiles):
                    rows_ref[pl.ds(first + at * 8 + j, size, stride=8), :] = low[
                        :, j * LANES : (j + 1) * LANES
                    ]
            own[row : row + size, :] = total
        m1eg[...] += dot_rows(edge[...].reshape(block, edge_width), low_one[...])
        total = (
            low_three[...].astype(F32)
            + dot(low_edge[...], e_first[:, width : width + edge_width])
            + dot_back(low_one[...], m1[width : width + edge_width, :])
        )
        edge_grad[...] = total.reshape(sb, rows, edge_width)

    @pl.when(step >= blocks)
    def _():
        deep = far_keep.shape[0]
        count = block * blocks // groups
        values, local = group_rows(order, (step - blocks) * count, count, rows_ref, moved, width)
        sums = group_sums(values, local, 2 * deep * rows).astype(BF16)
        near = jnp.concatenate(
            [ref[at, 0] for ref in (node_lo, node_hi) for at in range(deep)], axis=0
        )
        m1fg[...] += dot_rows(near, sums)
        height = rows // 16
        for at in range(2 * deep):
            out = (far_keep if at < deep else far_send).at[at % deep, 0]
            for j in range(tiles):
                tile = sums[at * rows : (at + 1) * rows, j * LANES : (j + 1) * LANES]
                out[j * height : (j + 1) * height] = tile.reshape(height, 16, LANES)

    @pl.when(step == blocks + groups - 1)
    def _():
        count = early.shape[0]
        slab[:count] = early[...]
        slab[count:] = jnp.zeros_like(slab[count:])
        pack(
            slab,
            [
                dot_rows(node[...], own[...].astype(BF16)),
                m2g[...],
                m1eg[...],
                padded_rows([column_sum(own[...]), column_sum(b2s[...])], width),
                m1fg[...],
                e1g[...],
                padded_rows([eb1[...]], edge_width),
            ],
            count,
        )
        order_out(slab, base[0], codes, keep, send)


def message_backward(
    groups, codes, base, order, v, a1, s1, s2, edge, low_three, low_edge, local_row, live_col, m1, m2,
    e_first, node_lo, node_hi, node, early, e1g, eb1,
):
    slots, rows, edge_width = edge.shape
    width = v.shape[1]
    sb = slot_block(slots)
    block = sb * rows
    blocks = slots // sb
    edges = slots * rows
    half = node_lo.shape[0]
    deep = half // rows // groups
    tiles = rows * width // (16 * LANES)
    slab = slab_tiles(weight_shapes(width, edge_width), len(codes)) * len(codes)
    node_lo, node_hi = [n.reshape(deep, groups, rows, width) for n in (node_lo, node_hi)]
    blk = lambda i: jnp.minimum(i, blocks - 1)
    group_at = lambda i: (0, jnp.maximum(i - blocks, 0))
    row_spec = pl.BlockSpec((block, width), lambda i: (blk(i), 0))
    slot_spec = pl.BlockSpec((sb, rows, edge_width), lambda i: (blk(i), 0, 0))
    edge_spec = pl.BlockSpec((block, edge_width), lambda i: (blk(i), 0))
    node_spec = pl.BlockSpec((deep, 1, rows, width), lambda i: (*group_at(i), 0, 0))
    far_spec = pl.BlockSpec((deep, 1, tiles, 16, LANES), lambda i: (*group_at(i), 0, 0, 0))
    slab_spec = pl.BlockSpec((slab // 2, 16, LANES), lambda i: (0, 0, 0))
    smem = pl.BlockSpec(memory_space=pltpu.SMEM)
    return pl.pallas_call(
        functools.partial(message_backward_kernel, sb, blocks, groups, codes),
        grid=(blocks + groups,),
        in_specs=[
            smem,
            smem,
            const_spec(v.shape),
            row_spec,
            row_spec,
            row_spec,
            slot_spec,
            edge_spec,
            edge_spec,
            pl.BlockSpec((1, block), lambda i: (0, blk(i))),
            const_spec(live_col.shape),
            const_spec(m1.shape),
            const_spec(m2.shape),
            const_spec(e_first.shape),
            node_spec,
            node_spec,
            const_spec(node.shape),
            const_spec(early.shape),
            const_spec(e1g.shape),
            const_spec(eb1.shape),
        ],
        out_specs=[slot_spec, far_spec, far_spec, pl.BlockSpec((rows, width), whole), slab_spec, slab_spec],
        out_shape=[
            jax.ShapeDtypeStruct((slots, rows, edge_width), F32),
            jax.ShapeDtypeStruct((deep, groups, tiles, 16, LANES), BF16),
            jax.ShapeDtypeStruct((deep, groups, tiles, 16, LANES), BF16),
            jax.ShapeDtypeStruct((rows, width), F32),
            jax.ShapeDtypeStruct((slab // 2, 16, LANES), BF16),
            jax.ShapeDtypeStruct((slab // 2, 16, LANES), BF16),
        ],
        scratch_shapes=[
            pltpu.VMEM((block, width), BF16),
            pltpu.VMEM((block, width), BF16),
            pltpu.VMEM((block, width), F32),
            pltpu.VMEM((edges * 8, LANES), F32),
            pltpu.VMEM((edges // groups * 8, LANES), F32),
            pltpu.VMEM((width, width), F32),
            pltpu.VMEM((edge_width, width), F32),
            pltpu.VMEM((width, width), F32),
            pltpu.VMEM((rows, width), F32),
            slab_scratch(slab),
        ],
        compiler_params=pltpu.CompilerParams(vmem_limit_bytes=VMEM),
        name="message_backward",
        cost_estimate=pl.CostEstimate(
            flops=2 * edges * width * (2 * width + 3 * edge_width + half // groups),
            bytes_accessed=edges * width * 6 + edges * edge_width * 10,
            transcendentals=0,
        ),
    )(
        base, order, v, a1, s1, s2, edge, low_three, low_edge, local_row, live_col, m1, m2, e_first,
        node_lo, node_hi, node, early, e1g, eb1,
    )


def node_kernel(pieces, g_u1, own, m1, *refs):
    far, grad_out = refs[:pieces], refs[pieces]
    rows, width = own.shape
    height = rows // 16
    tiles = height * (width // LANES)
    sums = far[0][:tiles].astype(F32)
    for ref in far[1:]:
        sums = sums + ref[:tiles].astype(F32)
    far_sum = jnp.concatenate(
        [sums[j * height : (j + 1) * height].reshape(rows, LANES) for j in range(width // LANES)],
        axis=1,
    )
    far_first = m1.shape[0] - width
    grad_out[...] = (
        g_u1[...]
        + fine(dot_back, own[...], m1[:width, :])
        + fine(dot_back, far_sum, m1[far_first:, :])
    )


def node_last(g_u1, own, m1, far):
    return small_call(
        functools.partial(node_kernel, len(far)),
        (g_u1, own, m1, *far), [(own.shape, F32)], "node_gradient",
        flops=8 * own.size * own.shape[1], moved=2 * MIB,
    )[0]


def weights_out_kernel(
    codes, base, first, second,
    m1g, b1, m2g, b2, m3g, e1g, e2g, e3g, b3, g1, g2, fb2, eb1, eb2, eb3, g3, slab,
):
    order_in(slab, base[0], codes, first, second)
    width, edge_width = m3g.shape[0], e2g.shape[0]
    shapes = weight_shapes(width, edge_width)
    starts = [all_tiles(shapes[:at]) for at in range(len(shapes))]
    m3g[...] = unpack(slab, starts[0], width, width)
    e1g[:, :width] = unpack(slab, starts[1], edge_width, width)
    middle = unpack(slab, starts[12], edge_width, edge_width)
    far = unpack(slab, starts[2], edge_width, width)
    over = edge_width % LANES
    base_col = width + edge_width - over
    e1g[:, width:base_col] = middle[:, : edge_width - over]
    far = pltpu.roll(jnp.concatenate([far, jnp.zeros((edge_width, LANES), F32)], axis=1), over, 1)
    lane = lax.broadcasted_iota(jnp.int32, (edge_width, LANES), 1)
    e1g[:, base_col : base_col + LANES] = jnp.where(
        lane < over, middle[:, edge_width - over : edge_width - over + LANES], far[:, :LANES]
    )
    rest = e1g.shape[1] - base_col - LANES
    e1g[:, base_col + LANES :] = far[:, LANES : LANES + rest]
    e2g[...] = unpack(slab, starts[3], edge_width, edge_width)[:, :edge_width]
    e3g[...] = unpack(slab, starts[4], edge_width, edge_width)[:, :edge_width]
    bias = unpack(slab, starts[5], 16, width)
    for row, out in enumerate((g1, g2, fb2, b3)):
        out[...] = bias[row : row + 1]
    bias = unpack(slab, starts[6], 16, edge_width)
    for row, out in enumerate((eb2, eb3, g3)):
        out[...] = bias[row : row + 1, :edge_width]
    m1g[:width, :] = unpack(slab, starts[7], width, width)
    m2g[...] = unpack(slab, starts[8], width, width)
    m1g[width : width + edge_width, :] = unpack(slab, starts[9], edge_width, width)
    bias = unpack(slab, starts[10], 16, width)
    b1[...] = bias[0:1]
    b2[...] = bias[1:2]
    eb1[...] = unpack(slab, starts[13], 16, edge_width)[:1, :edge_width]
    m1g[width + edge_width :, :] = unpack(slab, starts[11], width, width)


def weights_out(codes, base, halves_in, width, edge_width):
    shapes = [(2 * width + edge_width, width), (1, width), (width, width), (1, width)]
    shapes += [(width, width), (edge_width, 2 * width + edge_width)]
    shapes += [(edge_width, edge_width)] * 2 + [(1, width)] * 4 + [(1, edge_width)] * 4
    tiles = slab_tiles(weight_shapes(width, edge_width), len(codes)) * len(codes)
    return small_call(
        functools.partial(weights_out_kernel, codes),
        (base, *halves_in), [(s, F32) for s in shapes], "weight_gradients",
        [slab_scratch(tiles)], moved=10 * MIB, scalars=1,
    )


def exchange(value, mask, devices):
    return lax.ppermute(value, AXES, [(d, d ^ mask) for d in range(devices)])


def mask_groups(masks):
    return [masks[i : min(i + 2, len(masks) - 1)] for i in range(0, len(masks) - 1, 2)] + [masks[-1:]]


def order_codes(groups):
    masks = [mask for group in groups for mask in group]
    return [
        sum(mask for bit, mask in enumerate(masks) if place >> bit & 1)
        for place in range(1 << len(masks))
    ]


def combined(group, code):
    return sum(mask for bit, mask in enumerate(group) if code >> bit & 1)


def sent_around(value, group, devices):
    return [value] + [
        exchange(value, combined(group, code), devices) for code in range(1, 1 << len(group))
    ]


def shared_out(total, group, devices):
    parts = 1 << len(group)
    rows = total.shape[0] // parts
    return [total] + [
        exchange(total[code * rows : (code + 1) * rows].astype(BF16), combined(group, code), devices)
        for code in range(1, parts)
    ]


def add_up(terms):
    total = terms[0][: terms[1].shape[0]].astype(F32)
    for term in terms[1:]:
        total = total + term.astype(F32)
    return total


def tied(*values):
    return lax.optimization_barrier(values)


def split_three(value):
    rows = []
    for _ in range(3):
        high = lax.reduce_precision(value, 8, 7)
        rows.append(high.astype(BF16))
        value = value - high
    return jnp.concatenate(rows + [jnp.zeros((13, value.shape[1]), BF16)], axis=0)


def per_device(
    node_in,
    edge_in,
    neighbours,
    live_counts,
    message_first,
    message_first_bias,
    message_second,
    message_second_bias,
    message_third,
    message_third_bias,
    norm_one,
    feed_first,
    feed_first_bias,
    feed_second,
    feed_second_bias,
    norm_two,
    edge_first,
    edge_first_bias,
    edge_second,
    edge_second_bias,
    edge_third,
    edge_third_bias,
    norm_three,
    node_cotangent,
    edge_cotangent,
):
    rows, slots = neighbours.shape
    width = node_in.shape[1]
    edge_width = edge_in.shape[2]
    edges = rows * slots
    hid_count = lax.axis_size("hid")
    res_count = lax.axis_size("res")
    devices = res_count * hid_count
    bits = devices.bit_length() - 1
    masks = [1 << b for b in range(bits - 1, -1, -1)]
    groups = mask_groups(masks)
    codes = order_codes(groups)
    me = lax.axis_index("res") * hid_count + lax.axis_index("hid")
    base = me.reshape(1)
    row = lambda vector: vector.reshape(1, -1)

    names = neighbours.T.reshape(edges)
    apart = (names // rows) ^ me
    place = jnp.zeros_like(names)
    for bit, mask in enumerate(masks):
        place = place | jnp.where((apart & mask) != 0, 1 << bit, 0)
    idx_row = (place * rows + names % rows).reshape(1, edges)
    res_count = devices // hid_count
    local_row = (place // res_count * rows + names % rows).reshape(1, edges)
    edge_order = group_order(place % res_count, res_count)
    live_col = jnp.broadcast_to(live_counts[:, None], (rows, LANES))
    edge = edge_in.transpose(1, 0, 2)
    cot = edge_cotangent.transpose(1, 0, 2)
    e_first = edge_first.T
    e_far = e_first[:, width + edge_width :]
    f1x = jnp.concatenate([feed_first, split_three(row(feed_first_bias))], axis=0)
    f2x = feed_second

    stack = lambda pieces: jnp.concatenate(pieces, axis=0)
    *outer, near = groups

    held = stack(sent_around(node_in, outer[0], devices))
    held, idx_row, local_row = tied(held, idx_row, local_row)
    for group in outer[1:]:
        held = stack(sent_around(held, group, devices))
    held, f1x, f2x, edge_order, live_col = tied(held, f1x, f2x, edge_order, live_col)
    node_lo, node_hi = sent_around(held, near, devices)

    f1, f2 = [f1x], [f2x]
    hid_masks = [m for m in masks if m < hid_count]
    for mask in hid_masks[:-1]:
        f1, f2 = [pieces + [exchange(p, mask, devices) for p in pieces] for pieces in (f1, f2)]

    a1, s1, s2, total = message_forward(
        node_lo, node_hi, node_in, edge, idx_row, live_col, message_first,
        row(message_first_bias), message_second, row(message_second_bias),
    )
    total, f1, f2, e_far = tied(total, f1, f2, e_far)
    f1, f2 = [
        pieces + [exchange(p, hid_masks[-1], devices) for p in pieces] for pieces in (f1, f2)
    ]
    h1b, n1, sc1, n2, sc2, slope, h2b, far_part, own_part = residue_forward(
        node_in, total, message_third, row(message_third_bias), row(norm_one),
        row(feed_second_bias), row(norm_two), e_first, e_far, row(edge_first_bias), f1, f2,
    )

    held = stack(sent_around(far_part, outer[0], devices))
    for group in outer[1:]:
        held = stack(sent_around(held, group, devices))
    q_lo, q_hi = sent_around(held, near, devices)

    edge_out, act_one, act_two, low_three, low_two, low_one, hi, lo, own_sum, edge_gain = edge_branch(
        q_lo, q_hi, own_part, edge, cot, idx_row, live_col, e_first,
        edge_second, row(edge_second_bias), edge_third, row(edge_third_bias), row(norm_three),
    )

    terms = [lo, exchange(hi, near[0], devices)]
    made = None
    for group in reversed(outer):
        terms = shared_out(add_up(terms), group, devices)
        if made is None:
            made = edge_weights((act_two, act_one), (low_three, low_two), rows)
            terms, made = tied(terms, made)
    e3g, e2g, eb3, eb2 = made
    g_u1, v, both, early = residue_backward(
        (
            node_cotangent, own_sum, e_first, e_far, h1b, h2b, n1, sc1, n2, sc2, slope, row(norm_one),
            row(norm_two), message_third, total, e2g, e3g, eb2, eb3, edge_gain,
        ),
        terms, f1, f2,
    )

    both, low_here = tied(both, low_one)
    b_held = stack(sent_around(both, outer[0], devices))
    e1g, eb1 = edge_weights((low_here,), (edge,), rows)
    v, b_held, e1g, eb1 = tied(v, b_held, e1g, eb1)
    for group in outer[1:]:
        b_held = stack(sent_around(b_held, group, devices))
    edge_grad, far_keep, far_send, own, keep, send = message_backward(
        res_count, codes, base, edge_order, v, a1, s1, s2, edge, low_three, low_one, local_row, live_col,
        message_first, message_second, e_first, node_lo, node_hi, node_in, early, e1g, eb1,
    )
    keep, send, far_keep, far_send, b_held = tied(keep, send, far_keep, far_send, b_held)

    first, *others = reversed(outer)
    terms = [keep, exchange(send, near[0], devices)]
    total, b_held, far_send = tied(add_up(terms), b_held, far_send)
    terms = shared_out(total, first, devices)
    far_keep, far_send = [far.reshape(-1, 16, LANES) for far in (far_keep, far_send)]
    far_terms = [far_keep, exchange(far_send, near[0], devices)]
    b_near = sent_around(b_held, near, devices)
    total, b_first = tied(add_up(far_terms), b_near[0])
    far_terms = shared_out(total, first, devices)
    feed = feed_gradients((b_first, b_near[1]), feed_first, row(feed_first_bias), feed_second)
    terms, (f1g, f2g, fb1g) = tied(terms, feed)
    for group in others:
        terms = shared_out(add_up(terms), group, devices)
    held, *far_terms[:3] = tied(add_up(terms).astype(BF16), *far_terms[:3])

    for at, group in enumerate(outer):
        around = sent_around(held, group, devices)
        if at + 1 == len(outer):
            around, node_gradient = tied(around, node_last(g_u1, own, message_first, far_terms))
        held = stack(around)
        if at < len(others):
            held, *far_terms = tied(held, *far_terms)
            far_terms = shared_out(add_up(far_terms), others[at], devices)
    m1g, b1, m2g, b2, m3g, e1g, e2g, e3g, b3, g1, g2, fb2, eb1, eb2, eb3, g3 = weights_out(
        codes, base, sent_around(held, near, devices), width, edge_width
    )
    flat = lambda vector: vector.reshape(-1)
    return (
        h2b,
        edge_out.transpose(1, 0, 2),
        node_gradient,
        edge_grad.transpose(1, 0, 2),
        m1g,
        flat(b1),
        m2g,
        flat(b2),
        m3g,
        flat(b3),
        flat(g1),
        f1g,
        flat(fb1g),
        f2g,
        flat(fb2),
        flat(g2),
        e1g.T,
        flat(eb1),
        e2g,
        flat(eb2),
        e3g,
        flat(eb3),
        flat(g3),
    )


def solution(mesh):
    nodes, edges, shared = P(AXES, None), P(AXES, None, None), P()
    return jax.shard_map(
        per_device,
        mesh=mesh,
        in_specs=(nodes, edges, nodes, P(AXES))
        + (shared,) * 7
        + (P(None, "hid"), P("hid"), P("hid", None))
        + (shared,) * 9
        + (nodes, edges),
        out_specs=(nodes, edges, nodes, edges)
        + (shared,) * 7
        + (P(None, "hid"), P("hid"), P("hid", None))
        + (shared,) * 9,
        check_vma=False,
    )
```

profile of v0, /device:TPU:0, one launch (start us, length us, event | category | flops | bytes accessed | tf_op | source)
XLA Modules:
  0.0 264.0 jit_solution(10098505473595509887)
XLA Ops:
  0.7 5.1 %collective-permute-start.2 = (bf16[64,512]{1,0:T(8,128)(2,1)}, bf16[64,512]{1,0:T(8,128)(2,1)S(1)}, u32[]{:S(2)}, u32[]{:S(2)}) collective-permute-start(bf16[64,512]{1,0:T(8,128)(2,1)} %node.3), channel_id=1, source_target_pairs={{0,24},{1,25},{2,26},{3,27},{4,28},{5,29},{6,30},{7,31},{8,16},{9,... | collective-permute-start | bytes 196616 | tf_op jit(solution)/shard_map/ppermute | solution.py:1069
  12.5 2.5 collective-permute-start.5
  16.7 4.8 %group_order.1 = s32[30,128]{1,0:T(8,128)} custom-call(s32[32,128]{1,0:T(8,128)} %pad_bitcast_fusion.names), custom_call_target="tpu_custom_call" | custom-call | tf_op jit(solution)/shard_map/group_order/pallas_call | solution.py:180
  22.8 2.1 concatenate.30.refs_0_.refs_4_
  27.0 1.7 slice.110.e_far
  31.8 18.9 %message_forward.1 = (bf16[3840,512]{1,0:T(8,128)(2,1)}, bf16[3840,512]{1,0:T(8,128)(2,1)}, bf16[3840,512]{1,0:T(8,128)(2,1)}, f32[64,512]{1,0:T(8,128)}) custom-call(bf16[1024,512]{1,0:T(8,128)(2,1)} %copy-done.13, bf16[1024,512]{1,0:T(8,128)(2,1)} %copy-done.26, bf16[64,512]{1,0:T(8,128)(2,1)} %node.3, bf16[60,64,192]{2,1,0:T(8,128)(2,1)} %bitcast.48, ...), custom_call_target="tpu_custom_call" | custom-call | flops 10821304320 | bytes 15237120 | tf_op jit(solution)/shard_map/message_forward/pallas_call | solution.py:364
  50.7 4.0 %collective-permute-done.7.refs_1_.refs_5_ = bf16[528,512]{1,0:T(8,128)(2,1)S(1)} collective-permute-done((bf16[528,512]{1,0:T(8,128)(2,1)S(1)}, bf16[528,512]{1,0:T(8,128)(2,1)S(1)}, u32[]{:S(2)}, u32[]{:S(2)}) %collective-permute-start.7) | collective-permute-done | bytes 540704 | tf_op jit(solution)/shard_map/ppermute | solution.py:1069
  55.7 2.4 collective-permute-done.11.refs_6_.refs_10_
  60.1 5.4 %residue_forward.1 = (bf16[64,512]{1,0:T(8,128)(2,1)}, f32[64,512]{1,0:T(8,128)}, f32[64,128]{1,0:T(8,128)}, f32[64,512]{1,0:T(8,128)}, f32[64,128]{1,0:T(8,128)...) custom-call(bf16[64,512]{1,0:T(8,128)(2,1)} %node.3, ...), custom_call_target="tpu_custom_call" | custom-call | flops 268435456 | bytes 5242880 | tf_op jit(solution)/shard_map/residue_forward/pallas_call | solution.py:180
  65.5 2.5 collective-permute-start.15
  68.0 1.9 collective-permute-start.13
  70.7 2.7 %collective-permute-done.13 = bf16[64,192]{1,0:T(8,128)(2,1)S(1)} collective-permute-done((bf16[64,192]{1,0:T(8,128)(2,1)}, bf16[64,192]{1,0:T(8,128)(2,1)S(1)}, u32[]{:S(2)}, u32[]{:S(2)}) %collective-permute-start.13) | collective-permute-done | bytes 24608 | tf_op jit(solution)/shard_map/ppermute | solution.py:1069
  73.4 1.6 collective-permute-start.16
  77.0 1.7 collective-permute-done.16
  78.7 3.7 %collective-permute-done.17 = bf16[256,192]{1,0:T(8,128)(2,1)S(1)} collective-permute-done((bf16[256,192]{1,0:T(8,128)(2,1)S(1)}, bf16[256,192]{1,0:T(8,128)(2,1)S(1)}, u32[]{:S(2)}, u32[]{:S(2)}) %collective-permute-start.17) | collective-permute-done | bytes 98336 | tf_op jit(solution)/shard_map/ppermute | solution.py:1069
  82.5 1.9 collective-permute-done.19.far_hi
  85.2 23.7 %edge_branch.1 = (bf16[60,64,192]{2,1,0:T(8,128)(2,1)}, bf16[3840,192]{1,0:T(8,128)(2,1)}, bf16[3840,192]{1,0:T(8,128)(2,1)}, bf16[3840,192]{1,0:T(8,128)(2,1)},...) custom-call(bf16[1024,192]{1,0:T(8,128)(2,1)} %copy-done.22, ...), custom_call_target="tpu_custom_call" | custom-call | flops 7455375360 | bytes 11796480 | tf_op jit(solution)/shard_map/edge_branch/pallas_call | solution.py:573
  109.1 2.0 collective-permute-done.20
  112.5 1.6 collective-permute-start.23
  116.0 6.5 %edge_weights.2 = (f32[192,192]{1,0:T(8,128)}, f32[192,192]{1,0:T(8,128)}, f32[1,192]{1,0:T(1,128)}, f32[1,192]{1,0:T(1,128)}) custom-call(bf16[3840,192]{1,0:T(8,128)(2,1)} %get-tuple-element.167.refs_0_, bf16[3840,192]{1,0:T(8,128)(2,1)} %get-tuple-element.168.refs_1_, bf16[3840,192]{1,0:T(8,128)(2,1)} %get-tuple-element.169.refs_2_.low_three, ...), custom_call_target="tpu_custom_call" | custom-call | flops 566231040 | bytes 5898240 | tf_op jit(solution)/shard_map/edge_weights/pallas_call | solution.py:662
  123.3 1.6 collective-permute-start.26
  125.9 1.9 collective-permute-start.24
  127.8 1.6 collective-permute-done.26.refs_3_
  131.3 6.8 %residue_backward.1 = (f32[64,512]{1,0:T(8,128)}, f32[64,512]{1,0:T(8,128)}, bf16[64,1024]{1,0:T(8,128)(2,1)}, bf16[278,16,128]{2,1,0:T(8,128)(2,1)}) custom-call(bf16[64,512]{1,0:T(8,128)(2,1)} %node_cot.1, f32[64,192]{1,0:T(8,128)} %get-tuple-element.158.own_sum, bf16[192,1216]{1,0:T(8,128)(2,1)} %bitcast.46, bf16[192,512]{1,0:T(8,128)(2,1)} %slice.110.e_far, ...), custom_call_target="tpu_custom_call" | custom-call | flops 268435456 | bytes 8388608 | tf_op jit(solution)/shard_map/residue_backward/pallas_call | solution.py:180
  138.1 2.3 collective-permute-start.29
  140.7 1.9 collective-permute-start.27
  142.6 5.3 %edge_weights.3 = (f32[192,192]{1,0:T(8,128)}, f32[1,192]{1,0:T(1,128)}) custom-call(bf16[3840,192]{1,0:T(8,128)(2,1)} %get-tuple-element.188.refs_0_.low_edge, bf16[60,64,192]{2,1,0:T(8,128)(2,1)} %bitcast.50), custom_call_target="tpu_custom_call" | custom-call | flops 283115520 | bytes 2949120 | tf_op jit(solution)/shard_map/edge_weights/pallas_call | solution.py:662
  147.9 2.8 %collective-permute-done.27 = bf16[64,1024]{1,0:T(8,128)(2,1)S(1)} collective-permute-done((bf16[64,1024]{1,0:T(8,128)(2,1)}, bf16[64,1024]{1,0:T(8,128)(2,1)S(1)}, u32[]{:S(2)}, u32[]{:S(2)}) %collective-permute-start.27) | collective-permute-done | bytes 131104 | tf_op jit(solution)/shard_map/ppermute | solution.py:1069
  150.7 1.6 collective-permute-start.32
  154.3 27.7 %message_backward.1 = (f32[60,64,192]{2,1,0:T(8,128)}, bf16[2,8,16,16,128]{4,3,2,1,0:T(8,128)(2,1)}, bf16[2,8,16,16,128]{4,3,2,1,0:T(8,128)(2,1)}, f32[64,512]{1...) custom-call(s32[1]{0:T(128)} %bitcast.16.base, s32[1,3840]{1,0:T(1,128)} %bitcast.55, ...), custom_call_target="tpu_custom_call" | custom-call | flops 6794772480 | bytes 19169280 | tf_op jit(solution)/shard_map/message_backward/pallas_call | solution.py:929
  182.2 1.7 copy-done.25
  184.0 3.4 %collective-permute-done.33 = bf16[384,16,128]{2,1,0:T(8,128)(2,1)S(1)} collective-permute-done((bf16[384,16,128]{2,1,0:T(8,128)(2,1)S(1)}, bf16[384,16,128]{2,1,0:T(8,128)(2,1)S(1)}, u32[]{:S(2)}, u32[]{:S(2)}) %collective-permute-start.33) | collective-permute-done | bytes 1572896 | tf_op jit(solution)/shard_map/ppermute | solution.py:1069
  189.6 1.5 collective-permute-start.36
  196.3 9.2 %feed_gradients.1 = (f32[512,512]{1,0:T(8,128)}, f32[512,512]{1,0:T(8,128)}, f32[1,512]{1,0:T(1,128)}) custom-call(bf16[1024,1024]{1,0:T(8,128)(2,1)} %copy-done.10, bf16[1024,1024]{1,0:T(8,128)(2,1)} %copy-done.24, bf16[512,512]{1,0:T(8,128)(2,1)} %f1.1, f32[1,512]{1,0:T(1,128)} %bitcast.62, bf16[512,512]{1,0:T(8,128)(2,1)} %f2.1), custom_call_target="tpu_custom_call" | custom-call | flops 4294967296 | bytes 4194304 | tf_op jit(solution)/shard_map/feed_gradients/pallas_call | solution.py:777
  205.5 4.8 %collective-permute-done.35 = bf16[96,16,128]{2,1,0:T(8,128)(2,1)S(1)} collective-permute-done((bf16[96,16,128]{2,1,0:T(8,128)(2,1)}, bf16[96,16,128]{2,1,0:T(8,128)(2,1)S(1)}, u32[]{:S(2)}, u32[]{:S(2)}) %collective-permute-start.35) | collective-permute-done | bytes 393248 | tf_op jit(solution)/shard_map/ppermute | solution.py:1069
  211.9 2.3 collective-permute-start.41
  217.4 4.0 %collective-permute-done.39 = bf16[24,16,128]{2,1,0:T(8,128)(2,1)S(1)} collective-permute-done((bf16[24,16,128]{2,1,0:T(8,128)(2,1)S(1)}, bf16[24,16,128]{2,1,0:T(8,128)(2,1)S(1)}, u32[]{:S(2)}, u32[]{:S(2)}) %collective-permute-start.39) | collective-permute-done | bytes 98336 | tf_op jit(solution)/shard_map/ppermute | solution.py:1069
  221.4 1.5 collective-permute-start.47
  223.1 2.7 %collective-permute-start.46 = (bf16[24,16,128]{2,1,0:T(8,128)(2,1)S(1)}, bf16[24,16,128]{2,1,0:T(8,128)(2,1)S(1)}, u32[]{:S(2)}, u32[]{:S(2)}) collective-permute-start(bf16[24,16,128]{2,1,0:T(8,128)(2,1)S(1)} %fusion.2), channel_id=1, source_target_pairs={{0,24},{1,25},{2,26},{3,27},{4,28},{5,29},{6,30},{7,31},{8,16},{9,... | collective-permute-start | bytes 294920 | tf_op jit(solution)/shard_map/ppermute | solution.py:1069
  227.8 2.8 %collective-permute-done.46 = bf16[24,16,128]{2,1,0:T(8,128)(2,1)S(1)} collective-permute-done((bf16[24,16,128]{2,1,0:T(8,128)(2,1)S(1)}, bf16[24,16,128]{2,1,0:T(8,128)(2,1)S(1)}, u32[]{:S(2)}, u32[]{:S(2)}) %collective-permute-start.46) | collective-permute-done | bytes 98336 | tf_op jit(solution)/shard_map/ppermute | solution.py:1069
  231.6 3.0 %collective-permute-done.44 = bf16[24,16,128]{2,1,0:T(8,128)(2,1)S(1)} collective-permute-done((bf16[24,16,128]{2,1,0:T(8,128)(2,1)S(1)}, bf16[24,16,128]{2,1,0:T(8,128)(2,1)S(1)}, u32[]{:S(2)}, u32[]{:S(2)}) %collective-permute-start.44) | collective-permute-done | bytes 98336 | tf_op jit(solution)/shard_map/ppermute | solution.py:1069
  234.7 1.6 collective-permute-start.50
  239.2 1.8 collective-permute-start.53
  241.0 4.4 %collective-permute-done.53.refs_3_ = bf16[16,16,128]{2,1,0:T(8,128)(2,1)S(1)} collective-permute-done((bf16[16,16,128]{2,1,0:T(8,128)(2,1)S(1)}, bf16[16,16,128]{2,1,0:T(8,128)(2,1)S(1)}, u32[]{:S(2)}, u32[]{:S(2)}) %collective-permute-start.53) | collective-permute-done | bytes 65568 | tf_op jit(solution)/shard_map/ppermute | solution.py:1069
  246.3 4.3 %collective-permute-done.51.refs_1_ = bf16[16,16,128]{2,1,0:T(8,128)(2,1)S(1)} collective-permute-done((bf16[16,16,128]{2,1,0:T(8,128)(2,1)S(1)}, bf16[16,16,128]{2,1,0:T(8,128)(2,1)S(1)}, u32[]{:S(2)}, u32[]{:S(2)}) %collective-permute-start.51) | collective-permute-done | bytes 65568 | tf_op jit(solution)/shard_map/ppermute | solution.py:1069
  251.2 3.0 %node_gradient.1 = f32[64,512]{1,0:T(8,128)} custom-call(f32[64,512]{1,0:T(8,128)} %get-tuple-element.226.g_u1, f32[64,512]{1,0:T(8,128)} %get-tuple-element.227.own, bf16[1216,512]{1,0:T(8,128)(2,1)} %m1.5, f32[64,16,128]{2,1,0:T(8,128)} %get-tuple-element.258.refs_0_, bf16[16,16,128]{2,1,0:T(8,128)(2,1)} %copy-done.18, bf16[16,16,128]{2,1,0:T(8,128)(2,1)} %copy-done.17, ...), custom_call_target="tpu_custom_call" | custom-call | flops 134217728 | bytes 2097152 | tf_op jit(solution)/shard_map/node_gradient/pallas_call | solution.py:180
  254.5 3.4 %collective-permute-done.54.second = bf16[384,16,128]{2,1,0:T(8,128)(2,1)S(1)} collective-permute-done((bf16[384,16,128]{2,1,0:T(8,128)(2,1)S(1)}, bf16[384,16,128]{2,1,0:T(8,128)(2,1)S(1)}, u32[]{:S(2)}, u32[]{:S(2)}) %collective-permute-start.54) | collective-permute-done | bytes 1572896 | tf_op jit(solution)/shard_map/ppermute | solution.py:1069
  259.1 4.7 %weight_gradients.1 = (f32[1216,512]{1,0:T(8,128)}, f32[1,512]{1,0:T(1,128)}, f32[512,512]{1,0:T(8,128)}, f32[1,512]{1,0:T(1,128)}, f32[512,512]{1,0:T(8,128)}, ...) custom-call(s32[1]{0:T(128)} %bitcast.16.base, ...), custom_call_target="tpu_custom_call" | custom-call | bytes 10485760 | tf_op jit(solution)/shard_map/weight_gradients/pallas_call | solution.py:180
  (178 shorter events, 52.1 us)
Async XLA Ops:
  0.7 9.0 %collective-permute-start.2 = (bf16[64,512]{1,0:T(8,128)(2,1)}, bf16[64,512]{1,0:T(8,128)(2,1)S(1)}, u32[]{:S(2)}, u32[]{:S(2)}) collective-permute-start(bf16[64,512]{1,0:T(8,128)(2,1)} %node.3), channel_id=1, source_target_pairs={{0,24},{1,25},{2,26},{3,27},{4,28},{5,29},{6,30},{7,31},{8,16},{9,... | collective-permute-start | bytes 196616 | tf_op jit(solution)/shard_map/ppermute | solution.py:1069
  5.8 4.9 %collective-permute-start.1 = (bf16[64,512]{1,0:T(8,128)(2,1)}, bf16[64,512]{1,0:T(8,128)(2,1)S(1)}, u32[]{:S(2)}, u32[]{:S(2)}) collective-permute-start(bf16[64,512]{1,0:T(8,128)(2,1)} %node.3), channel_id=1, source_target_pairs={{0,8},{1,9},{2,10},{3,11},{4,12},{5,13},{6,14},{7,15},{8,0},{9,1},... | collective-permute-start | bytes 196616 | tf_op jit(solution)/shard_map/ppermute | solution.py:1069
  5.8 5.8 %collective-permute-start = (bf16[64,512]{1,0:T(8,128)(2,1)}, bf16[64,512]{1,0:T(8,128)(2,1)S(1)}, u32[]{:S(2)}, u32[]{:S(2)}) collective-permute-start(bf16[64,512]{1,0:T(8,128)(2,1)} %node.3), channel_id=1, source_target_pairs={{0,16},{1,17},{2,18},{3,19},{4,20},{5,21},{6,22},{7,23},{8,24},{9,... | collective-permute-start | bytes 196616 | tf_op jit(solution)/shard_map/ppermute | solution.py:1069
  12.5 12.5 %collective-permute-start.5 = (bf16[256,512]{1,0:T(8,128)(2,1)S(1)}, bf16[256,512]{1,0:T(8,128)(2,1)S(1)}, u32[]{:S(2)}, u32[]{:S(2)}) collective-permute-start(bf16[256,512]{1,0:T(8,128)(2,1)S(1)} %pad_maximum_fusion.4), channel_id=1, source_target_pairs={{0,6},{1,7},{2,4},{3,5},{4,2},{5,3},{6,0},{7,1},{8,14},{9,15},{10,... | collective-permute-start | bytes 786440 | tf_op jit(solution)/shard_map/ppermute | solution.py:1069
  15.0 10.8 %collective-permute-start.4 = (bf16[256,512]{1,0:T(8,128)(2,1)S(1)}, bf16[256,512]{1,0:T(8,128)(2,1)S(1)}, u32[]{:S(2)}, u32[]{:S(2)}) collective-permute-start(bf16[256,512]{1,0:T(8,128)(2,1)S(1)} %pad_maximum_fusion.4), channel_id=1, source_target_pairs={{0,2},{1,3},{2,0},{3,1},{4,6},{5,7},{6,4},{7,5},{8,10},{9,11},{10,... | collective-permute-start | bytes 786440 | tf_op jit(solution)/shard_map/ppermute | solution.py:1069
  15.5 10.6 %collective-permute-start.3 = (bf16[256,512]{1,0:T(8,128)(2,1)S(1)}, bf16[256,512]{1,0:T(8,128)(2,1)S(1)}, u32[]{:S(2)}, u32[]{:S(2)}) collective-permute-start(bf16[256,512]{1,0:T(8,128)(2,1)S(1)} %pad_maximum_fusion.4), channel_id=1, source_target_pairs={{0,4},{1,5},{2,6},{3,7},{4,0},{5,1},{6,2},{7,3},{8,12},{9,13},{10,... | collective-permute-start | bytes 786440 | tf_op jit(solution)/shard_map/ppermute | solution.py:1069
  28.8 21.9 %collective-permute-start.8 = (bf16[512,512]{1,0:T(8,128)(2,1)S(1)}, bf16[512,512]{1,0:T(8,128)(2,1)S(1)}, u32[]{:S(2)}, u32[]{:S(2)}) collective-permute-start(bf16[512,512]{1,0:T(8,128)(2,1)S(1)} %copy-done.6), channel_id=1, source_target_pairs={{0,2},{1,3},{2,0},{3,1},{4,6},{5,7},{6,4},{7,5},{8,10},{9,11},{10,... | collective-permute-start | bytes 1572872 | tf_op jit(solution)/shard_map/ppermute | solution.py:1069
  30.2 24.5 %collective-permute-start.7 = (bf16[528,512]{1,0:T(8,128)(2,1)S(1)}, bf16[528,512]{1,0:T(8,128)(2,1)S(1)}, u32[]{:S(2)}, u32[]{:S(2)}) collective-permute-start(bf16[528,512]{1,0:T(8,128)(2,1)S(1)} %concatenate.30.refs_0_.refs_4_), channel_id=1, source_target_pairs={{0,2},{1,3},{2,0},{3,1},{4,6},{5,7},{6,4},{7,5},{8,10},{9,11},{10,... | collective-permute-start | bytes 1622024 | tf_op jit(solution)/shard_map/ppermute | solution.py:1069
  54.7 4.2 %collective-permute-start.9 = (bf16[528,512]{1,0:T(8,128)(2,1)S(1)}, bf16[528,512]{1,0:T(8,128)(2,1)S(1)}, u32[]{:S(2)}, u32[]{:S(2)}) collective-permute-start(bf16[528,512]{1,0:T(8,128)(2,1)S(1)} %concatenate.30.refs_0_.refs_4_), channel_id=1, source_target_pairs={{0,1},{1,0},{2,3},{3,2},{4,5},{5,4},{6,7},{7,6},{8,9},{9,8},{10,11... | collective-permute-start | bytes 1622024 | tf_op jit(solution)/shard_map/ppermute | solution.py:1069
  54.7 4.2 %collective-permute-start.10 = (bf16[528,512]{1,0:T(8,128)(2,1)S(1)}, bf16[528,512]{1,0:T(8,128)(2,1)S(1)}, u32[]{:S(2)}, u32[]{:S(2)}) collective-permute-start(bf16[528,512]{1,0:T(8,128)(2,1)S(1)} %collective-permute-done.7.refs_1_.refs_5_), channel_id=1, source_target_pairs={{0,1},{1,0},{2,3},{3,2},{4,5},{5,4},{6,7},{7,6},{8,9},{9,8},{10,11... | collective-permute-start | bytes 1622024 | tf_op jit(solution)/shard_map/ppermute | solution.py:1069
  65.5 8.0 %collective-permute-start.15 = (bf16[64,192]{1,0:T(8,128)(2,1)}, bf16[64,192]{1,0:T(8,128)(2,1)S(1)}, u32[]{:S(2)}, u32[]{:S(2)}) collective-permute-start(bf16[64,192]{1,0:T(8,128)(2,1)} %get-tuple-element.154), channel_id=1, source_target_pairs={{0,24},{1,25},{2,26},{3,27},{4,28},{5,29},{6,30},{7,31},{8,16},{9,... | collective-permute-start | bytes 73736 | tf_op jit(solution)/shard_map/ppermute | solution.py:1069
  68.0 5.4 %collective-permute-start.14 = (bf16[64,192]{1,0:T(8,128)(2,1)}, bf16[64,192]{1,0:T(8,128)(2,1)S(1)}, u32[]{:S(2)}, u32[]{:S(2)}) collective-permute-start(bf16[64,192]{1,0:T(8,128)(2,1)} %get-tuple-element.154), channel_id=1, source_target_pairs={{0,8},{1,9},{2,10},{3,11},{4,12},{5,13},{6,14},{7,15},{8,0},{9,1},... | collective-permute-start | bytes 73736 | tf_op jit(solution)/shard_map/ppermute | solution.py:1069
  68.0 5.4 %collective-permute-start.13 = (bf16[64,192]{1,0:T(8,128)(2,1)}, bf16[64,192]{1,0:T(8,128)(2,1)S(1)}, u32[]{:S(2)}, u32[]{:S(2)}) collective-permute-start(bf16[64,192]{1,0:T(8,128)(2,1)} %get-tuple-element.154), channel_id=1, source_target_pairs={{0,16},{1,17},{2,18},{3,19},{4,20},{5,21},{6,22},{7,23},{8,24},{9,... | collective-permute-start | bytes 73736 | tf_op jit(solution)/shard_map/ppermute | solution.py:1069
  73.4 5.2 %collective-permute-start.16 = (bf16[256,192]{1,0:T(8,128)(2,1)S(1)}, bf16[256,192]{1,0:T(8,128)(2,1)S(1)}, u32[]{:S(2)}, u32[]{:S(2)}) collective-permute-start(bf16[256,192]{1,0:T(8,128)(2,1)S(1)} %get-tuple-element.286), channel_id=1, source_target_pairs={{0,4},{1,5},{2,6},{3,7},{4,0},{5,1},{6,2},{7,3},{8,12},{9,13},{10,... | collective-permute-start | bytes 294920 | tf_op jit(solution)/shard_map/ppermute | solution.py:1069
  75.0 7.4 %collective-permute-start.18 = (bf16[256,192]{1,0:T(8,128)(2,1)S(1)}, bf16[256,192]{1,0:T(8,128)(2,1)S(1)}, u32[]{:S(2)}, u32[]{:S(2)}) collective-permute-start(bf16[256,192]{1,0:T(8,128)(2,1)S(1)} %get-tuple-element.286), channel_id=1, source_target_pairs={{0,6},{1,7},{2,4},{3,5},{4,2},{5,3},{6,0},{7,1},{8,14},{9,15},{10,... | collective-permute-start | bytes 294920 | tf_op jit(solution)/shard_map/ppermute | solution.py:1069
  76.4 6.0 %collective-permute-start.17 = (bf16[256,192]{1,0:T(8,128)(2,1)S(1)}, bf16[256,192]{1,0:T(8,128)(2,1)S(1)}, u32[]{:S(2)}, u32[]{:S(2)}) collective-permute-start(bf16[256,192]{1,0:T(8,128)(2,1)S(1)} %get-tuple-element.286), channel_id=1, source_target_pairs={{0,2},{1,3},{2,0},{3,1},{4,6},{5,7},{6,4},{7,5},{8,10},{9,11},{10,... | collective-permute-start | bytes 294920 | tf_op jit(solution)/shard_map/ppermute | solution.py:1069
  112.5 10.0 %collective-permute-start.23 = (bf16[256,192]{1,0:T(8,128)(2,1)S(1)}, bf16[256,192]{1,0:T(8,128)(2,1)S(1)}, u32[]{:S(2)}, u32[]{:S(2)}) collective-permute-start(bf16[256,192]{1,0:T(8,128)(2,1)S(1)} %get-tuple-element.274), channel_id=1, source_target_pairs={{0,6},{1,7},{2,4},{3,5},{4,2},{5,3},{6,0},{7,1},{8,14},{9,15},{10,... | collective-permute-start | bytes 294920 | tf_op jit(solution)/shard_map/ppermute | solution.py:1069
  114.1 8.4 %collective-permute-start.22 = (bf16[256,192]{1,0:T(8,128)(2,1)S(1)}, bf16[256,192]{1,0:T(8,128)(2,1)S(1)}, u32[]{:S(2)}, u32[]{:S(2)}) collective-permute-start(bf16[256,192]{1,0:T(8,128)(2,1)S(1)} %get-tuple-element.275), channel_id=1, source_target_pairs={{0,2},{1,3},{2,0},{3,1},{4,6},{5,7},{6,4},{7,5},{8,10},{9,11},{10,... | collective-permute-start | bytes 294920 | tf_op jit(solution)/shard_map/ppermute | solution.py:1069
  114.8 7.7 %collective-permute-start.21 = (bf16[256,192]{1,0:T(8,128)(2,1)S(1)}, bf16[256,192]{1,0:T(8,128)(2,1)S(1)}, u32[]{:S(2)}, u32[]{:S(2)}) collective-permute-start(bf16[256,192]{1,0:T(8,128)(2,1)S(1)} %get-tuple-element.276), channel_id=1, source_target_pairs={{0,4},{1,5},{2,6},{3,7},{4,0},{5,1},{6,2},{7,3},{8,12},{9,13},{10,... | collective-permute-start | bytes 294920 | tf_op jit(solution)/shard_map/ppermute | solution.py:1069
  123.3 6.1 %collective-permute-start.26 = (bf16[64,192]{1,0:T(8,128)(2,1)S(1)}, bf16[64,192]{1,0:T(8,128)(2,1)S(1)}, u32[]{:S(2)}, u32[]{:S(2)}) collective-permute-start(bf16[64,192]{1,0:T(8,128)(2,1)S(1)} %get-tuple-element.283), channel_id=1, source_target_pairs={{0,24},{1,25},{2,26},{3,27},{4,28},{5,29},{6,30},{7,31},{8,16},{9,... | collective-permute-start | bytes 73736 | tf_op jit(solution)/shard_map/ppermute | solution.py:1069
  124.9 4.5 %collective-permute-start.25 = (bf16[64,192]{1,0:T(8,128)(2,1)S(1)}, bf16[64,192]{1,0:T(8,128)(2,1)S(1)}, u32[]{:S(2)}, u32[]{:S(2)}) collective-permute-start(bf16[64,192]{1,0:T(8,128)(2,1)S(1)} %get-tuple-element.284), channel_id=1, source_target_pairs={{0,8},{1,9},{2,10},{3,11},{4,12},{5,13},{6,14},{7,15},{8,0},{9,1},... | collective-permute-start | bytes 73736 | tf_op jit(solution)/shard_map/ppermute | solution.py:1069
  125.9 4.8 %collective-permute-start.24 = (bf16[64,192]{1,0:T(8,128)(2,1)S(1)}, bf16[64,192]{1,0:T(8,128)(2,1)S(1)}, u32[]{:S(2)}, u32[]{:S(2)}) collective-permute-start(bf16[64,192]{1,0:T(8,128)(2,1)S(1)} %get-tuple-element.285), channel_id=1, source_target_pairs={{0,16},{1,17},{2,18},{3,19},{4,20},{5,21},{6,22},{7,23},{8,24},{9,... | collective-permute-start | bytes 73736 | tf_op jit(solution)/shard_map/ppermute | solution.py:1069
  138.1 9.7 %collective-permute-start.29 = (bf16[64,1024]{1,0:T(8,128)(2,1)}, bf16[64,1024]{1,0:T(8,128)(2,1)S(1)}, u32[]{:S(2)}, u32[]{:S(2)}) collective-permute-start(bf16[64,1024]{1,0:T(8,128)(2,1)} %get-tuple-element.187), channel_id=1, source_target_pairs={{0,24},{1,25},{2,26},{3,27},{4,28},{5,29},{6,30},{7,31},{8,16},{9,... | collective-permute-start | bytes 393224 | tf_op jit(solution)/shard_map/ppermute | solution.py:1069
  140.5 7.4 %collective-permute-start.28 = (bf16[64,1024]{1,0:T(8,128)(2,1)}, bf16[64,1024]{1,0:T(8,128)(2,1)S(1)}, u32[]{:S(2)}, u32[]{:S(2)}) collective-permute-start(bf16[64,1024]{1,0:T(8,128)(2,1)} %get-tuple-element.187), channel_id=1, source_target_pairs={{0,8},{1,9},{2,10},{3,11},{4,12},{5,13},{6,14},{7,15},{8,0},{9,1},... | collective-permute-start | bytes 393224 | tf_op jit(solution)/shard_map/ppermute | solution.py:1069
  140.7 10.0 %collective-permute-start.27 = (bf16[64,1024]{1,0:T(8,128)(2,1)}, bf16[64,1024]{1,0:T(8,128)(2,1)S(1)}, u32[]{:S(2)}, u32[]{:S(2)}) collective-permute-start(bf16[64,1024]{1,0:T(8,128)(2,1)} %get-tuple-element.187), channel_id=1, source_target_pairs={{0,16},{1,17},{2,18},{3,19},{4,20},{5,21},{6,22},{7,23},{8,24},{9,... | collective-permute-start | bytes 393224 | tf_op jit(solution)/shard_map/ppermute | solution.py:1069
  150.7 31.3 %collective-permute-start.32 = (bf16[256,1024]{1,0:T(8,128)(2,1)S(1)}, bf16[256,1024]{1,0:T(8,128)(2,1)S(1)}, u32[]{:S(2)}, u32[]{:S(2)}) collective-permute-start(bf16[256,1024]{1,0:T(8,128)(2,1)S(1)} %pad_maximum_fusion.2), channel_id=1, source_target_pairs={{0,6},{1,7},{2,4},{3,5},{4,2},{5,3},{6,0},{7,1},{8,14},{9,15},{10,... | collective-permute-start | bytes 1572872 | tf_op jit(solution)/shard_map/ppermute | solution.py:1069
  152.3 29.8 %collective-permute-start.31 = (bf16[256,1024]{1,0:T(8,128)(2,1)S(1)}, bf16[256,1024]{1,0:T(8,128)(2,1)S(1)}, u32[]{:S(2)}, u32[]{:S(2)}) collective-permute-start(bf16[256,1024]{1,0:T(8,128)(2,1)S(1)} %pad_maximum_fusion.2), channel_id=1, source_target_pairs={{0,2},{1,3},{2,0},{3,1},{4,6},{5,7},{6,4},{7,5},{8,10},{9,11},{10,... | collective-permute-start | bytes 1572872 | tf_op jit(solution)/shard_map/ppermute | solution.py:1069
  153.0 29.1 %collective-permute-start.30 = (bf16[256,1024]{1,0:T(8,128)(2,1)S(1)}, bf16[256,1024]{1,0:T(8,128)(2,1)S(1)}, u32[]{:S(2)}, u32[]{:S(2)}) collective-permute-start(bf16[256,1024]{1,0:T(8,128)(2,1)S(1)} %pad_maximum_fusion.2), channel_id=1, source_target_pairs={{0,4},{1,5},{2,6},{3,7},{4,0},{5,1},{6,2},{7,3},{8,12},{9,13},{10,... | collective-permute-start | bytes 1572872 | tf_op jit(solution)/shard_map/ppermute | solution.py:1069
  187.8 7.2 %collective-permute-start.38 = (bf16[1024,1024]{1,0:T(8,128)(2,1)S(1)}, bf16[1024,1024]{1,0:T(8,128)(2,1)S(1)}, u32[]{:S(2)}, u32[]{:S(2)}) collective-permute-start(bf16[1024,1024]{1,0:T(8,128)(2,1)S(1)} %pad_maximum_fusion.first), channel_id=1, source_target_pairs={{0,1},{1,0},{2,3},{3,2},{4,5},{5,4},{6,7},{7,6},{8,9},{9,8},{10,11... | collective-permute-start | bytes 6291464 | tf_op jit(solution)/shard_map/ppermute | solution.py:1069
  188.0 5.5 %collective-permute-start.37 = (bf16[256,16,128]{2,1,0:T(8,128)(2,1)S(1)}, bf16[256,16,128]{2,1,0:T(8,128)(2,1)S(1)}, u32[]{:S(2)}, u32[]{:S(2)}) collective-permute-start(bf16[256,16,128]{2,1,0:T(8,128)(2,1)S(1)} %bitcast.66), channel_id=1, source_target_pairs={{0,1},{1,0},{2,3},{3,2},{4,5},{5,4},{6,7},{7,6},{8,9},{9,8},{10,11... | collective-permute-start | bytes 3145736 | tf_op jit(solution)/shard_map/ppermute | solution.py:1069
  189.6 15.9 %collective-permute-start.36 = (bf16[96,16,128]{2,1,0:T(8,128)(2,1)}, bf16[96,16,128]{2,1,0:T(8,128)(2,1)S(1)}, u32[]{:S(2)}, u32[]{:S(2)}) collective-permute-start(bf16[96,16,128]{2,1,0:T(8,128)(2,1)} %get-tuple-element.268), channel_id=1, source_target_pairs={{0,6},{1,7},{2,4},{3,5},{4,2},{5,3},{6,0},{7,1},{8,14},{9,15},{10,... | collective-permute-start | bytes 1179656 | tf_op jit(solution)/shard_map/ppermute | solution.py:1069
  191.1 19.2 %collective-permute-start.35 = (bf16[96,16,128]{2,1,0:T(8,128)(2,1)}, bf16[96,16,128]{2,1,0:T(8,128)(2,1)S(1)}, u32[]{:S(2)}, u32[]{:S(2)}) collective-permute-start(bf16[96,16,128]{2,1,0:T(8,128)(2,1)} %get-tuple-element.269), channel_id=1, source_target_pairs={{0,2},{1,3},{2,0},{3,1},{4,6},{5,7},{6,4},{7,5},{8,10},{9,11},{10,... | collective-permute-start | bytes 1179656 | tf_op jit(solution)/shard_map/ppermute | solution.py:1069
  191.8 18.5 %collective-permute-start.34 = (bf16[96,16,128]{2,1,0:T(8,128)(2,1)}, bf16[96,16,128]{2,1,0:T(8,128)(2,1)}, u32[]{:S(2)}, u32[]{:S(2)}) collective-permute-start(bf16[96,16,128]{2,1,0:T(8,128)(2,1)} %get-tuple-element.270), channel_id=1, source_target_pairs={{0,4},{1,5},{2,6},{3,7},{4,0},{5,1},{6,2},{7,3},{8,12},{9,13},{10,... | collective-permute-start | bytes 1179656 | tf_op jit(solution)/shard_map/ppermute | solution.py:1069
  211.5 9.9 %collective-permute-start.39 = (bf16[24,16,128]{2,1,0:T(8,128)(2,1)S(1)}, bf16[24,16,128]{2,1,0:T(8,128)(2,1)S(1)}, u32[]{:S(2)}, u32[]{:S(2)}) collective-permute-start(bf16[24,16,128]{2,1,0:T(8,128)(2,1)S(1)} %get-tuple-element.277), channel_id=1, source_target_pairs={{0,16},{1,17},{2,18},{3,19},{4,20},{5,21},{6,22},{7,23},{8,24},{9,... | collective-permute-start | bytes 294920 | tf_op jit(solution)/shard_map/ppermute | solution.py:1069
  211.9 11.1 %collective-permute-start.41 = (bf16[24,16,128]{2,1,0:T(8,128)(2,1)S(1)}, bf16[24,16,128]{2,1,0:T(8,128)(2,1)S(1)}, u32[]{:S(2)}, u32[]{:S(2)}) collective-permute-start(bf16[24,16,128]{2,1,0:T(8,128)(2,1)S(1)} %get-tuple-element.278), channel_id=1, source_target_pairs={{0,24},{1,25},{2,26},{3,27},{4,28},{5,29},{6,30},{7,31},{8,16},{9,... | collective-permute-start | bytes 294920 | tf_op jit(solution)/shard_map/ppermute | solution.py:1069
  214.2 8.8 %collective-permute-start.40 = (bf16[24,16,128]{2,1,0:T(8,128)(2,1)S(1)}, bf16[24,16,128]{2,1,0:T(8,128)(2,1)S(1)}, u32[]{:S(2)}, u32[]{:S(2)}) collective-permute-start(bf16[24,16,128]{2,1,0:T(8,128)(2,1)S(1)} %get-tuple-element.279), channel_id=1, source_target_pairs={{0,8},{1,9},{2,10},{3,11},{4,12},{5,13},{6,14},{7,15},{8,0},{9,1},... | collective-permute-start | bytes 294920 | tf_op jit(solution)/shard_map/ppermute | solution.py:1069
  215.2 7.8 %collective-permute-start.43 = (bf16[64,16,128]{2,1,0:T(8,128)(2,1)S(1)}, bf16[64,16,128]{2,1,0:T(8,128)(2,1)S(1)}, u32[]{:S(2)}, u32[]{:S(2)}) collective-permute-start(bf16[64,16,128]{2,1,0:T(8,128)(2,1)S(1)} %get-tuple-element.272), channel_id=1, source_target_pairs={{0,2},{1,3},{2,0},{3,1},{4,6},{5,7},{6,4},{7,5},{8,10},{9,11},{10,... | collective-permute-start | bytes 786440 | tf_op jit(solution)/shard_map/ppermute | solution.py:1069
  216.0 7.1 %collective-permute-start.42 = (bf16[64,16,128]{2,1,0:T(8,128)(2,1)S(1)}, bf16[64,16,128]{2,1,0:T(8,128)(2,1)S(1)}, u32[]{:S(2)}, u32[]{:S(2)}) collective-permute-start(bf16[64,16,128]{2,1,0:T(8,128)(2,1)S(1)} %get-tuple-element.273), channel_id=1, source_target_pairs={{0,4},{1,5},{2,6},{3,7},{4,0},{5,1},{6,2},{7,3},{8,12},{9,13},{10,... | collective-permute-start | bytes 786440 | tf_op jit(solution)/shard_map/ppermute | solution.py:1069
  221.4 13.3 %collective-permute-start.47 = (bf16[64,16,128]{2,1,0:T(8,128)(2,1)S(1)}, bf16[64,16,128]{2,1,0:T(8,128)(2,1)S(1)}, u32[]{:S(2)}, u32[]{:S(2)}) collective-permute-start(bf16[64,16,128]{2,1,0:T(8,128)(2,1)S(1)} %get-tuple-element.271), channel_id=1, source_target_pairs={{0,6},{1,7},{2,4},{3,5},{4,2},{5,3},{6,0},{7,1},{8,14},{9,15},{10,... | collective-permute-start | bytes 786440 | tf_op jit(solution)/shard_map/ppermute | solution.py:1069
  223.1 7.5 %collective-permute-start.46 = (bf16[24,16,128]{2,1,0:T(8,128)(2,1)S(1)}, bf16[24,16,128]{2,1,0:T(8,128)(2,1)S(1)}, u32[]{:S(2)}, u32[]{:S(2)}) collective-permute-start(bf16[24,16,128]{2,1,0:T(8,128)(2,1)S(1)} %fusion.2), channel_id=1, source_target_pairs={{0,24},{1,25},{2,26},{3,27},{4,28},{5,29},{6,30},{7,31},{8,16},{9,... | collective-permute-start | bytes 294920 | tf_op jit(solution)/shard_map/ppermute | solution.py:1069
  225.8 5.8 %collective-permute-start.45 = (bf16[24,16,128]{2,1,0:T(8,128)(2,1)S(1)}, bf16[24,16,128]{2,1,0:T(8,128)(2,1)S(1)}, u32[]{:S(2)}, u32[]{:S(2)}) collective-permute-start(bf16[24,16,128]{2,1,0:T(8,128)(2,1)S(1)} %fusion.2), channel_id=1, source_target_pairs={{0,8},{1,9},{2,10},{3,11},{4,12},{5,13},{6,14},{7,15},{8,0},{9,1},... | collective-permute-start | bytes 294920 | tf_op jit(solution)/shard_map/ppermute | solution.py:1069
  226.4 8.3 %collective-permute-start.44 = (bf16[24,16,128]{2,1,0:T(8,128)(2,1)S(1)}, bf16[24,16,128]{2,1,0:T(8,128)(2,1)S(1)}, u32[]{:S(2)}, u32[]{:S(2)}) collective-permute-start(bf16[24,16,128]{2,1,0:T(8,128)(2,1)S(1)} %fusion.2), channel_id=1, source_target_pairs={{0,16},{1,17},{2,18},{3,19},{4,20},{5,21},{6,22},{7,23},{8,24},{9,... | collective-permute-start | bytes 294920 | tf_op jit(solution)/shard_map/ppermute | solution.py:1069
  234.7 19.5 %collective-permute-start.50 = (bf16[96,16,128]{2,1,0:T(8,128)(2,1)S(1)}, bf16[96,16,128]{2,1,0:T(8,128)(2,1)S(1)}, u32[]{:S(2)}, u32[]{:S(2)}) collective-permute-start(bf16[96,16,128]{2,1,0:T(8,128)(2,1)S(1)} %pad_maximum_fusion.3), channel_id=1, source_target_pairs={{0,6},{1,7},{2,4},{3,5},{4,2},{5,3},{6,0},{7,1},{8,14},{9,15},{10,... | collective-permute-start | bytes 1179656 | tf_op jit(solution)/shard_map/ppermute | solution.py:1069
  236.3 17.9 %collective-permute-start.49 = (bf16[96,16,128]{2,1,0:T(8,128)(2,1)S(1)}, bf16[96,16,128]{2,1,0:T(8,128)(2,1)S(1)}, u32[]{:S(2)}, u32[]{:S(2)}) collective-permute-start(bf16[96,16,128]{2,1,0:T(8,128)(2,1)S(1)} %pad_maximum_fusion.3), channel_id=1, source_target_pairs={{0,2},{1,3},{2,0},{3,1},{4,6},{5,7},{6,4},{7,5},{8,10},{9,11},{10,... | collective-permute-start | bytes 1179656 | tf_op jit(solution)/shard_map/ppermute | solution.py:1069
  237.0 17.2 %collective-permute-start.48 = (bf16[96,16,128]{2,1,0:T(8,128)(2,1)S(1)}, bf16[96,16,128]{2,1,0:T(8,128)(2,1)S(1)}, u32[]{:S(2)}, u32[]{:S(2)}) collective-permute-start(bf16[96,16,128]{2,1,0:T(8,128)(2,1)S(1)} %pad_maximum_fusion.3), channel_id=1, source_target_pairs={{0,4},{1,5},{2,6},{3,7},{4,0},{5,1},{6,2},{7,3},{8,12},{9,13},{10,... | collective-permute-start | bytes 1179656 | tf_op jit(solution)/shard_map/ppermute | solution.py:1069
  239.2 6.2 %collective-permute-start.53 = (bf16[16,16,128]{2,1,0:T(8,128)(2,1)S(1)}, bf16[16,16,128]{2,1,0:T(8,128)(2,1)S(1)}, u32[]{:S(2)}, u32[]{:S(2)}) collective-permute-start(bf16[16,16,128]{2,1,0:T(8,128)(2,1)S(1)} %get-tuple-element.280), channel_id=1, source_target_pairs={{0,24},{1,25},{2,26},{3,27},{4,28},{5,29},{6,30},{7,31},{8,16},{9,... | collective-permute-start | bytes 196616 | tf_op jit(solution)/shard_map/ppermute | solution.py:1069
  241.0 5.3 %collective-permute-start.52 = (bf16[16,16,128]{2,1,0:T(8,128)(2,1)S(1)}, bf16[16,16,128]{2,1,0:T(8,128)(2,1)S(1)}, u32[]{:S(2)}, u32[]{:S(2)}) collective-permute-start(bf16[16,16,128]{2,1,0:T(8,128)(2,1)S(1)} %get-tuple-element.281), channel_id=1, source_target_pairs={{0,8},{1,9},{2,10},{3,11},{4,12},{5,13},{6,14},{7,15},{8,0},{9,1},... | collective-permute-start | bytes 196616 | tf_op jit(solution)/shard_map/ppermute | solution.py:1069
  245.4 5.2 %collective-permute-start.51 = (bf16[16,16,128]{2,1,0:T(8,128)(2,1)S(1)}, bf16[16,16,128]{2,1,0:T(8,128)(2,1)S(1)}, u32[]{:S(2)}, u32[]{:S(2)}) collective-permute-start(bf16[16,16,128]{2,1,0:T(8,128)(2,1)S(1)} %get-tuple-element.282), channel_id=1, source_target_pairs={{0,16},{1,17},{2,18},{3,19},{4,20},{5,21},{6,22},{7,23},{8,24},{9,... | collective-permute-start | bytes 196616 | tf_op jit(solution)/shard_map/ppermute | solution.py:1069
  (36 other events, 183.7 us)
where the time goes:
time: 265 us; the launch traced here: 264 us
  Pallas kernels  116 us (44%)
  waiting for transfers between devices  60.5 us (23%)
  starting transfers between devices  58 us (22%)
  local copies, waits for them, and re-layouts  18.3 us (7%)
  other arithmetic  9.72 us (4%)
    ppermute x55, waiting for transfers between devices, exchange(): return lax.ppermute(value, AXES, [(d, d ^ mask) for d in range(devices)])  60.5 us
    ppermute x55, starting transfers between devices, exchange(): return lax.ppermute(value, AXES, [(d, d ^ mask) for d in range(devices)])  58 us
    pallas_call x1, Pallas kernels, message_backward(): pl.pallas_call(functools.partial(message_backward_kernel, sb, blocks, gro...  27.7 us
    pallas_call x5, Pallas kernels, small_call(): pl.pallas_call(kernel, grid=(1,), in_specs=[pl.BlockSpec(memory_space=plt...  24.7 us
    pallas_call x1, Pallas kernels, edge_branch(): pl.pallas_call(functools.partial(edge_kernel, sb, blocks, hi_chunks, by_r...  23.7 us
    pallas_call x1, Pallas kernels, message_forward(): pl.pallas_call(functools.partial(message_forward_kernel, sb, by_rows), gr...  18.9 us
    pallas_call x2, Pallas kernels, edge_weights(): pl.pallas_call(functools.partial(edge_weights_kernel, slots // sb, pairs)...  11.7 us
    unnamed x67, local copies, waits for them, and re-layouts  10.7 us
  transfers between devices with their start and end apart: 55, of which 27 were waited for; matrix products, arithmetic and copies ran while one was open for 5% of the time, Pallas kernels for 29%

commit v1 on v0

--- a/solution.py
+++ b/solution.py
@@ -397,9 +397,13 @@
     )(node_lo, node_hi, node_own, edge, idx_row, idx_row, live_col, m1, b1, m2, b2)
 
 
+def joined(refs, at):
+    return jnp.concatenate([refs[2 * at][...], refs[2 * at + 1][...]], axis=0)
+
+
 def residue_forward_kernel(parts, node, total, m3, b3, g1, fb2, g2, e_first, e_far, eb, *refs):
-    f1, f2 = refs[:parts], refs[parts : 2 * parts]
-    h1b_out, n1_out, sc1_out, n2_out, sc2_out, slope_out, h2b_out, far_out, own_out = refs[2 * parts :]
+    f1, f2 = refs[:parts], refs[parts : 3 * parts]
+    h1b_out, n1_out, sc1_out, n2_out, sc2_out, slope_out, h2b_out, far_out, own_out = refs[3 * parts :]
     width, hidden = node.shape[1], f1[0].shape[1]
     u1 = node[...].astype(F32) + fine(dot, total[...], m3[...]) + b3[...]
     n1, sc1 = norm(u1)
@@ -414,7 +418,7 @@
         bias = bias[0:1] + bias[1:2] + bias[2:3]
         act, slope = gelu_parts(dot(h1b, f1[p][:width, :]) + bias)
         slope_out[:, p * hidden : (p + 1) * hidden] = slope
-        part = dot(act.astype(BF16), f2[p][...])
+        part = dot(act.astype(BF16), joined(f2, p))
         y2 = part if y2 is None else y2 + part
     n2, sc2 = norm(h1 + (y2 + fb2[...]))
     h2b = (n2 * g2[...]).astype(BF16)
@@ -694,8 +698,8 @@
 ):
     far = refs[:pieces]
     f1 = refs[pieces : pieces + parts]
-    f2 = refs[pieces + parts : pieces + 2 * parts]
-    gu1_out, v_out, both_out, slab = refs[pieces + 2 * parts :]
+    f2 = refs[pieces + parts : pieces + 3 * parts]
+    gu1_out, v_out, both_out, slab = refs[pieces + 3 * parts :]
     width, hidden = h2b.shape[1], f1[0].shape[1]
     far_sum = far[0][: far[1].shape[0], :]
     for ref in far[1:]:
@@ -713,7 +717,7 @@
     both_out[:, width:] = gy2
     g_h1 = g_u2
     for p in range(parts):
-        gy1 = dot_back(gy2, f2[p][...]) * slope[:, p * hidden : (p + 1) * hidden]
+        gy1 = dot_back(gy2, joined(f2, p)) * slope[:, p * hidden : (p + 1) * hidden]
         g_h1 = g_h1 + dot_back(gy1.astype(BF16), f1[p][:width, :])
     gain_one = column_sum(g_h1 * n1[...])
     g_u1 = norm_back(g_h1 * g1[...], n1[...], sc1[:, :1])
@@ -808,7 +812,7 @@
 
 
 def message_backward_kernel(
-    sb, blocks, groups, codes, base, order, v, a1, s1, s2, edge, low_three, low_edge, local_row, live_col,
+    sb, blocks, groups, at_once, codes, base, order, v, a1, s1, s2, edge, low_three, low_edge, local_row, live_col,
     m1, m2, e_first, node_lo, node_hi, node, early, e1g, eb1,
     edge_grad, far_keep, far_send, own, keep, send,
     low_two, low_one, grad, rows_ref, moved, m2g, m1eg, m1fg, b2s, slab,
@@ -868,20 +872,26 @@
     def _():
         deep = far_keep.shape[0]
         count = block * blocks // groups
-        values, local = group_rows(order, (step - blocks) * count, count, rows_ref, moved, width)
-        sums = group_sums(values, local, 2 * deep * rows).astype(BF16)
-        near = jnp.concatenate(
-            [ref[at, 0] for ref in (node_lo, node_hi) for at in range(deep)], axis=0
-        )
-        m1fg[...] += dot_rows(near, sums)
         height = rows // 16
-        for at in range(2 * deep):
-            out = (far_keep if at < deep else far_send).at[at % deep, 0]
-            for j in range(tiles):
-                tile = sums[at * rows : (at + 1) * rows, j * LANES : (j + 1) * LANES]
-                out[j * height : (j + 1) * height] = tile.reshape(height, 16, LANES)
-
-    @pl.when(step == blocks + groups - 1)
+        picked = [
+            group_rows(
+                order, ((step - blocks) * at_once + i) * count, count, rows_ref, moved.at[i], width
+            )
+            for i in range(at_once)
+        ]
+        for i, (values, local) in enumerate(picked):
+            sums = group_sums(values, local, 2 * deep * rows).astype(BF16)
+            near = jnp.concatenate(
+                [ref[at, i] for ref in (node_lo, node_hi) for at in range(deep)], axis=0
+            )
+            m1fg[...] += dot_rows(near, sums)
+            for at in range(2 * deep):
+                out = (far_keep if at < deep else far_send).at[at % deep, i]
+                for j in range(tiles):
+                    tile = sums[at * rows : (at + 1) * rows, j * LANES : (j + 1) * LANES]
+                    out[j * height : (j + 1) * height] = tile.reshape(height, 16, LANES)
+
+    @pl.when(step == blocks + groups // at_once - 1)
     def _():
         count = early.shape[0]
         slab[:count] = early[...]
@@ -914,6 +924,7 @@
     edges = slots * rows
     half = node_lo.shape[0]
     deep = half // rows // groups
+    at_once = 2 if groups % 2 == 0 else 1
     tiles = rows * width // (16 * LANES)
     slab = slab_tiles(weight_shapes(width, edge_width), len(codes)) * len(codes)
     node_lo, node_hi = [n.reshape(deep, groups, rows, width) for n in (node_lo, node_hi)]
@@ -922,13 +933,13 @@
     row_spec = pl.BlockSpec((block, width), lambda i: (blk(i), 0))
     slot_spec = pl.BlockSpec((sb, rows, edge_width), lambda i: (blk(i), 0, 0))
     edge_spec = pl.BlockSpec((block, edge_width), lambda i: (blk(i), 0))
-    node_spec = pl.BlockSpec((deep, 1, rows, width), lambda i: (*group_at(i), 0, 0))
-    far_spec = pl.BlockSpec((deep, 1, tiles, 16, LANES), lambda i: (*group_at(i), 0, 0, 0))
+    node_spec = pl.BlockSpec((deep, at_once, rows, width), lambda i: (*group_at(i), 0, 0))
+    far_spec = pl.BlockSpec((deep, at_once, tiles, 16, LANES), lambda i: (*group_at(i), 0, 0, 0))
     slab_spec = pl.BlockSpec((slab // 2, 16, LANES), lambda i: (0, 0, 0))
     smem = pl.BlockSpec(memory_space=pltpu.SMEM)
     return pl.pallas_call(
-        functools.partial(message_backward_kernel, sb, blocks, groups, codes),
-        grid=(blocks + groups,),
+        functools.partial(message_backward_kernel, sb, blocks, groups, at_once, codes),
+        grid=(blocks + groups // at_once,),
         in_specs=[
             smem,
             smem,
@@ -965,7 +976,7 @@
             pltpu.VMEM((block, width), BF16),
             pltpu.VMEM((block, width), F32),
             pltpu.VMEM((edges * 8, LANES), F32),
-            pltpu.VMEM((edges // groups * 8, LANES), F32),
+            pltpu.VMEM((at_once, edges // groups * 8, LANES), F32),
             pltpu.VMEM((width, width), F32),
             pltpu.VMEM((edge_width, width), F32),
             pltpu.VMEM((width, width), F32),
@@ -1177,31 +1188,40 @@
     e_first = edge_first.T
     e_far = e_first[:, width + edge_width :]
     f1x = jnp.concatenate([feed_first, split_three(row(feed_first_bias))], axis=0)
-    f2x = feed_second
+    cut = feed_second.shape[0] // 2
+    hid_masks = [m for m in masks if m < hid_count]
+
+    def across(pieces):
+        for mask in hid_masks[:-1]:
+            pieces = pieces + [exchange(p, mask, devices) for p in pieces]
+        return pieces
+
+    def over(pieces):
+        return pieces + [exchange(p, hid_masks[-1], devices) for p in pieces]
+
+    f2a = across([feed_second[:cut]])
 
     stack = lambda pieces: jnp.concatenate(pieces, axis=0)
     *outer, near = groups
 
     held = stack(sent_around(node_in, outer[0], devices))
-    held, idx_row, local_row = tied(held, idx_row, local_row)
+    held, idx_row, local_row, f2a = tied(held, idx_row, local_row, f2a)
     for group in outer[1:]:
         held = stack(sent_around(held, group, devices))
-    held, f1x, f2x, edge_order, live_col = tied(held, f1x, f2x, edge_order, live_col)
+    f2b = feed_second[cut:]
+    held, f1x, f2a, f2b, edge_order, live_col = tied(held, f1x, f2a, f2b, edge_order, live_col)
     node_lo, node_hi = sent_around(held, near, devices)
 
-    f1, f2 = [f1x], [f2x]
-    hid_masks = [m for m in masks if m < hid_count]
-    for mask in hid_masks[:-1]:
-        f1, f2 = [pieces + [exchange(p, mask, devices) for p in pieces] for pieces in (f1, f2)]
+    f2a = over(f2a)
+    f1, f2b = across([f1x]), across([f2b])
 
     a1, s1, s2, total = message_forward(
         node_lo, node_hi, node_in, edge, idx_row, live_col, message_first,
         row(message_first_bias), message_second, row(message_second_bias),
     )
-    total, f1, f2, e_far = tied(total, f1, f2, e_far)
-    f1, f2 = [
-        pieces + [exchange(p, hid_masks[-1], devices) for p in pieces] for pieces in (f1, f2)
-    ]
+    total, f1, f2a, f2b, e_far = tied(total, f1, f2a, f2b, e_far)
+    f1, f2b = over(f1), over(f2b)
+    f2 = [half for pair in zip(f2a, f2b) for half in pair]
     h1b, n1, sc1, n2, sc2, slope, h2b, far_part, own_part = residue_forward(
         node_in, total, message_third, row(message_third_bias), row(norm_one),
         row(feed_second_bias), row(norm_two), e_first, e_far, row(edge_first_bias), f1, f2,
@@ -1218,13 +1238,17 @@
     )
 
     terms = [lo, exchange(hi, near[0], devices)]
-    made = None
+    pairs, made = [(act_two, low_three), (act_one, low_two)], []
     for group in reversed(outer):
-        terms = shared_out(add_up(terms), group, devices)
-        if made is None:
-            made = edge_weights((act_two, act_one), (low_three, low_two), rows)
-            terms, made = tied(terms, made)
-    e3g, e2g, eb3, eb2 = made
+        total_far = add_up(terms)
+        if pairs:
+            left, right = pairs.pop(0)
+            total_far, left = tied(total_far, left)
+        terms = shared_out(total_far, group, devices)
+        if len(made) < 2:
+            terms, got = tied(terms, edge_weights((left,), (right,), rows))
+            made.append(got)
+    (e3g, eb3), (e2g, eb2) = made
     g_u1, v, both, early = residue_backward(
         (
             node_cotangent, own_sum, e_first, e_far, h1b, h2b, n1, sc1, n2, sc2, slope, row(norm_one),

time: 265 us -> 263 us (level)
  waiting for transfers between devices: 60.5 us -> 55.6 us
    ppermute x55 -> x58, waiting for transfers between devices: 60.5 us -> 55.6 us  [exchange(): return lax.ppermute(value, AXES, [(d, d ^ mask) for d in range(devices)])]
    pallas_call x2 -> x3, Pallas kernels: 11.7 us -> 15.7 us  [edge_weights(): pl.pallas_call(functools.partial(edge_weights_kernel, slots // sb, pairs)...]
    ppermute x55 -> x58, starting transfers between devices: 58 us -> 60.4 us  [exchange(): return lax.ppermute(value, AXES, [(d, d ^ mask) for d in range(devices)])]
    unnamed x67 -> x79, local copies, waits for them, and re-layouts: 10.7 us -> 10.6 us
  transfers between devices with their start and end apart: 55 -> 58, of which waited for: 27 -> 25; matrix products, arithmetic and copies ran while one was open for 5% -> 5% of each run, Pallas kernels for 29% -> 30%
where the time goes in v1:
time: 263 us; the launch traced here: 262 us
  Pallas kernels  118 us (45%)
  starting transfers between devices  60.4 us (23%)
  waiting for transfers between devices  55.6 us (21%)
  local copies, waits for them, and re-layouts  17.4 us (7%)
  other arithmetic  9.06 us (3%)
    ppermute x58, starting transfers between devices, exchange(): return lax.ppermute(value, AXES, [(d, d ^ mask) for d in range(devices)])  60.4 us
    ppermute x58, waiting for transfers between devices, exchange(): return lax.ppermute(value, AXES, [(d, d ^ mask) for d in range(devices)])  55.6 us
    pallas_call x1, Pallas kernels, message_backward(): pl.pallas_call(functools.partial(message_backward_kernel, sb, blocks, gro...  25.7 us
    pallas_call x5, Pallas kernels, small_call(): pl.pallas_call(kernel, grid=(1,), in_specs=[pl.BlockSpec(memory_space=plt...  24.7 us
    pallas_call x1, Pallas kernels, edge_branch(): pl.pallas_call(functools.partial(edge_kernel, sb, blocks, hi_chunks, by_r...  23.7 us
    pallas_call x1, Pallas kernels, message_forward(): pl.pallas_call(functools.partial(message_forward_kernel, sb, by_rows), gr...  18.9 us
    pallas_call x3, Pallas kernels, edge_weights(): pl.pallas_call(functools.partial(edge_weights_kernel, slots // sb, pairs)...  15.7 us
    unnamed x79, local copies, waits for them, and re-layouts  10.6 us
  transfers between devices with their start and end apart: 58, of which 25 were waited for; matrix products, arithmetic and copies ran while one was open for 5% of the time, Pallas kernels for 30%

profile of v1, /device:TPU:0, one launch (start us, length us, event | category | flops | bytes accessed | tf_op | source)
XLA Modules:
  0.0 262.0 jit_solution(15489730422947114726)
XLA Ops:
  0.7 5.1 %collective-permute-start.2 = (bf16[64,512]{1,0:T(8,128)(2,1)}, bf16[64,512]{1,0:T(8,128)(2,1)S(1)}, u32[]{:S(2)}, u32[]{:S(2)}) collective-permute-start(bf16[64,512]{1,0:T(8,128)(2,1)} %node.3), channel_id=1, source_target_pairs={{0,24},{1,25},{2,26},{3,27},{4,28},{5,29},{6,30},{7,31},{8,16},{9,... | collective-permute-start | bytes 196616 | tf_op jit(solution)/shard_map/ppermute | solution.py:1080
  7.5 1.7 collective-permute-start.3
  13.4 1.7 collective-permute-done.3.refs_6_.refs_10_
  15.1 2.4 collective-permute-start.6
  19.2 4.8 %group_order.1 = s32[30,128]{1,0:T(8,128)} custom-call(s32[32,128]{1,0:T(8,128)} %pad_bitcast_fusion.names), custom_call_target="tpu_custom_call" | custom-call | tf_op jit(solution)/shard_map/group_order/pallas_call | solution.py:180
  25.7 2.4 collective-permute-done.5
  29.1 1.7 slice.118.e_far
  34.3 18.9 %message_forward.1 = (bf16[3840,512]{1,0:T(8,128)(2,1)}, bf16[3840,512]{1,0:T(8,128)(2,1)}, bf16[3840,512]{1,0:T(8,128)(2,1)}, f32[64,512]{1,0:T(8,128)}) custom-call(bf16[1024,512]{1,0:T(8,128)(2,1)} %copy-done.18, bf16[1024,512]{1,0:T(8,128)(2,1)} %copy-done.32, bf16[64,512]{1,0:T(8,128)(2,1)} %node.3, bf16[60,64,192]{2,1,0:T(8,128)(2,1)} %bitcast.48, ...), custom_call_target="tpu_custom_call" | custom-call | flops 10821304320 | bytes 15237120 | tf_op jit(solution)/shard_map/message_forward/pallas_call | solution.py:364
  54.4 2.1 collective-permute-done.14.refs_9_.refs_13_
  57.9 5.3 %residue_forward.1 = (bf16[64,512]{1,0:T(8,128)(2,1)}, f32[64,512]{1,0:T(8,128)}, f32[64,128]{1,0:T(8,128)}, f32[64,512]{1,0:T(8,128)}, f32[64,128]{1,0:T(8,128)...) custom-call(bf16[64,512]{1,0:T(8,128)(2,1)} %node.3, ...), custom_call_target="tpu_custom_call" | custom-call | flops 268435456 | bytes 5242880 | tf_op jit(solution)/shard_map/residue_forward/pallas_call | solution.py:180
  63.2 3.4 %collective-permute-start.18 = (bf16[64,192]{1,0:T(8,128)(2,1)}, bf16[64,192]{1,0:T(8,128)(2,1)S(1)}, u32[]{:S(2)}, u32[]{:S(2)}) collective-permute-start(bf16[64,192]{1,0:T(8,128)(2,1)} %get-tuple-element.178), channel_id=1, source_target_pairs={{0,24},{1,25},{2,26},{3,27},{4,28},{5,29},{6,30},{7,31},{8,16},{9,... | collective-permute-start | bytes 73736 | tf_op jit(solution)/shard_map/ppermute | solution.py:1080
  68.5 3.5 %collective-permute-done.16 = bf16[64,192]{1,0:T(8,128)(2,1)S(1)} collective-permute-done((bf16[64,192]{1,0:T(8,128)(2,1)}, bf16[64,192]{1,0:T(8,128)(2,1)S(1)}, u32[]{:S(2)}, u32[]{:S(2)}) %collective-permute-start.16) | collective-permute-done | bytes 24608 | tf_op jit(solution)/shard_map/ppermute | solution.py:1080
  75.6 1.7 collective-permute-done.19
  77.3 3.6 %collective-permute-done.20 = bf16[256,192]{1,0:T(8,128)(2,1)S(1)} collective-permute-done((bf16[256,192]{1,0:T(8,128)(2,1)S(1)}, bf16[256,192]{1,0:T(8,128)(2,1)S(1)}, u32[]{:S(2)}, u32[]{:S(2)}) %collective-permute-start.20) | collective-permute-done | bytes 98336 | tf_op jit(solution)/shard_map/ppermute | solution.py:1080
  81.1 1.9 collective-permute-done.22.far_hi
  83.8 23.7 %edge_branch.1 = (bf16[60,64,192]{2,1,0:T(8,128)(2,1)}, bf16[3840,192]{1,0:T(8,128)(2,1)}, bf16[3840,192]{1,0:T(8,128)(2,1)}, bf16[3840,192]{1,0:T(8,128)(2,1)},...) custom-call(bf16[1024,192]{1,0:T(8,128)(2,1)} %copy-done.28, ...), custom_call_target="tpu_custom_call" | custom-call | flops 7455375360 | bytes 11796480 | tf_op jit(solution)/shard_map/edge_branch/pallas_call | solution.py:577
  107.7 2.0 collective-permute-done.23
  111.1 1.6 collective-permute-start.26
  114.6 5.2 %edge_weights.3 = (f32[192,192]{1,0:T(8,128)}, f32[1,192]{1,0:T(1,128)}) custom-call(bf16[3840,192]{1,0:T(8,128)(2,1)} %get-tuple-element.193.refs_0_, bf16[3840,192]{1,0:T(8,128)(2,1)} %get-tuple-element.194.refs_1_.low_three), custom_call_target="tpu_custom_call" | custom-call | flops 283115520 | bytes 2949120 | tf_op jit(solution)/shard_map/edge_weights/pallas_call | solution.py:666
  120.5 1.6 collective-permute-start.29
  122.5 2.5 collective-permute-start.27
  125.0 5.2 %edge_weights.4 = (f32[192,192]{1,0:T(8,128)}, f32[1,192]{1,0:T(1,128)}) custom-call(bf16[3840,192]{1,0:T(8,128)(2,1)} %get-tuple-element.203.refs_0_, bf16[3840,192]{1,0:T(8,128)(2,1)} %get-tuple-element.204.refs_1_), custom_call_target="tpu_custom_call" | custom-call | flops 283115520 | bytes 2949120 | tf_op jit(solution)/shard_map/edge_weights/pallas_call | solution.py:666
  130.8 6.8 %residue_backward.1 = (f32[64,512]{1,0:T(8,128)}, f32[64,512]{1,0:T(8,128)}, bf16[64,1024]{1,0:T(8,128)(2,1)}, bf16[278,16,128]{2,1,0:T(8,128)(2,1)}) custom-call(bf16[64,512]{1,0:T(8,128)(2,1)} %node_cot.1, f32[64,192]{1,0:T(8,128)} %get-tuple-element.182.own_sum, bf16[192,1216]{1,0:T(8,128)(2,1)} %bitcast.46, bf16[192,512]{1,0:T(8,128)(2,1)} %slice.118.e_far, ...), custom_call_target="tpu_custom_call" | custom-call | flops 268435456 | bytes 8388608 | tf_op jit(solution)/shard_map/residue_backward/pallas_call | solution.py:180
  137.7 1.6 collective-permute-start.32
  139.2 2.9 %collective-permute-start.30 = (bf16[64,1024]{1,0:T(8,128)(2,1)}, bf16[64,1024]{1,0:T(8,128)(2,1)S(1)}, u32[]{:S(2)}, u32[]{:S(2)}) collective-permute-start(bf16[64,1024]{1,0:T(8,128)(2,1)} %get-tuple-element.219), channel_id=1, source_target_pairs={{0,16},{1,17},{2,18},{3,19},{4,20},{5,21},{6,22},{7,23},{8,24},{9,... | collective-permute-start | bytes 393224 | tf_op jit(solution)/shard_map/ppermute | solution.py:1080
  142.1 5.3 %edge_weights.5 = (f32[192,192]{1,0:T(8,128)}, f32[1,192]{1,0:T(1,128)}) custom-call(bf16[3840,192]{1,0:T(8,128)(2,1)} %get-tuple-element.220.refs_0_.low_edge, bf16[60,64,192]{2,1,0:T(8,128)(2,1)} %bitcast.50), custom_call_target="tpu_custom_call" | custom-call | flops 283115520 | bytes 2949120 | tf_op jit(solution)/shard_map/edge_weights/pallas_call | solution.py:666
  147.6 3.7 %collective-permute-done.30 = bf16[64,1024]{1,0:T(8,128)(2,1)S(1)} collective-permute-done((bf16[64,1024]{1,0:T(8,128)(2,1)}, bf16[64,1024]{1,0:T(8,128)(2,1)S(1)}, u32[]{:S(2)}, u32[]{:S(2)}) %collective-permute-start.30) | collective-permute-done | bytes 131104 | tf_op jit(solution)/shard_map/ppermute | solution.py:1080
  151.4 1.6 collective-permute-start.35
  154.9 25.7 %message_backward.1 = (f32[60,64,192]{2,1,0:T(8,128)}, bf16[2,8,16,16,128]{4,3,2,1,0:T(8,128)(2,1)}, bf16[2,8,16,16,128]{4,3,2,1,0:T(8,128)(2,1)}, f32[64,512]{1...) custom-call(s32[1]{0:T(128)} %bitcast.16.base, s32[1,3840]{1,0:T(1,128)} %bitcast.55, ...), custom_call_target="tpu_custom_call" | custom-call | flops 6794772480 | bytes 19169280 | tf_op jit(solution)/shard_map/message_backward/pallas_call | solution.py:940
  180.9 1.7 copy-done.31
  182.6 3.4 %collective-permute-done.36 = bf16[384,16,128]{2,1,0:T(8,128)(2,1)S(1)} collective-permute-done((bf16[384,16,128]{2,1,0:T(8,128)(2,1)S(1)}, bf16[384,16,128]{2,1,0:T(8,128)(2,1)S(1)}, u32[]{:S(2)}, u32[]{:S(2)}) %collective-permute-start.36) | collective-permute-done | bytes 1572896 | tf_op jit(solution)/shard_map/ppermute | solution.py:1080
  188.3 1.6 collective-permute-start.39
  194.9 9.2 %feed_gradients.1 = (f32[512,512]{1,0:T(8,128)}, f32[512,512]{1,0:T(8,128)}, f32[1,512]{1,0:T(1,128)}) custom-call(bf16[1024,1024]{1,0:T(8,128)(2,1)} %copy-done.9, bf16[1024,1024]{1,0:T(8,128)(2,1)} %copy-done.30, bf16[512,512]{1,0:T(8,128)(2,1)} %f1.1, f32[1,512]{1,0:T(1,128)} %bitcast.62, bf16[512,512]{1,0:T(8,128)(2,1)} %f2.1), custom_call_target="tpu_custom_call" | custom-call | flops 4294967296 | bytes 4194304 | tf_op jit(solution)/shard_map/feed_gradients/pallas_call | solution.py:781
  204.2 4.8 %collective-permute-done.38 = bf16[96,16,128]{2,1,0:T(8,128)(2,1)S(1)} collective-permute-done((bf16[96,16,128]{2,1,0:T(8,128)(2,1)}, bf16[96,16,128]{2,1,0:T(8,128)(2,1)S(1)}, u32[]{:S(2)}, u32[]{:S(2)}) %collective-permute-start.38) | collective-permute-done | bytes 393248 | tf_op jit(solution)/shard_map/ppermute | solution.py:1080
  210.3 1.6 collective-permute-start.44
  211.9 1.8 collective-permute-start.43
  216.1 2.9 %collective-permute-done.42 = bf16[24,16,128]{2,1,0:T(8,128)(2,1)S(1)} collective-permute-done((bf16[24,16,128]{2,1,0:T(8,128)(2,1)S(1)}, bf16[24,16,128]{2,1,0:T(8,128)(2,1)S(1)}, u32[]{:S(2)}, u32[]{:S(2)}) %collective-permute-start.42) | collective-permute-done | bytes 98336 | tf_op jit(solution)/shard_map/ppermute | solution.py:1080
  219.0 1.6 collective-permute-start.50
  223.2 2.3 collective-permute-start.48
  226.3 3.1 %collective-permute-done.49 = bf16[24,16,128]{2,1,0:T(8,128)(2,1)S(1)} collective-permute-done((bf16[24,16,128]{2,1,0:T(8,128)(2,1)S(1)}, bf16[24,16,128]{2,1,0:T(8,128)(2,1)S(1)}, u32[]{:S(2)}, u32[]{:S(2)}) %collective-permute-start.49) | collective-permute-done | bytes 98336 | tf_op jit(solution)/shard_map/ppermute | solution.py:1080
  229.8 2.7 %collective-permute-done.47 = bf16[24,16,128]{2,1,0:T(8,128)(2,1)S(1)} collective-permute-done((bf16[24,16,128]{2,1,0:T(8,128)(2,1)S(1)}, bf16[24,16,128]{2,1,0:T(8,128)(2,1)S(1)}, u32[]{:S(2)}, u32[]{:S(2)}) %collective-permute-start.47) | collective-permute-done | bytes 98336 | tf_op jit(solution)/shard_map/ppermute | solution.py:1080
  232.6 1.6 collective-permute-start.53
  237.1 2.2 collective-permute-start.56
  239.3 4.1 %collective-permute-done.56.refs_3_ = bf16[16,16,128]{2,1,0:T(8,128)(2,1)S(1)} collective-permute-done((bf16[16,16,128]{2,1,0:T(8,128)(2,1)S(1)}, bf16[16,16,128]{2,1,0:T(8,128)(2,1)S(1)}, u32[]{:S(2)}, u32[]{:S(2)}) %collective-permute-start.56) | collective-permute-done | bytes 65568 | tf_op jit(solution)/shard_map/ppermute | solution.py:1080
  244.4 4.1 %collective-permute-done.54.refs_1_ = bf16[16,16,128]{2,1,0:T(8,128)(2,1)S(1)} collective-permute-done((bf16[16,16,128]{2,1,0:T(8,128)(2,1)S(1)}, bf16[16,16,128]{2,1,0:T(8,128)(2,1)S(1)}, u32[]{:S(2)}, u32[]{:S(2)}) %collective-permute-start.54) | collective-permute-done | bytes 65568 | tf_op jit(solution)/shard_map/ppermute | solution.py:1080
  249.2 3.0 %node_gradient.1 = f32[64,512]{1,0:T(8,128)} custom-call(f32[64,512]{1,0:T(8,128)} %get-tuple-element.258.g_u1, f32[64,512]{1,0:T(8,128)} %get-tuple-element.259.own, bf16[1216,512]{1,0:T(8,128)(2,1)} %m1.5, f32[64,16,128]{2,1,0:T(8,128)} %get-tuple-element.290.refs_0_, bf16[16,16,128]{2,1,0:T(8,128)(2,1)} %copy-done.24, bf16[16,16,128]{2,1,0:T(8,128)(2,1)} %copy-done.23, ...), custom_call_target="tpu_custom_call" | custom-call | flops 134217728 | bytes 2097152 | tf_op jit(solution)/shard_map/node_gradient/pallas_call | solution.py:180
  252.5 3.4 %collective-permute-done.57.second = bf16[384,16,128]{2,1,0:T(8,128)(2,1)S(1)} collective-permute-done((bf16[384,16,128]{2,1,0:T(8,128)(2,1)S(1)}, bf16[384,16,128]{2,1,0:T(8,128)(2,1)S(1)}, u32[]{:S(2)}, u32[]{:S(2)}) %collective-permute-start.57) | collective-permute-done | bytes 1572896 | tf_op jit(solution)/shard_map/ppermute | solution.py:1080
  257.0 4.7 %weight_gradients.1 = (f32[1216,512]{1,0:T(8,128)}, f32[1,512]{1,0:T(1,128)}, f32[512,512]{1,0:T(8,128)}, f32[1,512]{1,0:T(1,128)}, f32[512,512]{1,0:T(8,128)}, ...) custom-call(s32[1]{0:T(128)} %bitcast.16.base, ...), custom_call_target="tpu_custom_call" | custom-call | bytes 10485760 | tf_op jit(solution)/shard_map/weight_gradients/pallas_call | solution.py:180
  (200 shorter events, 50.8 us)
Async XLA Ops:
  0.7 11.8 %collective-permute-start.2 = (bf16[64,512]{1,0:T(8,128)(2,1)}, bf16[64,512]{1,0:T(8,128)(2,1)S(1)}, u32[]{:S(2)}, u32[]{:S(2)}) collective-permute-start(bf16[64,512]{1,0:T(8,128)(2,1)} %node.3), channel_id=1, source_target_pairs={{0,24},{1,25},{2,26},{3,27},{4,28},{5,29},{6,30},{7,31},{8,16},{9,... | collective-permute-start | bytes 196616 | tf_op jit(solution)/shard_map/ppermute | solution.py:1080
  5.8 6.7 %collective-permute-start.1 = (bf16[64,512]{1,0:T(8,128)(2,1)}, bf16[64,512]{1,0:T(8,128)(2,1)S(1)}, u32[]{:S(2)}, u32[]{:S(2)}) collective-permute-start(bf16[64,512]{1,0:T(8,128)(2,1)} %node.3), channel_id=1, source_target_pairs={{0,8},{1,9},{2,10},{3,11},{4,12},{5,13},{6,14},{7,15},{8,0},{9,1},... | collective-permute-start | bytes 196616 | tf_op jit(solution)/shard_map/ppermute | solution.py:1080
  5.8 6.7 %collective-permute-start = (bf16[64,512]{1,0:T(8,128)(2,1)}, bf16[64,512]{1,0:T(8,128)(2,1)S(1)}, u32[]{:S(2)}, u32[]{:S(2)}) collective-permute-start(bf16[64,512]{1,0:T(8,128)(2,1)} %node.3), channel_id=1, source_target_pairs={{0,16},{1,17},{2,18},{3,19},{4,20},{5,21},{6,22},{7,23},{8,24},{9,... | collective-permute-start | bytes 196616 | tf_op jit(solution)/shard_map/ppermute | solution.py:1080
  7.5 7.6 %collective-permute-start.3 = (bf16[256,512]{1,0:T(8,128)(2,1)S(1)}, bf16[256,512]{1,0:T(8,128)(2,1)S(1)}, u32[]{:S(2)}, u32[]{:S(2)}) collective-permute-start(bf16[256,512]{1,0:T(8,128)(2,1)S(1)} %get-tuple-element.171.refs_4_.refs_8_), channel_id=1, source_target_pairs={{0,2},{1,3},{2,0},{3,1},{4,6},{5,7},{6,4},{7,5},{8,10},{9,11},{10,... | collective-permute-start | bytes 786440 | tf_op jit(solution)/shard_map/ppermute | solution.py:1080
  15.1 10.6 %collective-permute-start.6 = (bf16[256,512]{1,0:T(8,128)(2,1)S(1)}, bf16[256,512]{1,0:T(8,128)(2,1)S(1)}, u32[]{:S(2)}, u32[]{:S(2)}) collective-permute-start(bf16[256,512]{1,0:T(8,128)(2,1)S(1)} %pad_maximum_fusion.4), channel_id=1, source_target_pairs={{0,6},{1,7},{2,4},{3,5},{4,2},{5,3},{6,0},{7,1},{8,14},{9,15},{10,... | collective-permute-start | bytes 786440 | tf_op jit(solution)/shard_map/ppermute | solution.py:1080
  17.5 10.6 %collective-permute-start.5 = (bf16[256,512]{1,0:T(8,128)(2,1)S(1)}, bf16[256,512]{1,0:T(8,128)(2,1)S(1)}, u32[]{:S(2)}, u32[]{:S(2)}) collective-permute-start(bf16[256,512]{1,0:T(8,128)(2,1)S(1)} %pad_maximum_fusion.4), channel_id=1, source_target_pairs={{0,2},{1,3},{2,0},{3,1},{4,6},{5,7},{6,4},{7,5},{8,10},{9,11},{10,... | collective-permute-start | bytes 786440 | tf_op jit(solution)/shard_map/ppermute | solution.py:1080
  18.0 10.1 %collective-permute-start.4 = (bf16[256,512]{1,0:T(8,128)(2,1)S(1)}, bf16[256,512]{1,0:T(8,128)(2,1)S(1)}, u32[]{:S(2)}, u32[]{:S(2)}) collective-permute-start(bf16[256,512]{1,0:T(8,128)(2,1)S(1)} %pad_maximum_fusion.4), channel_id=1, source_target_pairs={{0,4},{1,5},{2,6},{3,7},{4,0},{5,1},{6,2},{7,3},{8,12},{9,13},{10,... | collective-permute-start | bytes 786440 | tf_op jit(solution)/shard_map/ppermute | solution.py:1080
  30.8 22.4 %collective-permute-start.9 = (bf16[256,512]{1,0:T(8,128)(2,1)S(1)}, bf16[256,512]{1,0:T(8,128)(2,1)S(1)}, u32[]{:S(2)}, u32[]{:S(2)}) collective-permute-start(bf16[256,512]{1,0:T(8,128)(2,1)S(1)} %get-tuple-element.171.refs_4_.refs_8_), channel_id=1, source_target_pairs={{0,1},{1,0},{2,3},{3,2},{4,5},{5,4},{6,7},{7,6},{8,9},{9,8},{10,11... | collective-permute-start | bytes 786440 | tf_op jit(solution)/shard_map/ppermute | solution.py:1080
  31.3 21.9 %collective-permute-start.10 = (bf16[256,512]{1,0:T(8,128)(2,1)S(1)}, bf16[256,512]{1,0:T(8,128)(2,1)S(1)}, u32[]{:S(2)}, u32[]{:S(2)}) collective-permute-start(bf16[256,512]{1,0:T(8,128)(2,1)S(1)} %collective-permute-done.3.refs_6_.refs_10_), channel_id=1, source_target_pairs={{0,1},{1,0},{2,3},{3,2},{4,5},{5,4},{6,7},{7,6},{8,9},{9,8},{10,11... | collective-permute-start | bytes 786440 | tf_op jit(solution)/shard_map/ppermute | solution.py:1080
  31.3 21.9 %collective-permute-start.11 = (bf16[256,512]{1,0:T(8,128)(2,1)S(1)}, bf16[256,512]{1,0:T(8,128)(2,1)S(1)}, u32[]{:S(2)}, u32[]{:S(2)}) collective-permute-start(bf16[256,512]{1,0:T(8,128)(2,1)S(1)} %get-tuple-element.172.refs_5_.refs_9_), channel_id=1, source_target_pairs={{0,2},{1,3},{2,0},{3,1},{4,6},{5,7},{6,4},{7,5},{8,10},{9,11},{10,... | collective-permute-start | bytes 786440 | tf_op jit(solution)/shard_map/ppermute | solution.py:1080
  32.7 20.6 %collective-permute-start.8 = (bf16[528,512]{1,0:T(8,128)(2,1)S(1)}, bf16[528,512]{1,0:T(8,128)(2,1)S(1)}, u32[]{:S(2)}, u32[]{:S(2)}) collective-permute-start(bf16[528,512]{1,0:T(8,128)(2,1)S(1)} %concatenate.30.refs_0_.refs_4_), channel_id=1, source_target_pairs={{0,2},{1,3},{2,0},{3,1},{4,6},{5,7},{6,4},{7,5},{8,10},{9,11},{10,... | collective-permute-start | bytes 1622024 | tf_op jit(solution)/shard_map/ppermute | solution.py:1080
  63.2 8.8 %collective-permute-start.18 = (bf16[64,192]{1,0:T(8,128)(2,1)}, bf16[64,192]{1,0:T(8,128)(2,1)S(1)}, u32[]{:S(2)}, u32[]{:S(2)}) collective-permute-start(bf16[64,192]{1,0:T(8,128)(2,1)} %get-tuple-element.178), channel_id=1, source_target_pairs={{0,24},{1,25},{2,26},{3,27},{4,28},{5,29},{6,30},{7,31},{8,16},{9,... | collective-permute-start | bytes 73736 | tf_op jit(solution)/shard_map/ppermute | solution.py:1080
  66.6 5.4 %collective-permute-start.17 = (bf16[64,192]{1,0:T(8,128)(2,1)}, bf16[64,192]{1,0:T(8,128)(2,1)S(1)}, u32[]{:S(2)}, u32[]{:S(2)}) collective-permute-start(bf16[64,192]{1,0:T(8,128)(2,1)} %get-tuple-element.178), channel_id=1, source_target_pairs={{0,8},{1,9},{2,10},{3,11},{4,12},{5,13},{6,14},{7,15},{8,0},{9,1},... | collective-permute-start | bytes 73736 | tf_op jit(solution)/shard_map/ppermute | solution.py:1080
  66.6 5.4 %collective-permute-start.16 = (bf16[64,192]{1,0:T(8,128)(2,1)}, bf16[64,192]{1,0:T(8,128)(2,1)S(1)}, u32[]{:S(2)}, u32[]{:S(2)}) collective-permute-start(bf16[64,192]{1,0:T(8,128)(2,1)} %get-tuple-element.178), channel_id=1, source_target_pairs={{0,16},{1,17},{2,18},{3,19},{4,20},{5,21},{6,22},{7,23},{8,24},{9,... | collective-permute-start | bytes 73736 | tf_op jit(solution)/shard_map/ppermute | solution.py:1080
  72.0 5.2 %collective-permute-start.19 = (bf16[256,192]{1,0:T(8,128)(2,1)S(1)}, bf16[256,192]{1,0:T(8,128)(2,1)S(1)}, u32[]{:S(2)}, u32[]{:S(2)}) collective-permute-start(bf16[256,192]{1,0:T(8,128)(2,1)S(1)} %get-tuple-element.316), channel_id=1, source_target_pairs={{0,4},{1,5},{2,6},{3,7},{4,0},{5,1},{6,2},{7,3},{8,12},{9,13},{10,... | collective-permute-start | bytes 294920 | tf_op jit(solution)/shard_map/ppermute | solution.py:1080
  73.6 7.4 %collective-permute-start.21 = (bf16[256,192]{1,0:T(8,128)(2,1)S(1)}, bf16[256,192]{1,0:T(8,128)(2,1)S(1)}, u32[]{:S(2)}, u32[]{:S(2)}) collective-permute-start(bf16[256,192]{1,0:T(8,128)(2,1)S(1)} %get-tuple-element.316), channel_id=1, source_target_pairs={{0,6},{1,7},{2,4},{3,5},{4,2},{5,3},{6,0},{7,1},{8,14},{9,15},{10,... | collective-permute-start | bytes 294920 | tf_op jit(solution)/shard_map/ppermute | solution.py:1080
  75.0 6.0 %collective-permute-start.20 = (bf16[256,192]{1,0:T(8,128)(2,1)S(1)}, bf16[256,192]{1,0:T(8,128)(2,1)S(1)}, u32[]{:S(2)}, u32[]{:S(2)}) collective-permute-start(bf16[256,192]{1,0:T(8,128)(2,1)S(1)} %get-tuple-element.316), channel_id=1, source_target_pairs={{0,2},{1,3},{2,0},{3,1},{4,6},{5,7},{6,4},{7,5},{8,10},{9,11},{10,... | collective-permute-start | bytes 294920 | tf_op jit(solution)/shard_map/ppermute | solution.py:1080
  111.1 8.8 %collective-permute-start.26 = (bf16[256,192]{1,0:T(8,128)(2,1)S(1)}, bf16[256,192]{1,0:T(8,128)(2,1)S(1)}, u32[]{:S(2)}, u32[]{:S(2)}) collective-permute-start(bf16[256,192]{1,0:T(8,128)(2,1)S(1)} %get-tuple-element.302), channel_id=1, source_target_pairs={{0,6},{1,7},{2,4},{3,5},{4,2},{5,3},{6,0},{7,1},{8,14},{9,15},{10,... | collective-permute-start | bytes 294920 | tf_op jit(solution)/shard_map/ppermute | solution.py:1080
  112.7 7.7 %collective-permute-start.25 = (bf16[256,192]{1,0:T(8,128)(2,1)S(1)}, bf16[256,192]{1,0:T(8,128)(2,1)S(1)}, u32[]{:S(2)}, u32[]{:S(2)}) collective-permute-start(bf16[256,192]{1,0:T(8,128)(2,1)S(1)} %get-tuple-element.303), channel_id=1, source_target_pairs={{0,2},{1,3},{2,0},{3,1},{4,6},{5,7},{6,4},{7,5},{8,10},{9,11},{10,... | collective-permute-start | bytes 294920 | tf_op jit(solution)/shard_map/ppermute | solution.py:1080
  113.4 7.0 %collective-permute-start.24 = (bf16[256,192]{1,0:T(8,128)(2,1)S(1)}, bf16[256,192]{1,0:T(8,128)(2,1)S(1)}, u32[]{:S(2)}, u32[]{:S(2)}) collective-permute-start(bf16[256,192]{1,0:T(8,128)(2,1)S(1)} %get-tuple-element.304), channel_id=1, source_target_pairs={{0,4},{1,5},{2,6},{3,7},{4,0},{5,1},{6,2},{7,3},{8,12},{9,13},{10,... | collective-permute-start | bytes 294920 | tf_op jit(solution)/shard_map/ppermute | solution.py:1080
  120.5 9.7 %collective-permute-start.29 = (bf16[64,192]{1,0:T(8,128)(2,1)S(1)}, bf16[64,192]{1,0:T(8,128)(2,1)S(1)}, u32[]{:S(2)}, u32[]{:S(2)}) collective-permute-start(bf16[64,192]{1,0:T(8,128)(2,1)S(1)} %get-tuple-element.313), channel_id=1, source_target_pairs={{0,24},{1,25},{2,26},{3,27},{4,28},{5,29},{6,30},{7,31},{8,16},{9,... | collective-permute-start | bytes 73736 | tf_op jit(solution)/shard_map/ppermute | solution.py:1080
  122.1 8.1 %collective-permute-start.28 = (bf16[64,192]{1,0:T(8,128)(2,1)S(1)}, bf16[64,192]{1,0:T(8,128)(2,1)S(1)}, u32[]{:S(2)}, u32[]{:S(2)}) collective-permute-start(bf16[64,192]{1,0:T(8,128)(2,1)S(1)} %get-tuple-element.314), channel_id=1, source_target_pairs={{0,8},{1,9},{2,10},{3,11},{4,12},{5,13},{6,14},{7,15},{8,0},{9,1},... | collective-permute-start | bytes 73736 | tf_op jit(solution)/shard_map/ppermute | solution.py:1080
  122.5 7.7 %collective-permute-start.27 = (bf16[64,192]{1,0:T(8,128)(2,1)S(1)}, bf16[64,192]{1,0:T(8,128)(2,1)S(1)}, u32[]{:S(2)}, u32[]{:S(2)}) collective-permute-start(bf16[64,192]{1,0:T(8,128)(2,1)S(1)} %get-tuple-element.315), channel_id=1, source_target_pairs={{0,16},{1,17},{2,18},{3,19},{4,20},{5,21},{6,22},{7,23},{8,24},{9,... | collective-permute-start | bytes 73736 | tf_op jit(solution)/shard_map/ppermute | solution.py:1080
  137.7 9.7 %collective-permute-start.32 = (bf16[64,1024]{1,0:T(8,128)(2,1)}, bf16[64,1024]{1,0:T(8,128)(2,1)S(1)}, u32[]{:S(2)}, u32[]{:S(2)}) collective-permute-start(bf16[64,1024]{1,0:T(8,128)(2,1)} %get-tuple-element.219), channel_id=1, source_target_pairs={{0,24},{1,25},{2,26},{3,27},{4,28},{5,29},{6,30},{7,31},{8,16},{9,... | collective-permute-start | bytes 393224 | tf_op jit(solution)/shard_map/ppermute | solution.py:1080
  139.2 8.4 %collective-permute-start.31 = (bf16[64,1024]{1,0:T(8,128)(2,1)}, bf16[64,1024]{1,0:T(8,128)(2,1)S(1)}, u32[]{:S(2)}, u32[]{:S(2)}) collective-permute-start(bf16[64,1024]{1,0:T(8,128)(2,1)} %get-tuple-element.219), channel_id=1, source_target_pairs={{0,8},{1,9},{2,10},{3,11},{4,12},{5,13},{6,14},{7,15},{8,0},{9,1},... | collective-permute-start | bytes 393224 | tf_op jit(solution)/shard_map/ppermute | solution.py:1080
  139.2 12.1 %collective-permute-start.30 = (bf16[64,1024]{1,0:T(8,128)(2,1)}, bf16[64,1024]{1,0:T(8,128)(2,1)S(1)}, u32[]{:S(2)}, u32[]{:S(2)}) collective-permute-start(bf16[64,1024]{1,0:T(8,128)(2,1)} %get-tuple-element.219), channel_id=1, source_target_pairs={{0,16},{1,17},{2,18},{3,19},{4,20},{5,21},{6,22},{7,23},{8,24},{9,... | collective-permute-start | bytes 393224 | tf_op jit(solution)/shard_map/ppermute | solution.py:1080
  151.4 29.3 %collective-permute-start.35 = (bf16[256,1024]{1,0:T(8,128)(2,1)S(1)}, bf16[256,1024]{1,0:T(8,128)(2,1)S(1)}, u32[]{:S(2)}, u32[]{:S(2)}) collective-permute-start(bf16[256,1024]{1,0:T(8,128)(2,1)S(1)} %pad_maximum_fusion.2), channel_id=1, source_target_pairs={{0,6},{1,7},{2,4},{3,5},{4,2},{5,3},{6,0},{7,1},{8,14},{9,15},{10,... | collective-permute-start | bytes 1572872 | tf_op jit(solution)/shard_map/ppermute | solution.py:1080
  153.0 27.7 %collective-permute-start.34 = (bf16[256,1024]{1,0:T(8,128)(2,1)S(1)}, bf16[256,1024]{1,0:T(8,128)(2,1)S(1)}, u32[]{:S(2)}, u32[]{:S(2)}) collective-permute-start(bf16[256,1024]{1,0:T(8,128)(2,1)S(1)} %pad_maximum_fusion.2), channel_id=1, source_target_pairs={{0,2},{1,3},{2,0},{3,1},{4,6},{5,7},{6,4},{7,5},{8,10},{9,11},{10,... | collective-permute-start | bytes 1572872 | tf_op jit(solution)/shard_map/ppermute | solution.py:1080
  153.7 27.0 %collective-permute-start.33 = (bf16[256,1024]{1,0:T(8,128)(2,1)S(1)}, bf16[256,1024]{1,0:T(8,128)(2,1)S(1)}, u32[]{:S(2)}, u32[]{:S(2)}) collective-permute-start(bf16[256,1024]{1,0:T(8,128)(2,1)S(1)} %pad_maximum_fusion.2), channel_id=1, source_target_pairs={{0,4},{1,5},{2,6},{3,7},{4,0},{5,1},{6,2},{7,3},{8,12},{9,13},{10,... | collective-permute-start | bytes 1572872 | tf_op jit(solution)/shard_map/ppermute | solution.py:1080
  186.5 7.2 %collective-permute-start.41 = (bf16[1024,1024]{1,0:T(8,128)(2,1)S(1)}, bf16[1024,1024]{1,0:T(8,128)(2,1)S(1)}, u32[]{:S(2)}, u32[]{:S(2)}) collective-permute-start(bf16[1024,1024]{1,0:T(8,128)(2,1)S(1)} %pad_maximum_fusion.first), channel_id=1, source_target_pairs={{0,1},{1,0},{2,3},{3,2},{4,5},{5,4},{6,7},{7,6},{8,9},{9,8},{10,11... | collective-permute-start | bytes 6291464 | tf_op jit(solution)/shard_map/ppermute | solution.py:1080
  186.7 5.5 %collective-permute-start.40 = (bf16[256,16,128]{2,1,0:T(8,128)(2,1)S(1)}, bf16[256,16,128]{2,1,0:T(8,128)(2,1)S(1)}, u32[]{:S(2)}, u32[]{:S(2)}) collective-permute-start(bf16[256,16,128]{2,1,0:T(8,128)(2,1)S(1)} %bitcast.66), channel_id=1, source_target_pairs={{0,1},{1,0},{2,3},{3,2},{4,5},{5,4},{6,7},{7,6},{8,9},{9,8},{10,11... | collective-permute-start | bytes 3145736 | tf_op jit(solution)/shard_map/ppermute | solution.py:1080
  188.3 15.9 %collective-permute-start.39 = (bf16[96,16,128]{2,1,0:T(8,128)(2,1)}, bf16[96,16,128]{2,1,0:T(8,128)(2,1)S(1)}, u32[]{:S(2)}, u32[]{:S(2)}) collective-permute-start(bf16[96,16,128]{2,1,0:T(8,128)(2,1)} %get-tuple-element.296), channel_id=1, source_target_pairs={{0,6},{1,7},{2,4},{3,5},{4,2},{5,3},{6,0},{7,1},{8,14},{9,15},{10,... | collective-permute-start | bytes 1179656 | tf_op jit(solution)/shard_map/ppermute | solution.py:1080
  189.9 19.1 %collective-permute-start.38 = (bf16[96,16,128]{2,1,0:T(8,128)(2,1)}, bf16[96,16,128]{2,1,0:T(8,128)(2,1)S(1)}, u32[]{:S(2)}, u32[]{:S(2)}) collective-permute-start(bf16[96,16,128]{2,1,0:T(8,128)(2,1)} %get-tuple-element.297), channel_id=1, source_target_pairs={{0,2},{1,3},{2,0},{3,1},{4,6},{5,7},{6,4},{7,5},{8,10},{9,11},{10,... | collective-permute-start | bytes 1179656 | tf_op jit(solution)/shard_map/ppermute | solution.py:1080
  190.6 18.4 %collective-permute-start.37 = (bf16[96,16,128]{2,1,0:T(8,128)(2,1)}, bf16[96,16,128]{2,1,0:T(8,128)(2,1)}, u32[]{:S(2)}, u32[]{:S(2)}) collective-permute-start(bf16[96,16,128]{2,1,0:T(8,128)(2,1)} %get-tuple-element.298), channel_id=1, source_target_pairs={{0,4},{1,5},{2,6},{3,7},{4,0},{5,1},{6,2},{7,3},{8,12},{9,13},{10,... | collective-permute-start | bytes 1179656 | tf_op jit(solution)/shard_map/ppermute | solution.py:1080
  210.2 8.8 %collective-permute-start.42 = (bf16[24,16,128]{2,1,0:T(8,128)(2,1)S(1)}, bf16[24,16,128]{2,1,0:T(8,128)(2,1)S(1)}, u32[]{:S(2)}, u32[]{:S(2)}) collective-permute-start(bf16[24,16,128]{2,1,0:T(8,128)(2,1)S(1)} %get-tuple-element.307), channel_id=1, source_target_pairs={{0,16},{1,17},{2,18},{3,19},{4,20},{5,21},{6,22},{7,23},{8,24},{9,... | collective-permute-start | bytes 294920 | tf_op jit(solution)/shard_map/ppermute | solution.py:1080
  210.3 10.3 %collective-permute-start.44 = (bf16[24,16,128]{2,1,0:T(8,128)(2,1)S(1)}, bf16[24,16,128]{2,1,0:T(8,128)(2,1)S(1)}, u32[]{:S(2)}, u32[]{:S(2)}) collective-permute-start(bf16[24,16,128]{2,1,0:T(8,128)(2,1)S(1)} %get-tuple-element.308), channel_id=1, source_target_pairs={{0,24},{1,25},{2,26},{3,27},{4,28},{5,29},{6,30},{7,31},{8,16},{9,... | collective-permute-start | bytes 294920 | tf_op jit(solution)/shard_map/ppermute | solution.py:1080
  211.9 8.7 %collective-permute-start.43 = (bf16[24,16,128]{2,1,0:T(8,128)(2,1)S(1)}, bf16[24,16,128]{2,1,0:T(8,128)(2,1)S(1)}, u32[]{:S(2)}, u32[]{:S(2)}) collective-permute-start(bf16[24,16,128]{2,1,0:T(8,128)(2,1)S(1)} %get-tuple-element.309), channel_id=1, source_target_pairs={{0,8},{1,9},{2,10},{3,11},{4,12},{5,13},{6,14},{7,15},{8,0},{9,1},... | collective-permute-start | bytes 294920 | tf_op jit(solution)/shard_map/ppermute | solution.py:1080
  213.9 7.5 %collective-permute-start.46 = (bf16[64,16,128]{2,1,0:T(8,128)(2,1)S(1)}, bf16[64,16,128]{2,1,0:T(8,128)(2,1)S(1)}, u32[]{:S(2)}, u32[]{:S(2)}) collective-permute-start(bf16[64,16,128]{2,1,0:T(8,128)(2,1)S(1)} %get-tuple-element.300), channel_id=1, source_target_pairs={{0,2},{1,3},{2,0},{3,1},{4,6},{5,7},{6,4},{7,5},{8,10},{9,11},{10,... | collective-permute-start | bytes 786440 | tf_op jit(solution)/shard_map/ppermute | solution.py:1080
  214.7 7.3 %collective-permute-start.45 = (bf16[64,16,128]{2,1,0:T(8,128)(2,1)S(1)}, bf16[64,16,128]{2,1,0:T(8,128)(2,1)S(1)}, u32[]{:S(2)}, u32[]{:S(2)}) collective-permute-start(bf16[64,16,128]{2,1,0:T(8,128)(2,1)S(1)} %get-tuple-element.301), channel_id=1, source_target_pairs={{0,4},{1,5},{2,6},{3,7},{4,0},{5,1},{6,2},{7,3},{8,12},{9,13},{10,... | collective-permute-start | bytes 786440 | tf_op jit(solution)/shard_map/ppermute | solution.py:1080
  219.0 13.6 %collective-permute-start.50 = (bf16[64,16,128]{2,1,0:T(8,128)(2,1)S(1)}, bf16[64,16,128]{2,1,0:T(8,128)(2,1)S(1)}, u32[]{:S(2)}, u32[]{:S(2)}) collective-permute-start(bf16[64,16,128]{2,1,0:T(8,128)(2,1)S(1)} %get-tuple-element.299), channel_id=1, source_target_pairs={{0,6},{1,7},{2,4},{3,5},{4,2},{5,3},{6,0},{7,1},{8,14},{9,15},{10,... | collective-permute-start | bytes 786440 | tf_op jit(solution)/shard_map/ppermute | solution.py:1080
  221.9 7.5 %collective-permute-start.49 = (bf16[24,16,128]{2,1,0:T(8,128)(2,1)S(1)}, bf16[24,16,128]{2,1,0:T(8,128)(2,1)S(1)}, u32[]{:S(2)}, u32[]{:S(2)}) collective-permute-start(bf16[24,16,128]{2,1,0:T(8,128)(2,1)S(1)} %fusion.2), channel_id=1, source_target_pairs={{0,24},{1,25},{2,26},{3,27},{4,28},{5,29},{6,30},{7,31},{8,16},{9,... | collective-permute-start | bytes 294920 | tf_op jit(solution)/shard_map/ppermute | solution.py:1080
  223.2 6.7 %collective-permute-start.48 = (bf16[24,16,128]{2,1,0:T(8,128)(2,1)S(1)}, bf16[24,16,128]{2,1,0:T(8,128)(2,1)S(1)}, u32[]{:S(2)}, u32[]{:S(2)}) collective-permute-start(bf16[24,16,128]{2,1,0:T(8,128)(2,1)S(1)} %fusion.2), channel_id=1, source_target_pairs={{0,8},{1,9},{2,10},{3,11},{4,12},{5,13},{6,14},{7,15},{8,0},{9,1},... | collective-permute-start | bytes 294920 | tf_op jit(solution)/shard_map/ppermute | solution.py:1080
  225.5 7.1 %collective-permute-start.47 = (bf16[24,16,128]{2,1,0:T(8,128)(2,1)S(1)}, bf16[24,16,128]{2,1,0:T(8,128)(2,1)S(1)}, u32[]{:S(2)}, u32[]{:S(2)}) collective-permute-start(bf16[24,16,128]{2,1,0:T(8,128)(2,1)S(1)} %fusion.2), channel_id=1, source_target_pairs={{0,16},{1,17},{2,18},{3,19},{4,20},{5,21},{6,22},{7,23},{8,24},{9,... | collective-permute-start | bytes 294920 | tf_op jit(solution)/shard_map/ppermute | solution.py:1080
  232.6 19.6 %collective-permute-start.53 = (bf16[96,16,128]{2,1,0:T(8,128)(2,1)S(1)}, bf16[96,16,128]{2,1,0:T(8,128)(2,1)S(1)}, u32[]{:S(2)}, u32[]{:S(2)}) collective-permute-start(bf16[96,16,128]{2,1,0:T(8,128)(2,1)S(1)} %pad_maximum_fusion.3), channel_id=1, source_target_pairs={{0,6},{1,7},{2,4},{3,5},{4,2},{5,3},{6,0},{7,1},{8,14},{9,15},{10,... | collective-permute-start | bytes 1179656 | tf_op jit(solution)/shard_map/ppermute | solution.py:1080
  234.2 17.9 %collective-permute-start.52 = (bf16[96,16,128]{2,1,0:T(8,128)(2,1)S(1)}, bf16[96,16,128]{2,1,0:T(8,128)(2,1)S(1)}, u32[]{:S(2)}, u32[]{:S(2)}) collective-permute-start(bf16[96,16,128]{2,1,0:T(8,128)(2,1)S(1)} %pad_maximum_fusion.3), channel_id=1, source_target_pairs={{0,2},{1,3},{2,0},{3,1},{4,6},{5,7},{6,4},{7,5},{8,10},{9,11},{10,... | collective-permute-start | bytes 1179656 | tf_op jit(solution)/shard_map/ppermute | solution.py:1080
  235.0 17.1 %collective-permute-start.51 = (bf16[96,16,128]{2,1,0:T(8,128)(2,1)S(1)}, bf16[96,16,128]{2,1,0:T(8,128)(2,1)S(1)}, u32[]{:S(2)}, u32[]{:S(2)}) collective-permute-start(bf16[96,16,128]{2,1,0:T(8,128)(2,1)S(1)} %pad_maximum_fusion.3), channel_id=1, source_target_pairs={{0,4},{1,5},{2,6},{3,7},{4,0},{5,1},{6,2},{7,3},{8,12},{9,13},{10,... | collective-permute-start | bytes 1179656 | tf_op jit(solution)/shard_map/ppermute | solution.py:1080
  237.1 6.3 %collective-permute-start.56 = (bf16[16,16,128]{2,1,0:T(8,128)(2,1)S(1)}, bf16[16,16,128]{2,1,0:T(8,128)(2,1)S(1)}, u32[]{:S(2)}, u32[]{:S(2)}) collective-permute-start(bf16[16,16,128]{2,1,0:T(8,128)(2,1)S(1)} %get-tuple-element.310), channel_id=1, source_target_pairs={{0,24},{1,25},{2,26},{3,27},{4,28},{5,29},{6,30},{7,31},{8,16},{9,... | collective-permute-start | bytes 196616 | tf_op jit(solution)/shard_map/ppermute | solution.py:1080
  243.4 5.2 %collective-permute-start.54 = (bf16[16,16,128]{2,1,0:T(8,128)(2,1)S(1)}, bf16[16,16,128]{2,1,0:T(8,128)(2,1)S(1)}, u32[]{:S(2)}, u32[]{:S(2)}) collective-permute-start(bf16[16,16,128]{2,1,0:T(8,128)(2,1)S(1)} %get-tuple-element.312), channel_id=1, source_target_pairs={{0,16},{1,17},{2,18},{3,19},{4,20},{5,21},{6,22},{7,23},{8,24},{9,... | collective-permute-start | bytes 196616 | tf_op jit(solution)/shard_map/ppermute | solution.py:1080
  (45 other events, 313.0 us)

commit v2 on v1

--- a/solution.py
+++ b/solution.py
@@ -685,8 +685,6 @@
         (width, width),
         (edge_width, width),
         (edge_width, width),
-        (edge_width, edge_width),
-        (edge_width, edge_width),
         (16, width),
         (16, edge_width),
     ]
@@ -694,7 +692,7 @@
 
 def residue_backward_kernel(
     parts, pieces, node_cot, own_sum, e_first, e_far, h1b, h2b, n1, sc1, n2, sc2, slope, g1, g2, m3,
-    total, e2g, e3g, eb2, eb3, edge_gain, *refs,
+    total, edge_gain, *refs,
 ):
     far = refs[:pieces]
     f1 = refs[pieces : pieces + parts]
@@ -731,10 +729,8 @@
             dot_rows(total[...].astype(BF16), g_u1.astype(BF16)),
             dot_rows(own.astype(BF16), h2b[...]),
             dot_rows(far_sum.astype(BF16), h2b[...]),
-            e2g[...],
-            e3g[...],
             padded_rows(bias, width),
-            padded_rows([eb2[...], eb3[...], edge_gain[...]], own.shape[1]),
+            padded_rows([edge_gain[...]], own.shape[1]),
         ],
     )
 
@@ -803,6 +799,8 @@
         (16, width),
         (width, width),
         (edge_width, edge_width),
+        (edge_width, edge_width),
+        (edge_width, edge_width),
         (16, edge_width),
     ]
 
@@ -813,7 +811,8 @@
 
 def message_backward_kernel(
     sb, blocks, groups, at_once, codes, base, order, v, a1, s1, s2, edge, low_three, low_edge, local_row, live_col,
-    m1, m2, e_first, node_lo, node_hi, node, early, e1g, eb1,
+    m1, m2, e_first, node_lo, node_hi, node, early,
+    e1g, e2g, e3g, eb1, eb2, eb3,
     edge_grad, far_keep, far_send, own, keep, send,
     low_two, low_one, grad, rows_ref, moved, m2g, m1eg, m1fg, b2s, slab,
 ):
@@ -905,7 +904,9 @@
                 padded_rows([column_sum(own[...]), column_sum(b2s[...])], width),
                 m1fg[...],
                 e1g[...],
-                padded_rows([eb1[...]], edge_width),
+                e2g[...],
+                e3g[...],
+                padded_rows([eb1[...], eb2[...], eb3[...]], edge_width),
             ],
             count,
         )
@@ -914,7 +915,7 @@
 
 def message_backward(
     groups, codes, base, order, v, a1, s1, s2, edge, low_three, low_edge, local_row, live_col, m1, m2,
-    e_first, node_lo, node_hi, node, early, e1g, eb1,
+    e_first, node_lo, node_hi, node, early, edge_grads,
 ):
     slots, rows, edge_width = edge.shape
     width = v.shape[1]
@@ -959,9 +960,8 @@
             node_spec,
             const_spec(node.shape),
             const_spec(early.shape),
-            const_spec(e1g.shape),
-            const_spec(eb1.shape),
-        ],
+        ]
+        + [const_spec(a.shape) for a in edge_grads],
         out_specs=[slot_spec, far_spec, far_spec, pl.BlockSpec((rows, width), whole), slab_spec, slab_spec],
         out_shape=[
             jax.ShapeDtypeStruct((slots, rows, edge_width), F32),
@@ -992,7 +992,7 @@
         ),
     )(
         base, order, v, a1, s1, s2, edge, low_three, low_edge, local_row, live_col, m1, m2, e_first,
-        node_lo, node_hi, node, early, e1g, eb1,
+        node_lo, node_hi, node, early, *edge_grads,
     )
 
 
@@ -1034,7 +1034,7 @@
     starts = [all_tiles(shapes[:at]) for at in range(len(shapes))]
     m3g[...] = unpack(slab, starts[0], width, width)
     e1g[:, :width] = unpack(slab, starts[1], edge_width, width)
-    middle = unpack(slab, starts[12], edge_width, edge_width)
+    middle = unpack(slab, starts[10], edge_width, edge_width)
     far = unpack(slab, starts[2], edge_width, width)
     over = edge_width % LANES
     base_col = width + edge_width - over
@@ -1046,22 +1046,22 @@
     )
     rest = e1g.shape[1] - base_col - LANES
     e1g[:, base_col + LANES :] = far[:, LANES : LANES + rest]
-    e2g[...] = unpack(slab, starts[3], edge_width, edge_width)[:, :edge_width]
-    e3g[...] = unpack(slab, starts[4], edge_width, edge_width)[:, :edge_width]
-    bias = unpack(slab, starts[5], 16, width)
+    bias = unpack(slab, starts[3], 16, width)
     for row, out in enumerate((g1, g2, fb2, b3)):
         out[...] = bias[row : row + 1]
-    bias = unpack(slab, starts[6], 16, edge_width)
-    for row, out in enumerate((eb2, eb3, g3)):
-        out[...] = bias[row : row + 1, :edge_width]
-    m1g[:width, :] = unpack(slab, starts[7], width, width)
-    m2g[...] = unpack(slab, starts[8], width, width)
-    m1g[width : width + edge_width, :] = unpack(slab, starts[9], edge_width, width)
-    bias = unpack(slab, starts[10], 16, width)
+    g3[...] = unpack(slab, starts[4], 16, edge_width)[:1, :edge_width]
+    m1g[:width, :] = unpack(slab, starts[5], width, width)
+    m2g[...] = unpack(slab, starts[6], width, width)
+    m1g[width : width + edge_width, :] = unpack(slab, starts[7], edge_width, width)
+    bias = unpack(slab, starts[8], 16, width)
     b1[...] = bias[0:1]
     b2[...] = bias[1:2]
-    eb1[...] = unpack(slab, starts[13], 16, edge_width)[:1, :edge_width]
-    m1g[width + edge_width :, :] = unpack(slab, starts[11], width, width)
+    m1g[width + edge_width :, :] = unpack(slab, starts[9], width, width)
+    e2g[...] = unpack(slab, starts[11], edge_width, edge_width)[:, :edge_width]
+    e3g[...] = unpack(slab, starts[12], edge_width, edge_width)[:, :edge_width]
+    bias = unpack(slab, starts[13], 16, edge_width)
+    for row, out in enumerate((eb1, eb2, eb3)):
+        out[...] = bias[row : row + 1, :edge_width]
 
 
 def weights_out(codes, base, halves_in, width, edge_width):
@@ -1238,34 +1238,25 @@
     )
 
     terms = [lo, exchange(hi, near[0], devices)]
-    pairs, made = [(act_two, low_three), (act_one, low_two)], []
     for group in reversed(outer):
-        total_far = add_up(terms)
-        if pairs:
-            left, right = pairs.pop(0)
-            total_far, left = tied(total_far, left)
-        terms = shared_out(total_far, group, devices)
-        if len(made) < 2:
-            terms, got = tied(terms, edge_weights((left,), (right,), rows))
-            made.append(got)
-    (e3g, eb3), (e2g, eb2) = made
+        terms = shared_out(add_up(terms), group, devices)
     g_u1, v, both, early = residue_backward(
         (
             node_cotangent, own_sum, e_first, e_far, h1b, h2b, n1, sc1, n2, sc2, slope, row(norm_one),
-            row(norm_two), message_third, total, e2g, e3g, eb2, eb3, edge_gain,
+            row(norm_two), message_third, total, edge_gain,
         ),
         terms, f1, f2,
     )
 
     both, low_here = tied(both, low_one)
     b_held = stack(sent_around(both, outer[0], devices))
-    e1g, eb1 = edge_weights((low_here,), (edge,), rows)
-    v, b_held, e1g, eb1 = tied(v, b_held, e1g, eb1)
+    edge_grads = edge_weights((low_here, act_one, act_two), (edge, low_two, low_three), rows)
+    v, b_held, edge_grads = tied(v, b_held, edge_grads)
     for group in outer[1:]:
         b_held = stack(sent_around(b_held, group, devices))
     edge_grad, far_keep, far_send, own, keep, send = message_backward(
         res_count, codes, base, edge_order, v, a1, s1, s2, edge, low_three, low_one, local_row, live_col,
-        message_first, message_second, e_first, node_lo, node_hi, node_in, early, e1g, eb1,
+        message_first, message_second, e_first, node_lo, node_hi, node_in, early, edge_grads,
     )
     keep, send, far_keep, far_send, b_held = tied(keep, send, far_keep, far_send, b_held)
 

time: 263 us -> 261 us (level)
  Pallas kernels: 118 us -> 110 us
  waiting for transfers between devices: 55.6 us -> 61.3 us
    pallas_call x3 -> x1, Pallas kernels: 15.7 us -> 7.66 us  [edge_weights(): pl.pallas_call(functools.partial(edge_weights_kernel, slots // sb, pairs)...]
    ppermute x58, waiting for transfers between devices: 55.6 us -> 61.3 us  [exchange(): return lax.ppermute(value, AXES, [(d, d ^ mask) for d in range(devices)])]
    unnamed x79 -> x77, local copies, waits for them, and re-layouts: 10.6 us -> 10.6 us
  transfers between devices with their start and end apart: 58 -> 58, of which waited for: 25 -> 28; matrix products, arithmetic and copies ran while one was open for 5% -> 5% of each run, Pallas kernels for 30% -> 27%
where the time goes in v2:
time: 261 us; the launch traced here: 260 us
  Pallas kernels  110 us (42%)
  waiting for transfers between devices  61.3 us (23%)
  starting transfers between devices  60.4 us (23%)
  local copies, waits for them, and re-layouts  17.5 us (7%)
  other arithmetic  9.73 us (4%)
    ppermute x58, waiting for transfers between devices, exchange(): return lax.ppermute(value, AXES, [(d, d ^ mask) for d in range(devices)])  61.3 us
    ppermute x58, starting transfers between devices, exchange(): return lax.ppermute(value, AXES, [(d, d ^ mask) for d in range(devices)])  60.4 us
    pallas_call x1, Pallas kernels, message_backward(): pl.pallas_call(functools.partial(message_backward_kernel, sb, blocks, gro...  25.7 us
    pallas_call x5, Pallas kernels, small_call(): pl.pallas_call(kernel, grid=(1,), in_specs=[pl.BlockSpec(memory_space=plt...  24.5 us
    pallas_call x1, Pallas kernels, edge_branch(): pl.pallas_call(functools.partial(edge_kernel, sb, blocks, hi_chunks, by_r...  24 us
    pallas_call x1, Pallas kernels, message_forward(): pl.pallas_call(functools.partial(message_forward_kernel, sb, by_rows), gr...  18.9 us
    unnamed x77, local copies, waits for them, and re-layouts  10.6 us
    pallas_call x1, Pallas kernels, feed_gradients(): pl.pallas_call(feed_kernel, grid=(half // chunk,), in_specs=[pl.BlockSpec...  9.23 us
  transfers between devices with their start and end apart: 58, of which 28 were waited for; matrix products, arithmetic and copies ran while one was open for 5% of the time, Pallas kernels for 27%

profile of v2, /device:TPU:0, one launch (start us, length us, event | category | flops | bytes accessed | tf_op | source)
XLA Modules:
  0.0 260.4 jit_solution(4180373532246605049)
XLA Ops:
  0.7 5.1 %collective-permute-start.2 = (bf16[64,512]{1,0:T(8,128)(2,1)}, bf16[64,512]{1,0:T(8,128)(2,1)S(1)}, u32[]{:S(2)}, u32[]{:S(2)}) collective-permute-start(bf16[64,512]{1,0:T(8,128)(2,1)} %node.3), channel_id=1, source_target_pairs={{0,24},{1,25},{2,26},{3,27},{4,28},{5,29},{6,30},{7,31},{8,16},{9,... | collective-permute-start | bytes 196616 | tf_op jit(solution)/shard_map/ppermute | solution.py:1080
  7.5 1.7 collective-permute-start.3
  13.4 1.7 collective-permute-done.3.refs_6_.refs_10_
  15.1 2.4 collective-permute-start.6
  19.2 4.8 %group_order.1 = s32[30,128]{1,0:T(8,128)} custom-call(s32[32,128]{1,0:T(8,128)} %pad_bitcast_fusion.names), custom_call_target="tpu_custom_call" | custom-call | tf_op jit(solution)/shard_map/group_order/pallas_call | solution.py:180
  25.7 2.5 collective-permute-done.5
  29.1 1.7 slice.118.e_far
  34.3 18.9 %message_forward.1 = (bf16[3840,512]{1,0:T(8,128)(2,1)}, bf16[3840,512]{1,0:T(8,128)(2,1)}, bf16[3840,512]{1,0:T(8,128)(2,1)}, f32[64,512]{1,0:T(8,128)}) custom-call(bf16[1024,512]{1,0:T(8,128)(2,1)} %copy-done.17, bf16[1024,512]{1,0:T(8,128)(2,1)} %copy-done.31, bf16[64,512]{1,0:T(8,128)(2,1)} %node.3, bf16[60,64,192]{2,1,0:T(8,128)(2,1)} %bitcast.48, ...), custom_call_target="tpu_custom_call" | custom-call | flops 10821304320 | bytes 15237120 | tf_op jit(solution)/shard_map/message_forward/pallas_call | solution.py:364
  54.4 2.1 collective-permute-done.14.refs_9_.refs_13_
  58.0 5.3 %residue_forward.1 = (bf16[64,512]{1,0:T(8,128)(2,1)}, f32[64,512]{1,0:T(8,128)}, f32[64,128]{1,0:T(8,128)}, f32[64,512]{1,0:T(8,128)}, f32[64,128]{1,0:T(8,128)...) custom-call(bf16[64,512]{1,0:T(8,128)(2,1)} %node.3, ...), custom_call_target="tpu_custom_call" | custom-call | flops 268435456 | bytes 5242880 | tf_op jit(solution)/shard_map/residue_forward/pallas_call | solution.py:180
  63.3 3.3 %collective-permute-start.18 = (bf16[64,192]{1,0:T(8,128)(2,1)}, bf16[64,192]{1,0:T(8,128)(2,1)S(1)}, u32[]{:S(2)}, u32[]{:S(2)}) collective-permute-start(bf16[64,192]{1,0:T(8,128)(2,1)} %get-tuple-element.166), channel_id=1, source_target_pairs={{0,24},{1,25},{2,26},{3,27},{4,28},{5,29},{6,30},{7,31},{8,16},{9,... | collective-permute-start | bytes 73736 | tf_op jit(solution)/shard_map/ppermute | solution.py:1080
  68.6 3.5 %collective-permute-done.16 = bf16[64,192]{1,0:T(8,128)(2,1)S(1)} collective-permute-done((bf16[64,192]{1,0:T(8,128)(2,1)}, bf16[64,192]{1,0:T(8,128)(2,1)S(1)}, u32[]{:S(2)}, u32[]{:S(2)}) %collective-permute-start.16) | collective-permute-done | bytes 24608 | tf_op jit(solution)/shard_map/ppermute | solution.py:1080
  72.1 1.6 collective-permute-start.19
  73.6 1.4 collective-permute-start.21
  75.6 1.7 collective-permute-done.19
  77.3 3.7 %collective-permute-done.20 = bf16[256,192]{1,0:T(8,128)(2,1)S(1)} collective-permute-done((bf16[256,192]{1,0:T(8,128)(2,1)S(1)}, bf16[256,192]{1,0:T(8,128)(2,1)S(1)}, u32[]{:S(2)}, u32[]{:S(2)}) %collective-permute-start.20) | collective-permute-done | bytes 98336 | tf_op jit(solution)/shard_map/ppermute | solution.py:1080
  81.1 1.9 collective-permute-done.22.far_hi
  83.8 24.0 %edge_branch.1 = (bf16[60,64,192]{2,1,0:T(8,128)(2,1)}, bf16[3840,192]{1,0:T(8,128)(2,1)}, bf16[3840,192]{1,0:T(8,128)(2,1)}, bf16[3840,192]{1,0:T(8,128)(2,1)},...) custom-call(bf16[1024,192]{1,0:T(8,128)(2,1)} %copy-done.27, ...), custom_call_target="tpu_custom_call" | custom-call | flops 7455375360 | bytes 11796480 | tf_op jit(solution)/shard_map/edge_branch/pallas_call | solution.py:577
  108.0 2.0 collective-permute-done.23
  113.5 1.4 collective-permute-start.25
  114.9 2.9 %collective-permute-done.24 = bf16[256,192]{1,0:T(8,128)(2,1)S(1)} collective-permute-done((bf16[256,192]{1,0:T(8,128)(2,1)S(1)}, bf16[256,192]{1,0:T(8,128)(2,1)S(1)}, u32[]{:S(2)}, u32[]{:S(2)}) %collective-permute-start.24) | collective-permute-done | bytes 98336 | tf_op jit(solution)/shard_map/ppermute | solution.py:1080
  117.8 2.2 collective-permute-done.26
  122.1 1.5 collective-permute-start.29
  124.0 2.5 collective-permute-start.27
  129.4 6.6 %residue_backward.1 = (f32[64,512]{1,0:T(8,128)}, f32[64,512]{1,0:T(8,128)}, bf16[64,1024]{1,0:T(8,128)(2,1)}, bf16[230,16,128]{2,1,0:T(8,128)(2,1)}) custom-call(bf16[64,512]{1,0:T(8,128)(2,1)} %node_cot.1, f32[64,192]{1,0:T(8,128)} %get-tuple-element.170.own_sum, bf16[192,1216]{1,0:T(8,128)(2,1)} %bitcast.46, bf16[192,512]{1,0:T(8,128)(2,1)} %slice.118.e_far, ...), custom_call_target="tpu_custom_call" | custom-call | flops 268435456 | bytes 8388608 | tf_op jit(solution)/shard_map/residue_backward/pallas_call | solution.py:180
  136.0 2.9 %collective-permute-start.32 = (bf16[64,1024]{1,0:T(8,128)(2,1)}, bf16[64,1024]{1,0:T(8,128)(2,1)S(1)}, u32[]{:S(2)}, u32[]{:S(2)}) collective-permute-start(bf16[64,1024]{1,0:T(8,128)(2,1)} %get-tuple-element.183), channel_id=1, source_target_pairs={{0,24},{1,25},{2,26},{3,27},{4,28},{5,29},{6,30},{7,31},{8,16},{9,... | collective-permute-start | bytes 393224 | tf_op jit(solution)/shard_map/ppermute | solution.py:1080
  140.5 7.7 %edge_weights.1 = (f32[192,192]{1,0:T(8,128)}, f32[192,192]{1,0:T(8,128)}, f32[192,192]{1,0:T(8,128)}, f32[1,192]{1,0:T(1,128)}, f32[1,192]{1,0:T(1,128)}, /*index=5*/f32[1,192]{1,0:T(1,128)}) custom-call(bf16[3840,192]{1,0:T(8,128)(2,1)} %get-tuple-element.184.refs_0_.low_edge, bf16[3840,192]{1,0:T(8,128)(2,1)} %get-tuple-element.185.refs_1_, ...), custom_call_target="tpu_custom_call" | custom-call | flops 849346560 | bytes 8847360 | tf_op jit(solution)/shard_map/edge_weights/pallas_call | solution.py:666
  148.7 1.8 collective-permute-start.35
  152.3 25.7 %message_backward.1 = (f32[60,64,192]{2,1,0:T(8,128)}, bf16[2,8,16,16,128]{4,3,2,1,0:T(8,128)(2,1)}, bf16[2,8,16,16,128]{4,3,2,1,0:T(8,128)(2,1)}, f32[64,512]{1...) custom-call(s32[1]{0:T(128)} %bitcast.16.base, s32[1,3840]{1,0:T(1,128)} %bitcast.55, ...), custom_call_target="tpu_custom_call" | custom-call | flops 6794772480 | bytes 19169280 | tf_op jit(solution)/shard_map/message_backward/pallas_call | solution.py:941
  178.3 1.7 copy-done.30
  180.0 3.4 %collective-permute-done.36 = bf16[384,16,128]{2,1,0:T(8,128)(2,1)S(1)} collective-permute-done((bf16[384,16,128]{2,1,0:T(8,128)(2,1)S(1)}, bf16[384,16,128]{2,1,0:T(8,128)(2,1)S(1)}, u32[]{:S(2)}, u32[]{:S(2)}) %collective-permute-start.36) | collective-permute-done | bytes 1572896 | tf_op jit(solution)/shard_map/ppermute | solution.py:1080
  185.6 1.7 collective-permute-start.39
  192.3 9.2 %feed_gradients.1 = (f32[512,512]{1,0:T(8,128)}, f32[512,512]{1,0:T(8,128)}, f32[1,512]{1,0:T(1,128)}) custom-call(bf16[1024,1024]{1,0:T(8,128)(2,1)} %copy-done.8, bf16[1024,1024]{1,0:T(8,128)(2,1)} %copy-done.29, bf16[512,512]{1,0:T(8,128)(2,1)} %f1.1, f32[1,512]{1,0:T(1,128)} %bitcast.62, bf16[512,512]{1,0:T(8,128)(2,1)} %f2.1), custom_call_target="tpu_custom_call" | custom-call | flops 4294967296 | bytes 4194304 | tf_op jit(solution)/shard_map/feed_gradients/pallas_call | solution.py:777
  201.5 4.8 %collective-permute-done.38 = bf16[96,16,128]{2,1,0:T(8,128)(2,1)S(1)} collective-permute-done((bf16[96,16,128]{2,1,0:T(8,128)(2,1)}, bf16[96,16,128]{2,1,0:T(8,128)(2,1)S(1)}, u32[]{:S(2)}, u32[]{:S(2)}) %collective-permute-start.38) | collective-permute-done | bytes 393248 | tf_op jit(solution)/shard_map/ppermute | solution.py:1080
  208.8 1.6 collective-permute-start.44
  211.4 1.4 collective-permute-start.46
  213.6 4.1 %collective-permute-done.42 = bf16[24,16,128]{2,1,0:T(8,128)(2,1)S(1)} collective-permute-done((bf16[24,16,128]{2,1,0:T(8,128)(2,1)S(1)}, bf16[24,16,128]{2,1,0:T(8,128)(2,1)S(1)}, u32[]{:S(2)}, u32[]{:S(2)}) %collective-permute-start.42) | collective-permute-done | bytes 98336 | tf_op jit(solution)/shard_map/ppermute | solution.py:1080
  217.7 1.6 collective-permute-start.50
  219.9 2.6 collective-permute-start.49
  224.2 3.2 %collective-permute-done.49 = bf16[24,16,128]{2,1,0:T(8,128)(2,1)S(1)} collective-permute-done((bf16[24,16,128]{2,1,0:T(8,128)(2,1)S(1)}, bf16[24,16,128]{2,1,0:T(8,128)(2,1)S(1)}, u32[]{:S(2)}, u32[]{:S(2)}) %collective-permute-start.49) | collective-permute-done | bytes 98336 | tf_op jit(solution)/shard_map/ppermute | solution.py:1080
  228.6 2.3 collective-permute-done.47
  231.0 1.7 collective-permute-start.53
  235.5 2.0 collective-permute-start.56
  237.5 4.3 %collective-permute-done.56.refs_3_ = bf16[16,16,128]{2,1,0:T(8,128)(2,1)S(1)} collective-permute-done((bf16[16,16,128]{2,1,0:T(8,128)(2,1)S(1)}, bf16[16,16,128]{2,1,0:T(8,128)(2,1)S(1)}, u32[]{:S(2)}, u32[]{:S(2)}) %collective-permute-start.56) | collective-permute-done | bytes 65568 | tf_op jit(solution)/shard_map/ppermute | solution.py:1080
  242.9 4.1 %collective-permute-done.54.refs_1_ = bf16[16,16,128]{2,1,0:T(8,128)(2,1)S(1)} collective-permute-done((bf16[16,16,128]{2,1,0:T(8,128)(2,1)S(1)}, bf16[16,16,128]{2,1,0:T(8,128)(2,1)S(1)}, u32[]{:S(2)}, u32[]{:S(2)}) %collective-permute-start.54) | collective-permute-done | bytes 65568 | tf_op jit(solution)/shard_map/ppermute | solution.py:1080
  247.6 3.0 %node_gradient.1 = f32[64,512]{1,0:T(8,128)} custom-call(f32[64,512]{1,0:T(8,128)} %get-tuple-element.234.g_u1, f32[64,512]{1,0:T(8,128)} %get-tuple-element.235.own, bf16[1216,512]{1,0:T(8,128)(2,1)} %m1.5, f32[64,16,128]{2,1,0:T(8,128)} %get-tuple-element.266.refs_0_, bf16[16,16,128]{2,1,0:T(8,128)(2,1)} %copy-done.23, bf16[16,16,128]{2,1,0:T(8,128)(2,1)} %copy-done.22, ...), custom_call_target="tpu_custom_call" | custom-call | flops 134217728 | bytes 2097152 | tf_op jit(solution)/shard_map/node_gradient/pallas_call | solution.py:180
  250.9 3.4 %collective-permute-done.57.second = bf16[384,16,128]{2,1,0:T(8,128)(2,1)S(1)} collective-permute-done((bf16[384,16,128]{2,1,0:T(8,128)(2,1)S(1)}, bf16[384,16,128]{2,1,0:T(8,128)(2,1)S(1)}, u32[]{:S(2)}, u32[]{:S(2)}) %collective-permute-start.57) | collective-permute-done | bytes 1572896 | tf_op jit(solution)/shard_map/ppermute | solution.py:1080
  255.4 4.7 %weight_gradients.1 = (f32[1216,512]{1,0:T(8,128)}, f32[1,512]{1,0:T(1,128)}, f32[512,512]{1,0:T(8,128)}, f32[1,512]{1,0:T(1,128)}, f32[512,512]{1,0:T(8,128)}, ...) custom-call(s32[1]{0:T(128)} %bitcast.16.base, ...), custom_call_target="tpu_custom_call" | custom-call | bytes 10485760 | tf_op jit(solution)/shard_map/weight_gradients/pallas_call | solution.py:180
  (194 shorter events, 53.6 us)
Async XLA Ops:
  0.7 11.8 %collective-permute-start.2 = (bf16[64,512]{1,0:T(8,128)(2,1)}, bf16[64,512]{1,0:T(8,128)(2,1)S(1)}, u32[]{:S(2)}, u32[]{:S(2)}) collective-permute-start(bf16[64,512]{1,0:T(8,128)(2,1)} %node.3), channel_id=1, source_target_pairs={{0,24},{1,25},{2,26},{3,27},{4,28},{5,29},{6,30},{7,31},{8,16},{9,... | collective-permute-start | bytes 196616 | tf_op jit(solution)/shard_map/ppermute | solution.py:1080
  5.8 6.7 %collective-permute-start.1 = (bf16[64,512]{1,0:T(8,128)(2,1)}, bf16[64,512]{1,0:T(8,128)(2,1)S(1)}, u32[]{:S(2)}, u32[]{:S(2)}) collective-permute-start(bf16[64,512]{1,0:T(8,128)(2,1)} %node.3), channel_id=1, source_target_pairs={{0,8},{1,9},{2,10},{3,11},{4,12},{5,13},{6,14},{7,15},{8,0},{9,1},... | collective-permute-start | bytes 196616 | tf_op jit(solution)/shard_map/ppermute | solution.py:1080
  5.8 6.7 %collective-permute-start = (bf16[64,512]{1,0:T(8,128)(2,1)}, bf16[64,512]{1,0:T(8,128)(2,1)S(1)}, u32[]{:S(2)}, u32[]{:S(2)}) collective-permute-start(bf16[64,512]{1,0:T(8,128)(2,1)} %node.3), channel_id=1, source_target_pairs={{0,16},{1,17},{2,18},{3,19},{4,20},{5,21},{6,22},{7,23},{8,24},{9,... | collective-permute-start | bytes 196616 | tf_op jit(solution)/shard_map/ppermute | solution.py:1080
  7.5 7.6 %collective-permute-start.3 = (bf16[256,512]{1,0:T(8,128)(2,1)S(1)}, bf16[256,512]{1,0:T(8,128)(2,1)S(1)}, u32[]{:S(2)}, u32[]{:S(2)}) collective-permute-start(bf16[256,512]{1,0:T(8,128)(2,1)S(1)} %get-tuple-element.159.refs_4_.refs_8_), channel_id=1, source_target_pairs={{0,2},{1,3},{2,0},{3,1},{4,6},{5,7},{6,4},{7,5},{8,10},{9,11},{10,... | collective-permute-start | bytes 786440 | tf_op jit(solution)/shard_map/ppermute | solution.py:1080
  15.1 10.6 %collective-permute-start.6 = (bf16[256,512]{1,0:T(8,128)(2,1)S(1)}, bf16[256,512]{1,0:T(8,128)(2,1)S(1)}, u32[]{:S(2)}, u32[]{:S(2)}) collective-permute-start(bf16[256,512]{1,0:T(8,128)(2,1)S(1)} %pad_maximum_fusion.4), channel_id=1, source_target_pairs={{0,6},{1,7},{2,4},{3,5},{4,2},{5,3},{6,0},{7,1},{8,14},{9,15},{10,... | collective-permute-start | bytes 786440 | tf_op jit(solution)/shard_map/ppermute | solution.py:1080
  17.5 10.6 %collective-permute-start.5 = (bf16[256,512]{1,0:T(8,128)(2,1)S(1)}, bf16[256,512]{1,0:T(8,128)(2,1)S(1)}, u32[]{:S(2)}, u32[]{:S(2)}) collective-permute-start(bf16[256,512]{1,0:T(8,128)(2,1)S(1)} %pad_maximum_fusion.4), channel_id=1, source_target_pairs={{0,2},{1,3},{2,0},{3,1},{4,6},{5,7},{6,4},{7,5},{8,10},{9,11},{10,... | collective-permute-start | bytes 786440 | tf_op jit(solution)/shard_map/ppermute | solution.py:1080
  18.0 10.1 %collective-permute-start.4 = (bf16[256,512]{1,0:T(8,128)(2,1)S(1)}, bf16[256,512]{1,0:T(8,128)(2,1)S(1)}, u32[]{:S(2)}, u32[]{:S(2)}) collective-permute-start(bf16[256,512]{1,0:T(8,128)(2,1)S(1)} %pad_maximum_fusion.4), channel_id=1, source_target_pairs={{0,4},{1,5},{2,6},{3,7},{4,0},{5,1},{6,2},{7,3},{8,12},{9,13},{10,... | collective-permute-start | bytes 786440 | tf_op jit(solution)/shard_map/ppermute | solution.py:1080
  30.8 22.4 %collective-permute-start.9 = (bf16[256,512]{1,0:T(8,128)(2,1)S(1)}, bf16[256,512]{1,0:T(8,128)(2,1)S(1)}, u32[]{:S(2)}, u32[]{:S(2)}) collective-permute-start(bf16[256,512]{1,0:T(8,128)(2,1)S(1)} %get-tuple-element.159.refs_4_.refs_8_), channel_id=1, source_target_pairs={{0,1},{1,0},{2,3},{3,2},{4,5},{5,4},{6,7},{7,6},{8,9},{9,8},{10,11... | collective-permute-start | bytes 786440 | tf_op jit(solution)/shard_map/ppermute | solution.py:1080
  31.3 21.9 %collective-permute-start.10 = (bf16[256,512]{1,0:T(8,128)(2,1)S(1)}, bf16[256,512]{1,0:T(8,128)(2,1)S(1)}, u32[]{:S(2)}, u32[]{:S(2)}) collective-permute-start(bf16[256,512]{1,0:T(8,128)(2,1)S(1)} %collective-permute-done.3.refs_6_.refs_10_), channel_id=1, source_target_pairs={{0,1},{1,0},{2,3},{3,2},{4,5},{5,4},{6,7},{7,6},{8,9},{9,8},{10,11... | collective-permute-start | bytes 786440 | tf_op jit(solution)/shard_map/ppermute | solution.py:1080
  31.3 21.9 %collective-permute-start.11 = (bf16[256,512]{1,0:T(8,128)(2,1)S(1)}, bf16[256,512]{1,0:T(8,128)(2,1)S(1)}, u32[]{:S(2)}, u32[]{:S(2)}) collective-permute-start(bf16[256,512]{1,0:T(8,128)(2,1)S(1)} %get-tuple-element.160.refs_5_.refs_9_), channel_id=1, source_target_pairs={{0,2},{1,3},{2,0},{3,1},{4,6},{5,7},{6,4},{7,5},{8,10},{9,11},{10,... | collective-permute-start | bytes 786440 | tf_op jit(solution)/shard_map/ppermute | solution.py:1080
  32.7 20.6 %collective-permute-start.8 = (bf16[528,512]{1,0:T(8,128)(2,1)S(1)}, bf16[528,512]{1,0:T(8,128)(2,1)S(1)}, u32[]{:S(2)}, u32[]{:S(2)}) collective-permute-start(bf16[528,512]{1,0:T(8,128)(2,1)S(1)} %concatenate.30.refs_0_.refs_4_), channel_id=1, source_target_pairs={{0,2},{1,3},{2,0},{3,1},{4,6},{5,7},{6,4},{7,5},{8,10},{9,11},{10,... | collective-permute-start | bytes 1622024 | tf_op jit(solution)/shard_map/ppermute | solution.py:1080
  63.3 8.7 %collective-permute-start.18 = (bf16[64,192]{1,0:T(8,128)(2,1)}, bf16[64,192]{1,0:T(8,128)(2,1)S(1)}, u32[]{:S(2)}, u32[]{:S(2)}) collective-permute-start(bf16[64,192]{1,0:T(8,128)(2,1)} %get-tuple-element.166), channel_id=1, source_target_pairs={{0,24},{1,25},{2,26},{3,27},{4,28},{5,29},{6,30},{7,31},{8,16},{9,... | collective-permute-start | bytes 73736 | tf_op jit(solution)/shard_map/ppermute | solution.py:1080
  66.6 5.4 %collective-permute-start.17 = (bf16[64,192]{1,0:T(8,128)(2,1)}, bf16[64,192]{1,0:T(8,128)(2,1)S(1)}, u32[]{:S(2)}, u32[]{:S(2)}) collective-permute-start(bf16[64,192]{1,0:T(8,128)(2,1)} %get-tuple-element.166), channel_id=1, source_target_pairs={{0,8},{1,9},{2,10},{3,11},{4,12},{5,13},{6,14},{7,15},{8,0},{9,1},... | collective-permute-start | bytes 73736 | tf_op jit(solution)/shard_map/ppermute | solution.py:1080
  66.6 5.4 %collective-permute-start.16 = (bf16[64,192]{1,0:T(8,128)(2,1)}, bf16[64,192]{1,0:T(8,128)(2,1)S(1)}, u32[]{:S(2)}, u32[]{:S(2)}) collective-permute-start(bf16[64,192]{1,0:T(8,128)(2,1)} %get-tuple-element.166), channel_id=1, source_target_pairs={{0,16},{1,17},{2,18},{3,19},{4,20},{5,21},{6,22},{7,23},{8,24},{9,... | collective-permute-start | bytes 73736 | tf_op jit(solution)/shard_map/ppermute | solution.py:1080
  72.1 5.2 %collective-permute-start.19 = (bf16[256,192]{1,0:T(8,128)(2,1)S(1)}, bf16[256,192]{1,0:T(8,128)(2,1)S(1)}, u32[]{:S(2)}, u32[]{:S(2)}) collective-permute-start(bf16[256,192]{1,0:T(8,128)(2,1)S(1)} %get-tuple-element.296), channel_id=1, source_target_pairs={{0,4},{1,5},{2,6},{3,7},{4,0},{5,1},{6,2},{7,3},{8,12},{9,13},{10,... | collective-permute-start | bytes 294920 | tf_op jit(solution)/shard_map/ppermute | solution.py:1080
  73.6 7.4 %collective-permute-start.21 = (bf16[256,192]{1,0:T(8,128)(2,1)S(1)}, bf16[256,192]{1,0:T(8,128)(2,1)S(1)}, u32[]{:S(2)}, u32[]{:S(2)}) collective-permute-start(bf16[256,192]{1,0:T(8,128)(2,1)S(1)} %get-tuple-element.296), channel_id=1, source_target_pairs={{0,6},{1,7},{2,4},{3,5},{4,2},{5,3},{6,0},{7,1},{8,14},{9,15},{10,... | collective-permute-start | bytes 294920 | tf_op jit(solution)/shard_map/ppermute | solution.py:1080
  75.0 6.0 %collective-permute-start.20 = (bf16[256,192]{1,0:T(8,128)(2,1)S(1)}, bf16[256,192]{1,0:T(8,128)(2,1)S(1)}, u32[]{:S(2)}, u32[]{:S(2)}) collective-permute-start(bf16[256,192]{1,0:T(8,128)(2,1)S(1)} %get-tuple-element.296), channel_id=1, source_target_pairs={{0,2},{1,3},{2,0},{3,1},{4,6},{5,7},{6,4},{7,5},{8,10},{9,11},{10,... | collective-permute-start | bytes 294920 | tf_op jit(solution)/shard_map/ppermute | solution.py:1080
  111.4 6.4 %collective-permute-start.24 = (bf16[256,192]{1,0:T(8,128)(2,1)S(1)}, bf16[256,192]{1,0:T(8,128)(2,1)S(1)}, u32[]{:S(2)}, u32[]{:S(2)}) collective-permute-start(bf16[256,192]{1,0:T(8,128)(2,1)S(1)} %get-tuple-element.282), channel_id=1, source_target_pairs={{0,4},{1,5},{2,6},{3,7},{4,0},{5,1},{6,2},{7,3},{8,12},{9,13},{10,... | collective-permute-start | bytes 294920 | tf_op jit(solution)/shard_map/ppermute | solution.py:1080
  112.2 7.7 %collective-permute-start.26 = (bf16[256,192]{1,0:T(8,128)(2,1)S(1)}, bf16[256,192]{1,0:T(8,128)(2,1)S(1)}, u32[]{:S(2)}, u32[]{:S(2)}) collective-permute-start(bf16[256,192]{1,0:T(8,128)(2,1)S(1)} %get-tuple-element.283), channel_id=1, source_target_pairs={{0,6},{1,7},{2,4},{3,5},{4,2},{5,3},{6,0},{7,1},{8,14},{9,15},{10,... | collective-permute-start | bytes 294920 | tf_op jit(solution)/shard_map/ppermute | solution.py:1080
  113.5 7.8 %collective-permute-start.25 = (bf16[256,192]{1,0:T(8,128)(2,1)S(1)}, bf16[256,192]{1,0:T(8,128)(2,1)S(1)}, u32[]{:S(2)}, u32[]{:S(2)}) collective-permute-start(bf16[256,192]{1,0:T(8,128)(2,1)S(1)} %get-tuple-element.284), channel_id=1, source_target_pairs={{0,2},{1,3},{2,0},{3,1},{4,6},{5,7},{6,4},{7,5},{8,10},{9,11},{10,... | collective-permute-start | bytes 294920 | tf_op jit(solution)/shard_map/ppermute | solution.py:1080
  122.1 5.8 %collective-permute-start.29 = (bf16[64,192]{1,0:T(8,128)(2,1)S(1)}, bf16[64,192]{1,0:T(8,128)(2,1)S(1)}, u32[]{:S(2)}, u32[]{:S(2)}) collective-permute-start(bf16[64,192]{1,0:T(8,128)(2,1)S(1)} %get-tuple-element.293), channel_id=1, source_target_pairs={{0,24},{1,25},{2,26},{3,27},{4,28},{5,29},{6,30},{7,31},{8,16},{9,... | collective-permute-start | bytes 73736 | tf_op jit(solution)/shard_map/ppermute | solution.py:1080
  124.0 4.8 %collective-permute-start.27 = (bf16[64,192]{1,0:T(8,128)(2,1)S(1)}, bf16[64,192]{1,0:T(8,128)(2,1)S(1)}, u32[]{:S(2)}, u32[]{:S(2)}) collective-permute-start(bf16[64,192]{1,0:T(8,128)(2,1)S(1)} %get-tuple-element.295), channel_id=1, source_target_pairs={{0,16},{1,17},{2,18},{3,19},{4,20},{5,21},{6,22},{7,23},{8,24},{9,... | collective-permute-start | bytes 73736 | tf_op jit(solution)/shard_map/ppermute | solution.py:1080
  136.0 12.1 %collective-permute-start.32 = (bf16[64,1024]{1,0:T(8,128)(2,1)}, bf16[64,1024]{1,0:T(8,128)(2,1)S(1)}, u32[]{:S(2)}, u32[]{:S(2)}) collective-permute-start(bf16[64,1024]{1,0:T(8,128)(2,1)} %get-tuple-element.183), channel_id=1, source_target_pairs={{0,24},{1,25},{2,26},{3,27},{4,28},{5,29},{6,30},{7,31},{8,16},{9,... | collective-permute-start | bytes 393224 | tf_op jit(solution)/shard_map/ppermute | solution.py:1080
  138.9 9.2 %collective-permute-start.31 = (bf16[64,1024]{1,0:T(8,128)(2,1)}, bf16[64,1024]{1,0:T(8,128)(2,1)S(1)}, u32[]{:S(2)}, u32[]{:S(2)}) collective-permute-start(bf16[64,1024]{1,0:T(8,128)(2,1)} %get-tuple-element.183), channel_id=1, source_target_pairs={{0,8},{1,9},{2,10},{3,11},{4,12},{5,13},{6,14},{7,15},{8,0},{9,1},... | collective-permute-start | bytes 393224 | tf_op jit(solution)/shard_map/ppermute | solution.py:1080
  139.2 9.5 %collective-permute-start.30 = (bf16[64,1024]{1,0:T(8,128)(2,1)}, bf16[64,1024]{1,0:T(8,128)(2,1)S(1)}, u32[]{:S(2)}, u32[]{:S(2)}) collective-permute-start(bf16[64,1024]{1,0:T(8,128)(2,1)} %get-tuple-element.183), channel_id=1, source_target_pairs={{0,16},{1,17},{2,18},{3,19},{4,20},{5,21},{6,22},{7,23},{8,24},{9,... | collective-permute-start | bytes 393224 | tf_op jit(solution)/shard_map/ppermute | solution.py:1080
  148.7 29.3 %collective-permute-start.35 = (bf16[256,1024]{1,0:T(8,128)(2,1)S(1)}, bf16[256,1024]{1,0:T(8,128)(2,1)S(1)}, u32[]{:S(2)}, u32[]{:S(2)}) collective-permute-start(bf16[256,1024]{1,0:T(8,128)(2,1)S(1)} %pad_maximum_fusion.2), channel_id=1, source_target_pairs={{0,6},{1,7},{2,4},{3,5},{4,2},{5,3},{6,0},{7,1},{8,14},{9,15},{10,... | collective-permute-start | bytes 1572872 | tf_op jit(solution)/shard_map/ppermute | solution.py:1080
  150.5 27.5 %collective-permute-start.34 = (bf16[256,1024]{1,0:T(8,128)(2,1)S(1)}, bf16[256,1024]{1,0:T(8,128)(2,1)S(1)}, u32[]{:S(2)}, u32[]{:S(2)}) collective-permute-start(bf16[256,1024]{1,0:T(8,128)(2,1)S(1)} %pad_maximum_fusion.2), channel_id=1, source_target_pairs={{0,2},{1,3},{2,0},{3,1},{4,6},{5,7},{6,4},{7,5},{8,10},{9,11},{10,... | collective-permute-start | bytes 1572872 | tf_op jit(solution)/shard_map/ppermute | solution.py:1080
  151.8 26.3 %collective-permute-start.33 = (bf16[256,1024]{1,0:T(8,128)(2,1)S(1)}, bf16[256,1024]{1,0:T(8,128)(2,1)S(1)}, u32[]{:S(2)}, u32[]{:S(2)}) collective-permute-start(bf16[256,1024]{1,0:T(8,128)(2,1)S(1)} %pad_maximum_fusion.2), channel_id=1, source_target_pairs={{0,4},{1,5},{2,6},{3,7},{4,0},{5,1},{6,2},{7,3},{8,12},{9,13},{10,... | collective-permute-start | bytes 1572872 | tf_op jit(solution)/shard_map/ppermute | solution.py:1080
  183.8 7.2 %collective-permute-start.41 = (bf16[1024,1024]{1,0:T(8,128)(2,1)S(1)}, bf16[1024,1024]{1,0:T(8,128)(2,1)S(1)}, u32[]{:S(2)}, u32[]{:S(2)}) collective-permute-start(bf16[1024,1024]{1,0:T(8,128)(2,1)S(1)} %pad_maximum_fusion.first), channel_id=1, source_target_pairs={{0,1},{1,0},{2,3},{3,2},{4,5},{5,4},{6,7},{7,6},{8,9},{9,8},{10,11... | collective-permute-start | bytes 6291464 | tf_op jit(solution)/shard_map/ppermute | solution.py:1080
  184.0 5.5 %collective-permute-start.40 = (bf16[256,16,128]{2,1,0:T(8,128)(2,1)S(1)}, bf16[256,16,128]{2,1,0:T(8,128)(2,1)S(1)}, u32[]{:S(2)}, u32[]{:S(2)}) collective-permute-start(bf16[256,16,128]{2,1,0:T(8,128)(2,1)S(1)} %bitcast.66), channel_id=1, source_target_pairs={{0,1},{1,0},{2,3},{3,2},{4,5},{5,4},{6,7},{7,6},{8,9},{9,8},{10,11... | collective-permute-start | bytes 3145736 | tf_op jit(solution)/shard_map/ppermute | solution.py:1080
  185.6 15.9 %collective-permute-start.39 = (bf16[96,16,128]{2,1,0:T(8,128)(2,1)}, bf16[96,16,128]{2,1,0:T(8,128)(2,1)S(1)}, u32[]{:S(2)}, u32[]{:S(2)}) collective-permute-start(bf16[96,16,128]{2,1,0:T(8,128)(2,1)} %get-tuple-element.276), channel_id=1, source_target_pairs={{0,6},{1,7},{2,4},{3,5},{4,2},{5,3},{6,0},{7,1},{8,14},{9,15},{10,... | collective-permute-start | bytes 1179656 | tf_op jit(solution)/shard_map/ppermute | solution.py:1080
  187.4 19.0 %collective-permute-start.38 = (bf16[96,16,128]{2,1,0:T(8,128)(2,1)}, bf16[96,16,128]{2,1,0:T(8,128)(2,1)S(1)}, u32[]{:S(2)}, u32[]{:S(2)}) collective-permute-start(bf16[96,16,128]{2,1,0:T(8,128)(2,1)} %get-tuple-element.277), channel_id=1, source_target_pairs={{0,2},{1,3},{2,0},{3,1},{4,6},{5,7},{6,4},{7,5},{8,10},{9,11},{10,... | collective-permute-start | bytes 1179656 | tf_op jit(solution)/shard_map/ppermute | solution.py:1080
  188.6 17.8 %collective-permute-start.37 = (bf16[96,16,128]{2,1,0:T(8,128)(2,1)}, bf16[96,16,128]{2,1,0:T(8,128)(2,1)}, u32[]{:S(2)}, u32[]{:S(2)}) collective-permute-start(bf16[96,16,128]{2,1,0:T(8,128)(2,1)} %get-tuple-element.278), channel_id=1, source_target_pairs={{0,4},{1,5},{2,6},{3,7},{4,0},{5,1},{6,2},{7,3},{8,12},{9,13},{10,... | collective-permute-start | bytes 1179656 | tf_op jit(solution)/shard_map/ppermute | solution.py:1080
  207.7 10.0 %collective-permute-start.42 = (bf16[24,16,128]{2,1,0:T(8,128)(2,1)S(1)}, bf16[24,16,128]{2,1,0:T(8,128)(2,1)S(1)}, u32[]{:S(2)}, u32[]{:S(2)}) collective-permute-start(bf16[24,16,128]{2,1,0:T(8,128)(2,1)S(1)} %get-tuple-element.287), channel_id=1, source_target_pairs={{0,16},{1,17},{2,18},{3,19},{4,20},{5,21},{6,22},{7,23},{8,24},{9,... | collective-permute-start | bytes 294920 | tf_op jit(solution)/shard_map/ppermute | solution.py:1080
  208.8 10.5 %collective-permute-start.44 = (bf16[24,16,128]{2,1,0:T(8,128)(2,1)S(1)}, bf16[24,16,128]{2,1,0:T(8,128)(2,1)S(1)}, u32[]{:S(2)}, u32[]{:S(2)}) collective-permute-start(bf16[24,16,128]{2,1,0:T(8,128)(2,1)S(1)} %get-tuple-element.288), channel_id=1, source_target_pairs={{0,24},{1,25},{2,26},{3,27},{4,28},{5,29},{6,30},{7,31},{8,16},{9,... | collective-permute-start | bytes 294920 | tf_op jit(solution)/shard_map/ppermute | solution.py:1080
  210.4 8.9 %collective-permute-start.43 = (bf16[24,16,128]{2,1,0:T(8,128)(2,1)S(1)}, bf16[24,16,128]{2,1,0:T(8,128)(2,1)S(1)}, u32[]{:S(2)}, u32[]{:S(2)}) collective-permute-start(bf16[24,16,128]{2,1,0:T(8,128)(2,1)S(1)} %get-tuple-element.289), channel_id=1, source_target_pairs={{0,8},{1,9},{2,10},{3,11},{4,12},{5,13},{6,14},{7,15},{8,0},{9,1},... | collective-permute-start | bytes 294920 | tf_op jit(solution)/shard_map/ppermute | solution.py:1080
  211.4 8.0 %collective-permute-start.46 = (bf16[64,16,128]{2,1,0:T(8,128)(2,1)S(1)}, bf16[64,16,128]{2,1,0:T(8,128)(2,1)S(1)}, u32[]{:S(2)}, u32[]{:S(2)}) collective-permute-start(bf16[64,16,128]{2,1,0:T(8,128)(2,1)S(1)} %get-tuple-element.280), channel_id=1, source_target_pairs={{0,2},{1,3},{2,0},{3,1},{4,6},{5,7},{6,4},{7,5},{8,10},{9,11},{10,... | collective-permute-start | bytes 786440 | tf_op jit(solution)/shard_map/ppermute | solution.py:1080
  212.8 7.1 %collective-permute-start.45 = (bf16[64,16,128]{2,1,0:T(8,128)(2,1)S(1)}, bf16[64,16,128]{2,1,0:T(8,128)(2,1)S(1)}, u32[]{:S(2)}, u32[]{:S(2)}) collective-permute-start(bf16[64,16,128]{2,1,0:T(8,128)(2,1)S(1)} %get-tuple-element.281), channel_id=1, source_target_pairs={{0,4},{1,5},{2,6},{3,7},{4,0},{5,1},{6,2},{7,3},{8,12},{9,13},{10,... | collective-permute-start | bytes 786440 | tf_op jit(solution)/shard_map/ppermute | solution.py:1080
  217.7 13.3 %collective-permute-start.50 = (bf16[64,16,128]{2,1,0:T(8,128)(2,1)S(1)}, bf16[64,16,128]{2,1,0:T(8,128)(2,1)S(1)}, u32[]{:S(2)}, u32[]{:S(2)}) collective-permute-start(bf16[64,16,128]{2,1,0:T(8,128)(2,1)S(1)} %get-tuple-element.279), channel_id=1, source_target_pairs={{0,6},{1,7},{2,4},{3,5},{4,2},{5,3},{6,0},{7,1},{8,14},{9,15},{10,... | collective-permute-start | bytes 786440 | tf_op jit(solution)/shard_map/ppermute | solution.py:1080
  219.9 7.6 %collective-permute-start.49 = (bf16[24,16,128]{2,1,0:T(8,128)(2,1)S(1)}, bf16[24,16,128]{2,1,0:T(8,128)(2,1)S(1)}, u32[]{:S(2)}, u32[]{:S(2)}) collective-permute-start(bf16[24,16,128]{2,1,0:T(8,128)(2,1)S(1)} %fusion.4), channel_id=1, source_target_pairs={{0,24},{1,25},{2,26},{3,27},{4,28},{5,29},{6,30},{7,31},{8,16},{9,... | collective-permute-start | bytes 294920 | tf_op jit(solution)/shard_map/ppermute | solution.py:1080
  222.5 6.2 %collective-permute-start.48 = (bf16[24,16,128]{2,1,0:T(8,128)(2,1)S(1)}, bf16[24,16,128]{2,1,0:T(8,128)(2,1)S(1)}, u32[]{:S(2)}, u32[]{:S(2)}) collective-permute-start(bf16[24,16,128]{2,1,0:T(8,128)(2,1)S(1)} %fusion.4), channel_id=1, source_target_pairs={{0,8},{1,9},{2,10},{3,11},{4,12},{5,13},{6,14},{7,15},{8,0},{9,1},... | collective-permute-start | bytes 294920 | tf_op jit(solution)/shard_map/ppermute | solution.py:1080
  223.7 7.3 %collective-permute-start.47 = (bf16[24,16,128]{2,1,0:T(8,128)(2,1)S(1)}, bf16[24,16,128]{2,1,0:T(8,128)(2,1)S(1)}, u32[]{:S(2)}, u32[]{:S(2)}) collective-permute-start(bf16[24,16,128]{2,1,0:T(8,128)(2,1)S(1)} %fusion.4), channel_id=1, source_target_pairs={{0,16},{1,17},{2,18},{3,19},{4,20},{5,21},{6,22},{7,23},{8,24},{9,... | collective-permute-start | bytes 294920 | tf_op jit(solution)/shard_map/ppermute | solution.py:1080
  231.0 19.6 %collective-permute-start.53 = (bf16[96,16,128]{2,1,0:T(8,128)(2,1)S(1)}, bf16[96,16,128]{2,1,0:T(8,128)(2,1)S(1)}, u32[]{:S(2)}, u32[]{:S(2)}) collective-permute-start(bf16[96,16,128]{2,1,0:T(8,128)(2,1)S(1)} %pad_maximum_fusion.3), channel_id=1, source_target_pairs={{0,6},{1,7},{2,4},{3,5},{4,2},{5,3},{6,0},{7,1},{8,14},{9,15},{10,... | collective-permute-start | bytes 1179656 | tf_op jit(solution)/shard_map/ppermute | solution.py:1080
  232.6 17.9 %collective-permute-start.52 = (bf16[96,16,128]{2,1,0:T(8,128)(2,1)S(1)}, bf16[96,16,128]{2,1,0:T(8,128)(2,1)S(1)}, u32[]{:S(2)}, u32[]{:S(2)}) collective-permute-start(bf16[96,16,128]{2,1,0:T(8,128)(2,1)S(1)} %pad_maximum_fusion.3), channel_id=1, source_target_pairs={{0,2},{1,3},{2,0},{3,1},{4,6},{5,7},{6,4},{7,5},{8,10},{9,11},{10,... | collective-permute-start | bytes 1179656 | tf_op jit(solution)/shard_map/ppermute | solution.py:1080
  233.9 16.7 %collective-permute-start.51 = (bf16[96,16,128]{2,1,0:T(8,128)(2,1)S(1)}, bf16[96,16,128]{2,1,0:T(8,128)(2,1)S(1)}, u32[]{:S(2)}, u32[]{:S(2)}) collective-permute-start(bf16[96,16,128]{2,1,0:T(8,128)(2,1)S(1)} %pad_maximum_fusion.3), channel_id=1, source_target_pairs={{0,4},{1,5},{2,6},{3,7},{4,0},{5,1},{6,2},{7,3},{8,12},{9,13},{10,... | collective-permute-start | bytes 1179656 | tf_op jit(solution)/shard_map/ppermute | solution.py:1080
  235.5 6.3 %collective-permute-start.56 = (bf16[16,16,128]{2,1,0:T(8,128)(2,1)S(1)}, bf16[16,16,128]{2,1,0:T(8,128)(2,1)S(1)}, u32[]{:S(2)}, u32[]{:S(2)}) collective-permute-start(bf16[16,16,128]{2,1,0:T(8,128)(2,1)S(1)} %get-tuple-element.290), channel_id=1, source_target_pairs={{0,24},{1,25},{2,26},{3,27},{4,28},{5,29},{6,30},{7,31},{8,16},{9,... | collective-permute-start | bytes 196616 | tf_op jit(solution)/shard_map/ppermute | solution.py:1080
  237.5 5.4 %collective-permute-start.55 = (bf16[16,16,128]{2,1,0:T(8,128)(2,1)S(1)}, bf16[16,16,128]{2,1,0:T(8,128)(2,1)S(1)}, u32[]{:S(2)}, u32[]{:S(2)}) collective-permute-start(bf16[16,16,128]{2,1,0:T(8,128)(2,1)S(1)} %get-tuple-element.291), channel_id=1, source_target_pairs={{0,8},{1,9},{2,10},{3,11},{4,12},{5,13},{6,14},{7,15},{8,0},{9,1},... | collective-permute-start | bytes 196616 | tf_op jit(solution)/shard_map/ppermute | solution.py:1080
  241.8 5.2 %collective-permute-start.54 = (bf16[16,16,128]{2,1,0:T(8,128)(2,1)S(1)}, bf16[16,16,128]{2,1,0:T(8,128)(2,1)S(1)}, u32[]{:S(2)}, u32[]{:S(2)}) collective-permute-start(bf16[16,16,128]{2,1,0:T(8,128)(2,1)S(1)} %get-tuple-element.292), channel_id=1, source_target_pairs={{0,16},{1,17},{2,18},{3,19},{4,20},{5,21},{6,22},{7,23},{8,24},{9,... | collective-permute-start | bytes 196616 | tf_op jit(solution)/shard_map/ppermute | solution.py:1080
  (44 other events, 297.8 us)

commit v3 on v2

--- a/solution.py
+++ b/solution.py
@@ -254,7 +254,7 @@
 
 
 def slot_block(slots):
-    for size in (10, 12, 8, 6, 5, 4, 3, 2):
+    for size in (12, 10, 8, 6, 5, 4, 3, 2):
         if slots % size == 0:
             return size
     return 1
@@ -925,7 +925,7 @@
     edges = slots * rows
     half = node_lo.shape[0]
     deep = half // rows // groups
-    at_once = 2 if groups % 2 == 0 else 1
+    at_once = 4 if groups % 4 == 0 else 1
     tiles = rows * width // (16 * LANES)
     slab = slab_tiles(weight_shapes(width, edge_width), len(codes)) * len(codes)
     node_lo, node_hi = [n.reshape(deep, groups, rows, width) for n in (node_lo, node_hi)]
@@ -1205,7 +1205,7 @@
     *outer, near = groups
 
     held = stack(sent_around(node_in, outer[0], devices))
-    held, idx_row, local_row, f2a = tied(held, idx_row, local_row, f2a)
+    held, idx_row, local_row, f2a, e_far = tied(held, idx_row, local_row, f2a, e_far)
     for group in outer[1:]:
         held = stack(sent_around(held, group, devices))
     f2b = feed_second[cut:]
@@ -1219,7 +1219,7 @@
         node_lo, node_hi, node_in, edge, idx_row, live_col, message_first,
         row(message_first_bias), message_second, row(message_second_bias),
     )
-    total, f1, f2a, f2b, e_far = tied(total, f1, f2a, f2b, e_far)
+    total, f1, f2a, f2b = tied(total, f1, f2a, f2b)
     f1, f2b = over(f1), over(f2b)
     f2 = [half for pair in zip(f2a, f2b) for half in pair]
     h1b, n1, sc1, n2, sc2, slope, h2b, far_part, own_part = residue_forward(

time: 261 us -> 259 us (level)
  transfers between devices with their start and end apart: 58 -> 58, of which waited for: 28 -> 26; matrix products, arithmetic and copies ran while one was open for 5% -> 5% of each run, Pallas kernels for 27% -> 26%
where the time goes in v3:
time: 259 us; the launch traced here: 258 us
  Pallas kernels  108 us (42%)
  waiting for transfers between devices  60.7 us (23%)
  starting transfers between devices  60.3 us (23%)
  local copies, waits for them, and re-layouts  17.5 us (7%)
  other arithmetic  9.73 us (4%)
    ppermute x58, waiting for transfers between devices, exchange(): return lax.ppermute(value, AXES, [(d, d ^ mask) for d in range(devices)])  60.7 us
    ppermute x58, starting transfers between devices, exchange(): return lax.ppermute(value, AXES, [(d, d ^ mask) for d in range(devices)])  60.3 us
    pallas_call x1, Pallas kernels, message_backward(): pl.pallas_call(functools.partial(message_backward_kernel, sb, blocks, gro...  24.6 us
    pallas_call x5, Pallas kernels, small_call(): pl.pallas_call(kernel, grid=(1,), in_specs=[pl.BlockSpec(memory_space=plt...  24.5 us
    pallas_call x1, Pallas kernels, edge_branch(): pl.pallas_call(functools.partial(edge_kernel, sb, blocks, hi_chunks, by_r...  23.9 us
    pallas_call x1, Pallas kernels, message_forward(): pl.pallas_call(functools.partial(message_forward_kernel, sb, by_rows), gr...  18.7 us
    unnamed x77, local copies, waits for them, and re-layouts  10.6 us
    pallas_call x1, Pallas kernels, feed_gradients(): pl.pallas_call(feed_kernel, grid=(half // chunk,), in_specs=[pl.BlockSpec...  9.21 us
  transfers between devices with their start and end apart: 58, of which 26 were waited for; matrix products, arithmetic and copies ran while one was open for 5% of the time, Pallas kernels for 26%

profile of v3, /device:TPU:0, one launch (start us, length us, event | category | flops | bytes accessed | tf_op | source)
XLA Modules:
  0.0 257.9 jit_solution(17482336463833761500)
XLA Ops:
  0.7 5.1 %collective-permute-start.2 = (bf16[64,512]{1,0:T(8,128)(2,1)}, bf16[64,512]{1,0:T(8,128)(2,1)S(1)}, u32[]{:S(2)}, u32[]{:S(2)}) collective-permute-start(bf16[64,512]{1,0:T(8,128)(2,1)} %node.3), channel_id=1, source_target_pairs={{0,24},{1,25},{2,26},{3,27},{4,28},{5,29},{6,30},{7,31},{8,16},{9,... | collective-permute-start | bytes 196616 | tf_op jit(solution)/shard_map/ppermute | solution.py:1080
  7.5 1.7 collective-permute-start.3
  12.5 1.7 slice.118.e_far
  15.1 2.4 collective-permute-start.6
  19.3 4.8 %group_order.1 = s32[30,128]{1,0:T(8,128)} custom-call(s32[32,128]{1,0:T(8,128)} %pad_bitcast_fusion.names), custom_call_target="tpu_custom_call" | custom-call | tf_op jit(solution)/shard_map/group_order/pallas_call | solution.py:180
  25.8 3.0 %collective-permute-done.5 = bf16[256,512]{1,0:T(8,128)(2,1)S(1)} collective-permute-done((bf16[256,512]{1,0:T(8,128)(2,1)S(1)}, bf16[256,512]{1,0:T(8,128)(2,1)S(1)}, u32[]{:S(2)}, u32[]{:S(2)}) %collective-permute-start.5) | collective-permute-done | bytes 262176 | tf_op jit(solution)/shard_map/ppermute | solution.py:1080
  33.3 18.7 %message_forward.1 = (bf16[3840,512]{1,0:T(8,128)(2,1)}, bf16[3840,512]{1,0:T(8,128)(2,1)}, bf16[3840,512]{1,0:T(8,128)(2,1)}, f32[64,512]{1,0:T(8,128)}) custom-call(bf16[1024,512]{1,0:T(8,128)(2,1)} %copy-done.17, bf16[1024,512]{1,0:T(8,128)(2,1)} %copy-done.31, bf16[64,512]{1,0:T(8,128)(2,1)} %node.3, bf16[60,64,192]{2,1,0:T(8,128)(2,1)} %bitcast.48, ...), custom_call_target="tpu_custom_call" | custom-call | flops 10821304320 | bytes 15237120 | tf_op jit(solution)/shard_map/message_forward/pallas_call | solution.py:364
  53.2 2.1 collective-permute-done.14.refs_9_.refs_13_
  56.7 5.3 %residue_forward.1 = (bf16[64,512]{1,0:T(8,128)(2,1)}, f32[64,512]{1,0:T(8,128)}, f32[64,128]{1,0:T(8,128)}, f32[64,512]{1,0:T(8,128)}, f32[64,128]{1,0:T(8,128)...) custom-call(bf16[64,512]{1,0:T(8,128)(2,1)} %node.3, ...), custom_call_target="tpu_custom_call" | custom-call | flops 268435456 | bytes 5242880 | tf_op jit(solution)/shard_map/residue_forward/pallas_call | solution.py:180
  62.1 3.5 %collective-permute-start.18 = (bf16[64,192]{1,0:T(8,128)(2,1)}, bf16[64,192]{1,0:T(8,128)(2,1)S(1)}, u32[]{:S(2)}, u32[]{:S(2)}) collective-permute-start(bf16[64,192]{1,0:T(8,128)(2,1)} %get-tuple-element.166), channel_id=1, source_target_pairs={{0,24},{1,25},{2,26},{3,27},{4,28},{5,29},{6,30},{7,31},{8,16},{9,... | collective-permute-start | bytes 73736 | tf_op jit(solution)/shard_map/ppermute | solution.py:1080
  67.3 3.6 %collective-permute-done.16 = bf16[64,192]{1,0:T(8,128)(2,1)S(1)} collective-permute-done((bf16[64,192]{1,0:T(8,128)(2,1)}, bf16[64,192]{1,0:T(8,128)(2,1)S(1)}, u32[]{:S(2)}, u32[]{:S(2)}) %collective-permute-start.16) | collective-permute-done | bytes 24608 | tf_op jit(solution)/shard_map/ppermute | solution.py:1080
  73.2 1.4 collective-permute-start.20
  74.6 1.7 collective-permute-done.19
  76.3 3.0 %collective-permute-done.20 = bf16[256,192]{1,0:T(8,128)(2,1)S(1)} collective-permute-done((bf16[256,192]{1,0:T(8,128)(2,1)S(1)}, bf16[256,192]{1,0:T(8,128)(2,1)S(1)}, u32[]{:S(2)}, u32[]{:S(2)}) %collective-permute-start.20) | collective-permute-done | bytes 98336 | tf_op jit(solution)/shard_map/ppermute | solution.py:1080
  79.4 1.9 collective-permute-done.22.far_hi
  82.1 23.9 %edge_branch.1 = (bf16[60,64,192]{2,1,0:T(8,128)(2,1)}, bf16[3840,192]{1,0:T(8,128)(2,1)}, bf16[3840,192]{1,0:T(8,128)(2,1)}, bf16[3840,192]{1,0:T(8,128)(2,1)},...) custom-call(bf16[1024,192]{1,0:T(8,128)(2,1)} %copy-done.27, ...), custom_call_target="tpu_custom_call" | custom-call | flops 7455375360 | bytes 11796480 | tf_op jit(solution)/shard_map/edge_branch/pallas_call | solution.py:577
  106.2 2.0 collective-permute-done.23
  109.6 1.4 collective-permute-start.24
  111.0 1.4 collective-permute-start.26
  113.2 2.9 %collective-permute-done.24 = bf16[256,192]{1,0:T(8,128)(2,1)S(1)} collective-permute-done((bf16[256,192]{1,0:T(8,128)(2,1)S(1)}, bf16[256,192]{1,0:T(8,128)(2,1)S(1)}, u32[]{:S(2)}, u32[]{:S(2)}) %collective-permute-start.24) | collective-permute-done | bytes 98336 | tf_op jit(solution)/shard_map/ppermute | solution.py:1080
  116.0 2.8 %collective-permute-done.26 = bf16[256,192]{1,0:T(8,128)(2,1)S(1)} collective-permute-done((bf16[256,192]{1,0:T(8,128)(2,1)S(1)}, bf16[256,192]{1,0:T(8,128)(2,1)S(1)}, u32[]{:S(2)}, u32[]{:S(2)}) %collective-permute-start.26) | collective-permute-done | bytes 98336 | tf_op jit(solution)/shard_map/ppermute | solution.py:1080
  121.0 1.6 collective-permute-start.29
  123.0 2.5 collective-permute-start.27
  125.4 1.4 collective-permute-done.29.refs_3_
  128.4 6.6 %residue_backward.1 = (f32[64,512]{1,0:T(8,128)}, f32[64,512]{1,0:T(8,128)}, bf16[64,1024]{1,0:T(8,128)(2,1)}, bf16[230,16,128]{2,1,0:T(8,128)(2,1)}) custom-call(bf16[64,512]{1,0:T(8,128)(2,1)} %node_cot.1, f32[64,192]{1,0:T(8,128)} %get-tuple-element.170.own_sum, bf16[192,1216]{1,0:T(8,128)(2,1)} %bitcast.46, bf16[192,512]{1,0:T(8,128)(2,1)} %slice.118.e_far, ...), custom_call_target="tpu_custom_call" | custom-call | flops 268435456 | bytes 8388608 | tf_op jit(solution)/shard_map/residue_backward/pallas_call | solution.py:180
  135.0 2.9 %collective-permute-start.32 = (bf16[64,1024]{1,0:T(8,128)(2,1)}, bf16[64,1024]{1,0:T(8,128)(2,1)S(1)}, u32[]{:S(2)}, u32[]{:S(2)}) collective-permute-start(bf16[64,1024]{1,0:T(8,128)(2,1)} %get-tuple-element.183), channel_id=1, source_target_pairs={{0,24},{1,25},{2,26},{3,27},{4,28},{5,29},{6,30},{7,31},{8,16},{9,... | collective-permute-start | bytes 393224 | tf_op jit(solution)/shard_map/ppermute | solution.py:1080
  139.4 7.4 %edge_weights.1 = (f32[192,192]{1,0:T(8,128)}, f32[192,192]{1,0:T(8,128)}, f32[192,192]{1,0:T(8,128)}, f32[1,192]{1,0:T(1,128)}, f32[1,192]{1,0:T(1,128)}, /*index=5*/f32[1,192]{1,0:T(1,128)}) custom-call(bf16[3840,192]{1,0:T(8,128)(2,1)} %get-tuple-element.184.refs_0_.low_edge, bf16[3840,192]{1,0:T(8,128)(2,1)} %get-tuple-element.185.refs_1_, ...), custom_call_target="tpu_custom_call" | custom-call | flops 849346560 | bytes 8847360 | tf_op jit(solution)/shard_map/edge_weights/pallas_call | solution.py:666
  147.7 1.6 collective-permute-start.35
  151.2 24.6 %message_backward.1 = (f32[60,64,192]{2,1,0:T(8,128)}, bf16[2,8,16,16,128]{4,3,2,1,0:T(8,128)(2,1)}, bf16[2,8,16,16,128]{4,3,2,1,0:T(8,128)(2,1)}, f32[64,512]{1...) custom-call(s32[1]{0:T(128)} %bitcast.16.base, s32[1,3840]{1,0:T(1,128)} %bitcast.55, ...), custom_call_target="tpu_custom_call" | custom-call | flops 6794772480 | bytes 19169280 | tf_op jit(solution)/shard_map/message_backward/pallas_call | solution.py:941
  176.1 1.7 copy-done.30
  177.8 3.4 %collective-permute-done.36 = bf16[384,16,128]{2,1,0:T(8,128)(2,1)S(1)} collective-permute-done((bf16[384,16,128]{2,1,0:T(8,128)(2,1)S(1)}, bf16[384,16,128]{2,1,0:T(8,128)(2,1)S(1)}, u32[]{:S(2)}, u32[]{:S(2)}) %collective-permute-start.36) | collective-permute-done | bytes 1572896 | tf_op jit(solution)/shard_map/ppermute | solution.py:1080
  183.5 1.5 collective-permute-start.39
  190.1 9.2 %feed_gradients.1 = (f32[512,512]{1,0:T(8,128)}, f32[512,512]{1,0:T(8,128)}, f32[1,512]{1,0:T(1,128)}) custom-call(bf16[1024,1024]{1,0:T(8,128)(2,1)} %copy-done.8, bf16[1024,1024]{1,0:T(8,128)(2,1)} %copy-done.29, bf16[512,512]{1,0:T(8,128)(2,1)} %f1.1, f32[1,512]{1,0:T(1,128)} %bitcast.62, bf16[512,512]{1,0:T(8,128)(2,1)} %f2.1), custom_call_target="tpu_custom_call" | custom-call | flops 4294967296 | bytes 4194304 | tf_op jit(solution)/shard_map/feed_gradients/pallas_call | solution.py:777
  199.3 4.8 %collective-permute-done.38 = bf16[96,16,128]{2,1,0:T(8,128)(2,1)S(1)} collective-permute-done((bf16[96,16,128]{2,1,0:T(8,128)(2,1)}, bf16[96,16,128]{2,1,0:T(8,128)(2,1)S(1)}, u32[]{:S(2)}, u32[]{:S(2)}) %collective-permute-start.38) | collective-permute-done | bytes 393248 | tf_op jit(solution)/shard_map/ppermute | solution.py:1080
  206.2 1.9 collective-permute-start.44
  209.8 1.4 collective-permute-start.45
  211.2 4.1 %collective-permute-done.42 = bf16[24,16,128]{2,1,0:T(8,128)(2,1)S(1)} collective-permute-done((bf16[24,16,128]{2,1,0:T(8,128)(2,1)S(1)}, bf16[24,16,128]{2,1,0:T(8,128)(2,1)S(1)}, u32[]{:S(2)}, u32[]{:S(2)}) %collective-permute-start.42) | collective-permute-done | bytes 98336 | tf_op jit(solution)/shard_map/ppermute | solution.py:1080
  215.3 1.6 collective-permute-start.50
  217.0 2.6 collective-permute-start.49
  221.4 3.1 %collective-permute-done.49 = bf16[24,16,128]{2,1,0:T(8,128)(2,1)S(1)} collective-permute-done((bf16[24,16,128]{2,1,0:T(8,128)(2,1)S(1)}, bf16[24,16,128]{2,1,0:T(8,128)(2,1)S(1)}, u32[]{:S(2)}, u32[]{:S(2)}) %collective-permute-start.49) | collective-permute-done | bytes 98336 | tf_op jit(solution)/shard_map/ppermute | solution.py:1080
  226.0 2.6 collective-permute-done.47
  228.6 1.7 collective-permute-start.53
  233.1 1.8 collective-permute-start.56
  234.9 4.4 %collective-permute-done.56.refs_3_ = bf16[16,16,128]{2,1,0:T(8,128)(2,1)S(1)} collective-permute-done((bf16[16,16,128]{2,1,0:T(8,128)(2,1)S(1)}, bf16[16,16,128]{2,1,0:T(8,128)(2,1)S(1)}, u32[]{:S(2)}, u32[]{:S(2)}) %collective-permute-start.56) | collective-permute-done | bytes 65568 | tf_op jit(solution)/shard_map/ppermute | solution.py:1080
  240.5 3.9 %collective-permute-done.54.refs_1_ = bf16[16,16,128]{2,1,0:T(8,128)(2,1)S(1)} collective-permute-done((bf16[16,16,128]{2,1,0:T(8,128)(2,1)S(1)}, bf16[16,16,128]{2,1,0:T(8,128)(2,1)S(1)}, u32[]{:S(2)}, u32[]{:S(2)}) %collective-permute-start.54) | collective-permute-done | bytes 65568 | tf_op jit(solution)/shard_map/ppermute | solution.py:1080
  245.1 3.0 %node_gradient.1 = f32[64,512]{1,0:T(8,128)} custom-call(f32[64,512]{1,0:T(8,128)} %get-tuple-element.234.g_u1, f32[64,512]{1,0:T(8,128)} %get-tuple-element.235.own, bf16[1216,512]{1,0:T(8,128)(2,1)} %m1.5, f32[64,16,128]{2,1,0:T(8,128)} %get-tuple-element.266.refs_0_, bf16[16,16,128]{2,1,0:T(8,128)(2,1)} %copy-done.23, bf16[16,16,128]{2,1,0:T(8,128)(2,1)} %copy-done.22, ...), custom_call_target="tpu_custom_call" | custom-call | flops 134217728 | bytes 2097152 | tf_op jit(solution)/shard_map/node_gradient/pallas_call | solution.py:180
  248.4 3.4 %collective-permute-done.57.second = bf16[384,16,128]{2,1,0:T(8,128)(2,1)S(1)} collective-permute-done((bf16[384,16,128]{2,1,0:T(8,128)(2,1)S(1)}, bf16[384,16,128]{2,1,0:T(8,128)(2,1)S(1)}, u32[]{:S(2)}, u32[]{:S(2)}) %collective-permute-start.57) | collective-permute-done | bytes 1572896 | tf_op jit(solution)/shard_map/ppermute | solution.py:1080
  253.0 4.7 %weight_gradients.1 = (f32[1216,512]{1,0:T(8,128)}, f32[1,512]{1,0:T(1,128)}, f32[512,512]{1,0:T(8,128)}, f32[1,512]{1,0:T(1,128)}, f32[512,512]{1,0:T(8,128)}, ...) custom-call(s32[1]{0:T(128)} %bitcast.16.base, ...), custom_call_target="tpu_custom_call" | custom-call | bytes 10485760 | tf_op jit(solution)/shard_map/weight_gradients/pallas_call | solution.py:180
  (194 shorter events, 52.7 us)
Async XLA Ops:
  0.7 13.6 %collective-permute-start.2 = (bf16[64,512]{1,0:T(8,128)(2,1)}, bf16[64,512]{1,0:T(8,128)(2,1)S(1)}, u32[]{:S(2)}, u32[]{:S(2)}) collective-permute-start(bf16[64,512]{1,0:T(8,128)(2,1)} %node.3), channel_id=1, source_target_pairs={{0,24},{1,25},{2,26},{3,27},{4,28},{5,29},{6,30},{7,31},{8,16},{9,... | collective-permute-start | bytes 196616 | tf_op jit(solution)/shard_map/ppermute | solution.py:1080
  5.8 8.5 %collective-permute-start.1 = (bf16[64,512]{1,0:T(8,128)(2,1)}, bf16[64,512]{1,0:T(8,128)(2,1)S(1)}, u32[]{:S(2)}, u32[]{:S(2)}) collective-permute-start(bf16[64,512]{1,0:T(8,128)(2,1)} %node.3), channel_id=1, source_target_pairs={{0,8},{1,9},{2,10},{3,11},{4,12},{5,13},{6,14},{7,15},{8,0},{9,1},... | collective-permute-start | bytes 196616 | tf_op jit(solution)/shard_map/ppermute | solution.py:1080
  5.8 8.5 %collective-permute-start = (bf16[64,512]{1,0:T(8,128)(2,1)}, bf16[64,512]{1,0:T(8,128)(2,1)S(1)}, u32[]{:S(2)}, u32[]{:S(2)}) collective-permute-start(bf16[64,512]{1,0:T(8,128)(2,1)} %node.3), channel_id=1, source_target_pairs={{0,16},{1,17},{2,18},{3,19},{4,20},{5,21},{6,22},{7,23},{8,24},{9,... | collective-permute-start | bytes 196616 | tf_op jit(solution)/shard_map/ppermute | solution.py:1080
  7.5 7.6 %collective-permute-start.3 = (bf16[256,512]{1,0:T(8,128)(2,1)S(1)}, bf16[256,512]{1,0:T(8,128)(2,1)S(1)}, u32[]{:S(2)}, u32[]{:S(2)}) collective-permute-start(bf16[256,512]{1,0:T(8,128)(2,1)S(1)} %get-tuple-element.159.refs_4_.refs_8_), channel_id=1, source_target_pairs={{0,2},{1,3},{2,0},{3,1},{4,6},{5,7},{6,4},{7,5},{8,10},{9,11},{10,... | collective-permute-start | bytes 786440 | tf_op jit(solution)/shard_map/ppermute | solution.py:1080
  15.1 10.7 %collective-permute-start.6 = (bf16[256,512]{1,0:T(8,128)(2,1)S(1)}, bf16[256,512]{1,0:T(8,128)(2,1)S(1)}, u32[]{:S(2)}, u32[]{:S(2)}) collective-permute-start(bf16[256,512]{1,0:T(8,128)(2,1)S(1)} %pad_maximum_fusion.4), channel_id=1, source_target_pairs={{0,6},{1,7},{2,4},{3,5},{4,2},{5,3},{6,0},{7,1},{8,14},{9,15},{10,... | collective-permute-start | bytes 786440 | tf_op jit(solution)/shard_map/ppermute | solution.py:1080
  17.5 11.3 %collective-permute-start.5 = (bf16[256,512]{1,0:T(8,128)(2,1)S(1)}, bf16[256,512]{1,0:T(8,128)(2,1)S(1)}, u32[]{:S(2)}, u32[]{:S(2)}) collective-permute-start(bf16[256,512]{1,0:T(8,128)(2,1)S(1)} %pad_maximum_fusion.4), channel_id=1, source_target_pairs={{0,2},{1,3},{2,0},{3,1},{4,6},{5,7},{6,4},{7,5},{8,10},{9,11},{10,... | collective-permute-start | bytes 786440 | tf_op jit(solution)/shard_map/ppermute | solution.py:1080
  18.1 10.6 %collective-permute-start.4 = (bf16[256,512]{1,0:T(8,128)(2,1)S(1)}, bf16[256,512]{1,0:T(8,128)(2,1)S(1)}, u32[]{:S(2)}, u32[]{:S(2)}) collective-permute-start(bf16[256,512]{1,0:T(8,128)(2,1)S(1)} %pad_maximum_fusion.4), channel_id=1, source_target_pairs={{0,4},{1,5},{2,6},{3,7},{4,0},{5,1},{6,2},{7,3},{8,12},{9,13},{10,... | collective-permute-start | bytes 786440 | tf_op jit(solution)/shard_map/ppermute | solution.py:1080
  29.7 22.3 %collective-permute-start.9 = (bf16[256,512]{1,0:T(8,128)(2,1)S(1)}, bf16[256,512]{1,0:T(8,128)(2,1)S(1)}, u32[]{:S(2)}, u32[]{:S(2)}) collective-permute-start(bf16[256,512]{1,0:T(8,128)(2,1)S(1)} %get-tuple-element.159.refs_4_.refs_8_), channel_id=1, source_target_pairs={{0,1},{1,0},{2,3},{3,2},{4,5},{5,4},{6,7},{7,6},{8,9},{9,8},{10,11... | collective-permute-start | bytes 786440 | tf_op jit(solution)/shard_map/ppermute | solution.py:1080
  30.2 21.8 %collective-permute-start.10 = (bf16[256,512]{1,0:T(8,128)(2,1)S(1)}, bf16[256,512]{1,0:T(8,128)(2,1)S(1)}, u32[]{:S(2)}, u32[]{:S(2)}) collective-permute-start(bf16[256,512]{1,0:T(8,128)(2,1)S(1)} %collective-permute-done.3.refs_6_.refs_10_), channel_id=1, source_target_pairs={{0,1},{1,0},{2,3},{3,2},{4,5},{5,4},{6,7},{7,6},{8,9},{9,8},{10,11... | collective-permute-start | bytes 786440 | tf_op jit(solution)/shard_map/ppermute | solution.py:1080
  30.2 21.8 %collective-permute-start.11 = (bf16[256,512]{1,0:T(8,128)(2,1)S(1)}, bf16[256,512]{1,0:T(8,128)(2,1)S(1)}, u32[]{:S(2)}, u32[]{:S(2)}) collective-permute-start(bf16[256,512]{1,0:T(8,128)(2,1)S(1)} %get-tuple-element.160.refs_5_.refs_9_), channel_id=1, source_target_pairs={{0,2},{1,3},{2,0},{3,1},{4,6},{5,7},{6,4},{7,5},{8,10},{9,11},{10,... | collective-permute-start | bytes 786440 | tf_op jit(solution)/shard_map/ppermute | solution.py:1080
  31.0 21.1 %collective-permute-start.8 = (bf16[528,512]{1,0:T(8,128)(2,1)S(1)}, bf16[528,512]{1,0:T(8,128)(2,1)S(1)}, u32[]{:S(2)}, u32[]{:S(2)}) collective-permute-start(bf16[528,512]{1,0:T(8,128)(2,1)S(1)} %concatenate.30.refs_0_.refs_4_), channel_id=1, source_target_pairs={{0,2},{1,3},{2,0},{3,1},{4,6},{5,7},{6,4},{7,5},{8,10},{9,11},{10,... | collective-permute-start | bytes 1622024 | tf_op jit(solution)/shard_map/ppermute | solution.py:1080
  62.1 8.9 %collective-permute-start.18 = (bf16[64,192]{1,0:T(8,128)(2,1)}, bf16[64,192]{1,0:T(8,128)(2,1)S(1)}, u32[]{:S(2)}, u32[]{:S(2)}) collective-permute-start(bf16[64,192]{1,0:T(8,128)(2,1)} %get-tuple-element.166), channel_id=1, source_target_pairs={{0,24},{1,25},{2,26},{3,27},{4,28},{5,29},{6,30},{7,31},{8,16},{9,... | collective-permute-start | bytes 73736 | tf_op jit(solution)/shard_map/ppermute | solution.py:1080
  65.6 5.4 %collective-permute-start.17 = (bf16[64,192]{1,0:T(8,128)(2,1)}, bf16[64,192]{1,0:T(8,128)(2,1)S(1)}, u32[]{:S(2)}, u32[]{:S(2)}) collective-permute-start(bf16[64,192]{1,0:T(8,128)(2,1)} %get-tuple-element.166), channel_id=1, source_target_pairs={{0,8},{1,9},{2,10},{3,11},{4,12},{5,13},{6,14},{7,15},{8,0},{9,1},... | collective-permute-start | bytes 73736 | tf_op jit(solution)/shard_map/ppermute | solution.py:1080
  65.6 5.4 %collective-permute-start.16 = (bf16[64,192]{1,0:T(8,128)(2,1)}, bf16[64,192]{1,0:T(8,128)(2,1)S(1)}, u32[]{:S(2)}, u32[]{:S(2)}) collective-permute-start(bf16[64,192]{1,0:T(8,128)(2,1)} %get-tuple-element.166), channel_id=1, source_target_pairs={{0,16},{1,17},{2,18},{3,19},{4,20},{5,21},{6,22},{7,23},{8,24},{9,... | collective-permute-start | bytes 73736 | tf_op jit(solution)/shard_map/ppermute | solution.py:1080
  71.0 5.3 %collective-permute-start.19 = (bf16[256,192]{1,0:T(8,128)(2,1)S(1)}, bf16[256,192]{1,0:T(8,128)(2,1)S(1)}, u32[]{:S(2)}, u32[]{:S(2)}) collective-permute-start(bf16[256,192]{1,0:T(8,128)(2,1)S(1)} %get-tuple-element.296), channel_id=1, source_target_pairs={{0,4},{1,5},{2,6},{3,7},{4,0},{5,1},{6,2},{7,3},{8,12},{9,13},{10,... | collective-permute-start | bytes 294920 | tf_op jit(solution)/shard_map/ppermute | solution.py:1080
  72.0 7.3 %collective-permute-start.21 = (bf16[256,192]{1,0:T(8,128)(2,1)S(1)}, bf16[256,192]{1,0:T(8,128)(2,1)S(1)}, u32[]{:S(2)}, u32[]{:S(2)}) collective-permute-start(bf16[256,192]{1,0:T(8,128)(2,1)S(1)} %get-tuple-element.296), channel_id=1, source_target_pairs={{0,6},{1,7},{2,4},{3,5},{4,2},{5,3},{6,0},{7,1},{8,14},{9,15},{10,... | collective-permute-start | bytes 294920 | tf_op jit(solution)/shard_map/ppermute | solution.py:1080
  73.2 6.1 %collective-permute-start.20 = (bf16[256,192]{1,0:T(8,128)(2,1)S(1)}, bf16[256,192]{1,0:T(8,128)(2,1)S(1)}, u32[]{:S(2)}, u32[]{:S(2)}) collective-permute-start(bf16[256,192]{1,0:T(8,128)(2,1)S(1)} %get-tuple-element.296), channel_id=1, source_target_pairs={{0,2},{1,3},{2,0},{3,1},{4,6},{5,7},{6,4},{7,5},{8,10},{9,11},{10,... | collective-permute-start | bytes 294920 | tf_op jit(solution)/shard_map/ppermute | solution.py:1080
  109.6 6.4 %collective-permute-start.24 = (bf16[256,192]{1,0:T(8,128)(2,1)S(1)}, bf16[256,192]{1,0:T(8,128)(2,1)S(1)}, u32[]{:S(2)}, u32[]{:S(2)}) collective-permute-start(bf16[256,192]{1,0:T(8,128)(2,1)S(1)} %get-tuple-element.282), channel_id=1, source_target_pairs={{0,4},{1,5},{2,6},{3,7},{4,0},{5,1},{6,2},{7,3},{8,12},{9,13},{10,... | collective-permute-start | bytes 294920 | tf_op jit(solution)/shard_map/ppermute | solution.py:1080
  111.0 7.8 %collective-permute-start.26 = (bf16[256,192]{1,0:T(8,128)(2,1)S(1)}, bf16[256,192]{1,0:T(8,128)(2,1)S(1)}, u32[]{:S(2)}, u32[]{:S(2)}) collective-permute-start(bf16[256,192]{1,0:T(8,128)(2,1)S(1)} %get-tuple-element.283), channel_id=1, source_target_pairs={{0,6},{1,7},{2,4},{3,5},{4,2},{5,3},{6,0},{7,1},{8,14},{9,15},{10,... | collective-permute-start | bytes 294920 | tf_op jit(solution)/shard_map/ppermute | solution.py:1080
  112.4 7.8 %collective-permute-start.25 = (bf16[256,192]{1,0:T(8,128)(2,1)S(1)}, bf16[256,192]{1,0:T(8,128)(2,1)S(1)}, u32[]{:S(2)}, u32[]{:S(2)}) collective-permute-start(bf16[256,192]{1,0:T(8,128)(2,1)S(1)} %get-tuple-element.284), channel_id=1, source_target_pairs={{0,2},{1,3},{2,0},{3,1},{4,6},{5,7},{6,4},{7,5},{8,10},{9,11},{10,... | collective-permute-start | bytes 294920 | tf_op jit(solution)/shard_map/ppermute | solution.py:1080
  121.0 5.9 %collective-permute-start.29 = (bf16[64,192]{1,0:T(8,128)(2,1)S(1)}, bf16[64,192]{1,0:T(8,128)(2,1)S(1)}, u32[]{:S(2)}, u32[]{:S(2)}) collective-permute-start(bf16[64,192]{1,0:T(8,128)(2,1)S(1)} %get-tuple-element.293), channel_id=1, source_target_pairs={{0,24},{1,25},{2,26},{3,27},{4,28},{5,29},{6,30},{7,31},{8,16},{9,... | collective-permute-start | bytes 73736 | tf_op jit(solution)/shard_map/ppermute | solution.py:1080
  123.0 4.8 %collective-permute-start.27 = (bf16[64,192]{1,0:T(8,128)(2,1)S(1)}, bf16[64,192]{1,0:T(8,128)(2,1)S(1)}, u32[]{:S(2)}, u32[]{:S(2)}) collective-permute-start(bf16[64,192]{1,0:T(8,128)(2,1)S(1)} %get-tuple-element.295), channel_id=1, source_target_pairs={{0,16},{1,17},{2,18},{3,19},{4,20},{5,21},{6,22},{7,23},{8,24},{9,... | collective-permute-start | bytes 73736 | tf_op jit(solution)/shard_map/ppermute | solution.py:1080
  135.0 11.8 %collective-permute-start.32 = (bf16[64,1024]{1,0:T(8,128)(2,1)}, bf16[64,1024]{1,0:T(8,128)(2,1)S(1)}, u32[]{:S(2)}, u32[]{:S(2)}) collective-permute-start(bf16[64,1024]{1,0:T(8,128)(2,1)} %get-tuple-element.183), channel_id=1, source_target_pairs={{0,24},{1,25},{2,26},{3,27},{4,28},{5,29},{6,30},{7,31},{8,16},{9,... | collective-permute-start | bytes 393224 | tf_op jit(solution)/shard_map/ppermute | solution.py:1080
  137.9 8.9 %collective-permute-start.31 = (bf16[64,1024]{1,0:T(8,128)(2,1)}, bf16[64,1024]{1,0:T(8,128)(2,1)S(1)}, u32[]{:S(2)}, u32[]{:S(2)}) collective-permute-start(bf16[64,1024]{1,0:T(8,128)(2,1)} %get-tuple-element.183), channel_id=1, source_target_pairs={{0,8},{1,9},{2,10},{3,11},{4,12},{5,13},{6,14},{7,15},{8,0},{9,1},... | collective-permute-start | bytes 393224 | tf_op jit(solution)/shard_map/ppermute | solution.py:1080
  138.1 9.6 %collective-permute-start.30 = (bf16[64,1024]{1,0:T(8,128)(2,1)}, bf16[64,1024]{1,0:T(8,128)(2,1)S(1)}, u32[]{:S(2)}, u32[]{:S(2)}) collective-permute-start(bf16[64,1024]{1,0:T(8,128)(2,1)} %get-tuple-element.183), channel_id=1, source_target_pairs={{0,16},{1,17},{2,18},{3,19},{4,20},{5,21},{6,22},{7,23},{8,24},{9,... | collective-permute-start | bytes 393224 | tf_op jit(solution)/shard_map/ppermute | solution.py:1080
  147.7 28.2 %collective-permute-start.35 = (bf16[256,1024]{1,0:T(8,128)(2,1)S(1)}, bf16[256,1024]{1,0:T(8,128)(2,1)S(1)}, u32[]{:S(2)}, u32[]{:S(2)}) collective-permute-start(bf16[256,1024]{1,0:T(8,128)(2,1)S(1)} %pad_maximum_fusion.2), channel_id=1, source_target_pairs={{0,6},{1,7},{2,4},{3,5},{4,2},{5,3},{6,0},{7,1},{8,14},{9,15},{10,... | collective-permute-start | bytes 1572872 | tf_op jit(solution)/shard_map/ppermute | solution.py:1080
  149.3 26.6 %collective-permute-start.34 = (bf16[256,1024]{1,0:T(8,128)(2,1)S(1)}, bf16[256,1024]{1,0:T(8,128)(2,1)S(1)}, u32[]{:S(2)}, u32[]{:S(2)}) collective-permute-start(bf16[256,1024]{1,0:T(8,128)(2,1)S(1)} %pad_maximum_fusion.2), channel_id=1, source_target_pairs={{0,2},{1,3},{2,0},{3,1},{4,6},{5,7},{6,4},{7,5},{8,10},{9,11},{10,... | collective-permute-start | bytes 1572872 | tf_op jit(solution)/shard_map/ppermute | solution.py:1080
  150.1 25.8 %collective-permute-start.33 = (bf16[256,1024]{1,0:T(8,128)(2,1)S(1)}, bf16[256,1024]{1,0:T(8,128)(2,1)S(1)}, u32[]{:S(2)}, u32[]{:S(2)}) collective-permute-start(bf16[256,1024]{1,0:T(8,128)(2,1)S(1)} %pad_maximum_fusion.2), channel_id=1, source_target_pairs={{0,4},{1,5},{2,6},{3,7},{4,0},{5,1},{6,2},{7,3},{8,12},{9,13},{10,... | collective-permute-start | bytes 1572872 | tf_op jit(solution)/shard_map/ppermute | solution.py:1080
  181.6 7.2 %collective-permute-start.41 = (bf16[1024,1024]{1,0:T(8,128)(2,1)S(1)}, bf16[1024,1024]{1,0:T(8,128)(2,1)S(1)}, u32[]{:S(2)}, u32[]{:S(2)}) collective-permute-start(bf16[1024,1024]{1,0:T(8,128)(2,1)S(1)} %pad_maximum_fusion.first), channel_id=1, source_target_pairs={{0,1},{1,0},{2,3},{3,2},{4,5},{5,4},{6,7},{7,6},{8,9},{9,8},{10,11... | collective-permute-start | bytes 6291464 | tf_op jit(solution)/shard_map/ppermute | solution.py:1080
  181.8 5.5 %collective-permute-start.40 = (bf16[256,16,128]{2,1,0:T(8,128)(2,1)S(1)}, bf16[256,16,128]{2,1,0:T(8,128)(2,1)S(1)}, u32[]{:S(2)}, u32[]{:S(2)}) collective-permute-start(bf16[256,16,128]{2,1,0:T(8,128)(2,1)S(1)} %bitcast.66), channel_id=1, source_target_pairs={{0,1},{1,0},{2,3},{3,2},{4,5},{5,4},{6,7},{7,6},{8,9},{9,8},{10,11... | collective-permute-start | bytes 3145736 | tf_op jit(solution)/shard_map/ppermute | solution.py:1080
  183.5 15.9 %collective-permute-start.39 = (bf16[96,16,128]{2,1,0:T(8,128)(2,1)}, bf16[96,16,128]{2,1,0:T(8,128)(2,1)S(1)}, u32[]{:S(2)}, u32[]{:S(2)}) collective-permute-start(bf16[96,16,128]{2,1,0:T(8,128)(2,1)} %get-tuple-element.276), channel_id=1, source_target_pairs={{0,6},{1,7},{2,4},{3,5},{4,2},{5,3},{6,0},{7,1},{8,14},{9,15},{10,... | collective-permute-start | bytes 1179656 | tf_op jit(solution)/shard_map/ppermute | solution.py:1080
  185.0 19.1 %collective-permute-start.38 = (bf16[96,16,128]{2,1,0:T(8,128)(2,1)}, bf16[96,16,128]{2,1,0:T(8,128)(2,1)S(1)}, u32[]{:S(2)}, u32[]{:S(2)}) collective-permute-start(bf16[96,16,128]{2,1,0:T(8,128)(2,1)} %get-tuple-element.277), channel_id=1, source_target_pairs={{0,2},{1,3},{2,0},{3,1},{4,6},{5,7},{6,4},{7,5},{8,10},{9,11},{10,... | collective-permute-start | bytes 1179656 | tf_op jit(solution)/shard_map/ppermute | solution.py:1080
  185.8 18.3 %collective-permute-start.37 = (bf16[96,16,128]{2,1,0:T(8,128)(2,1)}, bf16[96,16,128]{2,1,0:T(8,128)(2,1)}, u32[]{:S(2)}, u32[]{:S(2)}) collective-permute-start(bf16[96,16,128]{2,1,0:T(8,128)(2,1)} %get-tuple-element.278), channel_id=1, source_target_pairs={{0,4},{1,5},{2,6},{3,7},{4,0},{5,1},{6,2},{7,3},{8,12},{9,13},{10,... | collective-permute-start | bytes 1179656 | tf_op jit(solution)/shard_map/ppermute | solution.py:1080
  205.4 9.9 %collective-permute-start.42 = (bf16[24,16,128]{2,1,0:T(8,128)(2,1)S(1)}, bf16[24,16,128]{2,1,0:T(8,128)(2,1)S(1)}, u32[]{:S(2)}, u32[]{:S(2)}) collective-permute-start(bf16[24,16,128]{2,1,0:T(8,128)(2,1)S(1)} %get-tuple-element.287), channel_id=1, source_target_pairs={{0,16},{1,17},{2,18},{3,19},{4,20},{5,21},{6,22},{7,23},{8,24},{9,... | collective-permute-start | bytes 294920 | tf_op jit(solution)/shard_map/ppermute | solution.py:1080
  206.2 10.7 %collective-permute-start.44 = (bf16[24,16,128]{2,1,0:T(8,128)(2,1)S(1)}, bf16[24,16,128]{2,1,0:T(8,128)(2,1)S(1)}, u32[]{:S(2)}, u32[]{:S(2)}) collective-permute-start(bf16[24,16,128]{2,1,0:T(8,128)(2,1)S(1)} %get-tuple-element.288), channel_id=1, source_target_pairs={{0,24},{1,25},{2,26},{3,27},{4,28},{5,29},{6,30},{7,31},{8,16},{9,... | collective-permute-start | bytes 294920 | tf_op jit(solution)/shard_map/ppermute | solution.py:1080
  208.1 8.8 %collective-permute-start.43 = (bf16[24,16,128]{2,1,0:T(8,128)(2,1)S(1)}, bf16[24,16,128]{2,1,0:T(8,128)(2,1)S(1)}, u32[]{:S(2)}, u32[]{:S(2)}) collective-permute-start(bf16[24,16,128]{2,1,0:T(8,128)(2,1)S(1)} %get-tuple-element.289), channel_id=1, source_target_pairs={{0,8},{1,9},{2,10},{3,11},{4,12},{5,13},{6,14},{7,15},{8,0},{9,1},... | collective-permute-start | bytes 294920 | tf_op jit(solution)/shard_map/ppermute | solution.py:1080
  209.1 7.9 %collective-permute-start.46 = (bf16[64,16,128]{2,1,0:T(8,128)(2,1)S(1)}, bf16[64,16,128]{2,1,0:T(8,128)(2,1)S(1)}, u32[]{:S(2)}, u32[]{:S(2)}) collective-permute-start(bf16[64,16,128]{2,1,0:T(8,128)(2,1)S(1)} %get-tuple-element.280), channel_id=1, source_target_pairs={{0,2},{1,3},{2,0},{3,1},{4,6},{5,7},{6,4},{7,5},{8,10},{9,11},{10,... | collective-permute-start | bytes 786440 | tf_op jit(solution)/shard_map/ppermute | solution.py:1080
  209.8 7.2 %collective-permute-start.45 = (bf16[64,16,128]{2,1,0:T(8,128)(2,1)S(1)}, bf16[64,16,128]{2,1,0:T(8,128)(2,1)S(1)}, u32[]{:S(2)}, u32[]{:S(2)}) collective-permute-start(bf16[64,16,128]{2,1,0:T(8,128)(2,1)S(1)} %get-tuple-element.281), channel_id=1, source_target_pairs={{0,4},{1,5},{2,6},{3,7},{4,0},{5,1},{6,2},{7,3},{8,12},{9,13},{10,... | collective-permute-start | bytes 786440 | tf_op jit(solution)/shard_map/ppermute | solution.py:1080
  215.3 13.3 %collective-permute-start.50 = (bf16[64,16,128]{2,1,0:T(8,128)(2,1)S(1)}, bf16[64,16,128]{2,1,0:T(8,128)(2,1)S(1)}, u32[]{:S(2)}, u32[]{:S(2)}) collective-permute-start(bf16[64,16,128]{2,1,0:T(8,128)(2,1)S(1)} %get-tuple-element.279), channel_id=1, source_target_pairs={{0,6},{1,7},{2,4},{3,5},{4,2},{5,3},{6,0},{7,1},{8,14},{9,15},{10,... | collective-permute-start | bytes 786440 | tf_op jit(solution)/shard_map/ppermute | solution.py:1080
  217.0 7.6 %collective-permute-start.49 = (bf16[24,16,128]{2,1,0:T(8,128)(2,1)S(1)}, bf16[24,16,128]{2,1,0:T(8,128)(2,1)S(1)}, u32[]{:S(2)}, u32[]{:S(2)}) collective-permute-start(bf16[24,16,128]{2,1,0:T(8,128)(2,1)S(1)} %fusion.4), channel_id=1, source_target_pairs={{0,24},{1,25},{2,26},{3,27},{4,28},{5,29},{6,30},{7,31},{8,16},{9,... | collective-permute-start | bytes 294920 | tf_op jit(solution)/shard_map/ppermute | solution.py:1080
  219.5 6.4 %collective-permute-start.48 = (bf16[24,16,128]{2,1,0:T(8,128)(2,1)S(1)}, bf16[24,16,128]{2,1,0:T(8,128)(2,1)S(1)}, u32[]{:S(2)}, u32[]{:S(2)}) collective-permute-start(bf16[24,16,128]{2,1,0:T(8,128)(2,1)S(1)} %fusion.4), channel_id=1, source_target_pairs={{0,8},{1,9},{2,10},{3,11},{4,12},{5,13},{6,14},{7,15},{8,0},{9,1},... | collective-permute-start | bytes 294920 | tf_op jit(solution)/shard_map/ppermute | solution.py:1080
  220.4 8.1 %collective-permute-start.47 = (bf16[24,16,128]{2,1,0:T(8,128)(2,1)S(1)}, bf16[24,16,128]{2,1,0:T(8,128)(2,1)S(1)}, u32[]{:S(2)}, u32[]{:S(2)}) collective-permute-start(bf16[24,16,128]{2,1,0:T(8,128)(2,1)S(1)} %fusion.4), channel_id=1, source_target_pairs={{0,16},{1,17},{2,18},{3,19},{4,20},{5,21},{6,22},{7,23},{8,24},{9,... | collective-permute-start | bytes 294920 | tf_op jit(solution)/shard_map/ppermute | solution.py:1080
  228.6 19.5 %collective-permute-start.53 = (bf16[96,16,128]{2,1,0:T(8,128)(2,1)S(1)}, bf16[96,16,128]{2,1,0:T(8,128)(2,1)S(1)}, u32[]{:S(2)}, u32[]{:S(2)}) collective-permute-start(bf16[96,16,128]{2,1,0:T(8,128)(2,1)S(1)} %pad_maximum_fusion.3), channel_id=1, source_target_pairs={{0,6},{1,7},{2,4},{3,5},{4,2},{5,3},{6,0},{7,1},{8,14},{9,15},{10,... | collective-permute-start | bytes 1179656 | tf_op jit(solution)/shard_map/ppermute | solution.py:1080
  230.2 17.8 %collective-permute-start.52 = (bf16[96,16,128]{2,1,0:T(8,128)(2,1)S(1)}, bf16[96,16,128]{2,1,0:T(8,128)(2,1)S(1)}, u32[]{:S(2)}, u32[]{:S(2)}) collective-permute-start(bf16[96,16,128]{2,1,0:T(8,128)(2,1)S(1)} %pad_maximum_fusion.3), channel_id=1, source_target_pairs={{0,2},{1,3},{2,0},{3,1},{4,6},{5,7},{6,4},{7,5},{8,10},{9,11},{10,... | collective-permute-start | bytes 1179656 | tf_op jit(solution)/shard_map/ppermute | solution.py:1080
  231.0 17.0 %collective-permute-start.51 = (bf16[96,16,128]{2,1,0:T(8,128)(2,1)S(1)}, bf16[96,16,128]{2,1,0:T(8,128)(2,1)S(1)}, u32[]{:S(2)}, u32[]{:S(2)}) collective-permute-start(bf16[96,16,128]{2,1,0:T(8,128)(2,1)S(1)} %pad_maximum_fusion.3), channel_id=1, source_target_pairs={{0,4},{1,5},{2,6},{3,7},{4,0},{5,1},{6,2},{7,3},{8,12},{9,13},{10,... | collective-permute-start | bytes 1179656 | tf_op jit(solution)/shard_map/ppermute | solution.py:1080
  233.1 6.2 %collective-permute-start.56 = (bf16[16,16,128]{2,1,0:T(8,128)(2,1)S(1)}, bf16[16,16,128]{2,1,0:T(8,128)(2,1)S(1)}, u32[]{:S(2)}, u32[]{:S(2)}) collective-permute-start(bf16[16,16,128]{2,1,0:T(8,128)(2,1)S(1)} %get-tuple-element.290), channel_id=1, source_target_pairs={{0,24},{1,25},{2,26},{3,27},{4,28},{5,29},{6,30},{7,31},{8,16},{9,... | collective-permute-start | bytes 196616 | tf_op jit(solution)/shard_map/ppermute | solution.py:1080
  234.9 5.6 %collective-permute-start.55 = (bf16[16,16,128]{2,1,0:T(8,128)(2,1)S(1)}, bf16[16,16,128]{2,1,0:T(8,128)(2,1)S(1)}, u32[]{:S(2)}, u32[]{:S(2)}) collective-permute-start(bf16[16,16,128]{2,1,0:T(8,128)(2,1)S(1)} %get-tuple-element.291), channel_id=1, source_target_pairs={{0,8},{1,9},{2,10},{3,11},{4,12},{5,13},{6,14},{7,15},{8,0},{9,1},... | collective-permute-start | bytes 196616 | tf_op jit(solution)/shard_map/ppermute | solution.py:1080
  239.3 5.2 %collective-permute-start.54 = (bf16[16,16,128]{2,1,0:T(8,128)(2,1)S(1)}, bf16[16,16,128]{2,1,0:T(8,128)(2,1)S(1)}, u32[]{:S(2)}, u32[]{:S(2)}) collective-permute-start(bf16[16,16,128]{2,1,0:T(8,128)(2,1)S(1)} %get-tuple-element.292), channel_id=1, source_target_pairs={{0,16},{1,17},{2,18},{3,19},{4,20},{5,21},{6,22},{7,23},{8,24},{9,... | collective-permute-start | bytes 196616 | tf_op jit(solution)/shard_map/ppermute | solution.py:1080
  (44 other events, 284.9 us)
